TPU v7x, 256 devices: a whole 4x4x8 slice. The times are simulated.
256 devices in a mesh: dp: 4 (over x), expert: 64 (over z, y, core).
Axes of the slice: x: 4, y: 4, z: 8, core: 2. Of those that a mesh axis runs over, the one named last changes fastest.
Arguments:
- latent: bfloat16 [1024, 1024], P('dp'), may hold values from -6 to 6
- residual: bfloat16 [1024, 4096], P('dp', 'expert'), may hold values from -6 to 6
- gates: float32 [1024, 22], P('dp'), may hold values from 0.1 to 1
- route_ids: int32 [1024, 22], P('dp'), may hold values from 0 to 63, all different within a row; in each aligned block of 256 rows (0 to 255, 256 to 511, ...) at most 184 rows name the same one
- w_gate: bfloat16 [64, 1024, 1344], P('expert', None, 'dp'), may hold values from -0.1875 to 0.1875
- w_up: bfloat16 [64, 1024, 1344], P('expert', None, 'dp'), may hold values from -0.1875 to 0.1875
- w_out: bfloat16 [64, 1344, 1024], P('expert', 'dp'), may hold values from -0.15625 to 0.15625
- w_lift: bfloat16 [1024, 4096], P(None, 'expert'), may hold values from -0.1875 to 0.1875
- norm_gain: bfloat16 [4096], replicated, may hold values from 0.25 to 1.75
- w_vocab: bfloat16 [4096, 65536], P(None, 'expert'), may hold values from -17 to 17
- targets: int32 [1024], P('dp'), may hold values from 0 to 65535
- loss_cot: float32 [1024], P('dp'), may hold values from -64 to 64
Outputs:
- row_loss: float32 [1024], P('dp')
- d_residual: float32 [1024, 4096], P('dp', 'expert')
- d_latent: float32 [1024, 1024], P('dp')
- d_gates: float32 [1024, 22], P('dp')
Inputs may be any that keep to these rules, and one draw needn't show every extreme that they name: `route_ids`: each row names 22 different experts. Among the rows of one index of dp no expert is named by more than 184 rows, a bound that some block reaches.
All inputs are finite; a program needn't handle non-finite values.
Results may differ from a plain program's by a relative error of at most 0.04.
Values may be sent and summed in bfloat16 or wider, within the bound.
No kernel may reach another device: no remote copies, remote signals or barrier semaphores. Data moves between devices by JAX's collectives and lax.ppermute only.
A program may use at most 128 MiB of HBM per device.

v0:
```python
import jax
import jax.numpy as jnp
from jax import lax
from jax.sharding import PartitionSpec as P

norm_epsilon = 1e-05
contract_last = (((1,), (1,)), ((), ()))


def on_device(
    latent,
    residual,
    gates,
    route_ids,
    w_gate,
    w_up,
    w_out,
    w_lift,
    norm_gain,
    w_vocab,
    targets,
    loss_cot,
):
    experts = lax.axis_size("expert")
    own_index = lax.axis_index("expert")
    tok_rows = latent.shape[0]
    top_count = route_ids.shape[1]
    capacity = min(tok_rows, (tok_rows * top_count // experts // 4 + 1) * 8)
    quarter = w_gate.shape[2]
    word_count = w_vocab.shape[1]
    col_count = residual.shape[1]
    gate_mat = w_gate[0]
    up_mat = w_up[0]
    out_mat = w_out[0]
    chosen = route_ids == own_index
    routed_here = jnp.any(chosen, axis=1)
    gate_own = jnp.sum(jnp.where(chosen, gates, 0.0), axis=1)
    slot_index = jnp.cumsum(routed_here.astype(jnp.int32)) - 1
    slot_range = jnp.arange(capacity, dtype=jnp.int32)
    select = (slot_index[None, :] == slot_range[:, None]) & routed_here[None, :]
    select_bf = select.astype(jnp.bfloat16)
    select_float = select.astype(jnp.float32)
    row_block = jnp.dot(select_bf, latent, preferred_element_type=jnp.float32).astype(jnp.bfloat16)
    piece_rows = lax.all_gather(row_block, "dp", axis=0, tiled=True)
    gate_part = jnp.dot(piece_rows, gate_mat, preferred_element_type=jnp.float32)
    up_part = jnp.dot(piece_rows, up_mat, preferred_element_type=jnp.float32)
    projected = jnp.concatenate([gate_part, up_part], axis=1)
    gate_pre = projected[:, :quarter]
    up_pre = projected[:, quarter:]
    active = (jax.nn.silu(gate_pre) * up_pre).astype(jnp.bfloat16)
    expert_out = lax.psum_scatter(
        jnp.dot(active, out_mat, preferred_element_type=jnp.float32),
        "dp",
        scatter_dimension=0,
        tiled=True,
    )
    routed_out = jnp.dot(select_float.T, expert_out, precision=lax.Precision.HIGHEST)
    combined = lax.psum(routed_out * gate_own[:, None], "expert").astype(jnp.bfloat16)
    lifted = jnp.dot(combined, w_lift, preferred_element_type=jnp.float32)
    hidden = (residual.astype(jnp.float32) + lifted).astype(jnp.bfloat16)
    hidden_all = lax.all_gather(hidden, "expert", axis=1, tiled=True)
    hidden_float = hidden_all.astype(jnp.float32)
    scale_inv = lax.rsqrt(
        jnp.mean(hidden_float * hidden_float, axis=1, keepdims=True) + norm_epsilon
    )
    gain_float = norm_gain.astype(jnp.float32)
    normed = (hidden_float * scale_inv * gain_float[None, :]).astype(jnp.bfloat16)
    logits = jnp.dot(normed, w_vocab, preferred_element_type=jnp.float32)
    word_range = jnp.arange(word_count, dtype=jnp.int32)
    is_target = targets[:, None] - own_index * word_count == word_range[None, :]
    target_part = jnp.sum(jnp.where(is_target, logits, 0.0), axis=1)
    top_part = jnp.max(logits, axis=1)
    row_peak = lax.pmax(top_part, "expert")
    total_part = jnp.sum(jnp.exp(logits - row_peak[:, None]), axis=1)
    row_total, target_logit = lax.psum((total_part, target_part), "expert")
    row_loss = row_peak + jnp.log(row_total) - target_logit
    softmax_probs = jnp.exp(logits - row_peak[:, None]) / row_total[:, None]
    logit_grad = (loss_cot[:, None] * (softmax_probs - is_target.astype(jnp.float32))).astype(
        jnp.bfloat16
    )
    normed_grad = lax.dot_general(
        logit_grad, w_vocab, contract_last, preferred_element_type=jnp.float32
    )
    full_grad = lax.psum(normed_grad, "expert")
    scaled = full_grad * gain_float[None, :]
    inner_term = jnp.mean(scaled * hidden_float, axis=1, keepdims=True)
    grad_all = scale_inv * scaled - hidden_float * scale_inv**3 * inner_term
    d_residual = lax.dynamic_slice_in_dim(grad_all, own_index * col_count, col_count, 1)
    comb_part = lax.dot_general(
        d_residual.astype(jnp.bfloat16), w_lift, contract_last, preferred_element_type=jnp.float32
    )
    combined_grad = lax.psum(comb_part, "expert").astype(jnp.bfloat16)
    comb_float = combined_grad.astype(jnp.float32)
    gate_term = jnp.sum(comb_float * routed_out, axis=1)
    gate_grad_part = jnp.where(chosen, gate_term[:, None], 0.0)
    routed_grad = jnp.dot(
        select_float, comb_float * gate_own[:, None], precision=lax.Precision.HIGHEST
    ).astype(jnp.bfloat16)
    grads_all = lax.all_gather(routed_grad, "dp", axis=0, tiled=True)
    act_grad = lax.dot_general(
        grads_all, out_mat, contract_last, preferred_element_type=jnp.float32
    )
    sigmoid_gate = jax.nn.sigmoid(gate_pre)
    gate_back = (act_grad * up_pre * sigmoid_gate * (1.0 + gate_pre * (1.0 - sigmoid_gate))).astype(
        jnp.bfloat16
    )
    up_back = (act_grad * gate_pre * sigmoid_gate).astype(jnp.bfloat16)
    first_term = lax.dot_general(
        gate_back, gate_mat, contract_last, preferred_element_type=jnp.float32
    )
    block_grad = lax.psum_scatter(
        first_term
        + lax.dot_general(up_back, up_mat, contract_last, preferred_element_type=jnp.float32),
        "dp",
        scatter_dimension=0,
        tiled=True,
    )
    latent_part = jnp.dot(select_float.T, block_grad, precision=lax.Precision.HIGHEST)
    d_latent, d_gates = lax.psum((latent_part, gate_grad_part), "expert")
    return (row_loss, d_residual, d_latent, d_gates)


def solution(mesh):
    in_specs = (
        P("dp", None),
        P("dp", "expert"),
        P("dp", None),
        P("dp", None),
        P("expert", None, "dp"),
        P("expert", None, "dp"),
        P("expert", "dp", None),
        P(None, "expert"),
        P(),
        P(None, "expert"),
        P("dp"),
        P("dp"),
    )
    out_specs = (P("dp"), P("dp", "expert"), P("dp", None), P("dp", None))
    return jax.shard_map(
        on_device, mesh=mesh, in_specs=in_specs, out_specs=out_specs, check_vma=False
    )
```

profile of v0, /device:TPU:1, one launch (start us, length us, event | category | flops | bytes accessed | tf_op | source)
XLA Modules:
  0.0 1481.6 jit_solution(15357824602519560702)
XLA Ops:
  7.2 0.0 copy-start
  7.2 0.0 copy-start.5
  7.2 0.0 all-gather.4.cloned.1.call-start
  7.2 0.9 select_reduce_fusion.1
  8.2 0.3 reduce-window.9
  8.5 0.1 slice.7
  8.6 0.1 slice_reduce_fusion
  8.7 0.1 add_bitcast_fusion
  8.8 2.1 convolution_convert_fusion.1
  10.8 0.0 all-gather.4.cloned.1.call-update
  10.8 0.0 reduce-scatter.3.cloned.1.call-start
  10.9 32.4 %all-gather.4.cloned.1.call-done = bf16[736,1024]{1,0:T(8,128)(2,1)} async-done(((bf16[184,1024]{1,0:T(8,128)(2,1)}), bf16[736,1024]{1,0:T(8,128)(2,1)}) %all-gather.4.cloned.1.call-update) | async-done | bytes 1507344 | tf_op jit(solution)/shard_map/all_gather | solution.py:44
  43.3 2.4 fusion.15
  45.8 0.7 fusion.11
  46.5 0.3 copy-done.3
  46.8 1.0 copy-done.15
  47.8 0.0 copy-done
  47.8 2.6 fusion.8
  50.4 0.0 reduce-scatter.3.cloned.1.call-update
  50.4 0.0 all-gather.6.cloned.1.call-start
  50.5 40.2 %reduce-scatter.3.cloned.1.call-done = f32[184,1024]{1,0:T(8,128)} async-done(((f32[736,1024]{1,0:T(8,128)}), f32[184,1024]{1,0:T(8,128)}) %reduce-scatter.3.cloned.1.call-update) | async-done | bytes 753680 | tf_op jit(solution)/shard_map/reduce_scatter | solution.py:51
  90.7 2.8 broadcast_multiply_fusion.1
  93.4 254.7 %all-reduce.9 = bf16[256,1024]{1,0:T(8,128)(2,1)S(1)} all-reduce(f32[256,1024]{1,0:T(8,128)S(1)} %get-tuple-element.14), channel_id=1, replica_groups=mesh['dp'=4,'expert'=64] {'expert'}, use_global_device_ids=true, to_apply=%region_5.6 | all-reduce | flops 262144 | bytes 1572864 | tf_op jit(solution)/shard_map/psum | solution.py:58
  348.2 0.9 fusion.3
  349.1 0.0 all-gather.6.cloned.1.call-update
  349.1 0.0 all-reduce.6.cloned.1.call-start
  349.2 77.3 %all-gather.6.cloned.1.call-done = bf16[256,4096]{0,1:T(8,128)(2,1)} async-done(((bf16[256,64]{0,1:T(8,128)(2,1)}), bf16[256,4096]{0,1:T(8,128)(2,1)}) %all-gather.6.cloned.1.call-update) | async-done | bytes 2097168 | tf_op jit(solution)/shard_map/all_gather | solution.py:61
  426.5 2.2 multiply_reduce_fusion.1
  428.7 6.6 fusion.50
  435.3 123.6 %pmax.7 = f32[256]{0:T(256)S(1)} all-reduce(f32[256]{0:T(256)S(1)} %get-tuple-element.16), channel_id=1, replica_groups=mesh['dp'=4,'expert'=64] {'expert'}, use_global_device_ids=true, to_apply=%region_8.9 | all-reduce | flops 256 | bytes 2048 | tf_op jit(solution)/shard_map/pmax | solution.py:73
  558.9 0.4 fusion.5
  559.3 126.6 %psum.50 = f32[256]{0:T(256)S(1)} all-reduce(f32[256]{0:T(256)S(1)} %get-tuple-element.4), channel_id=1, replica_groups=mesh['dp'=4,'expert'=64] {'expert'}, use_global_device_ids=true, to_apply=%region_10.11 | all-reduce | flops 256 | bytes 2048 | tf_op jit(solution)/shard_map/psum | solution.py:75
  685.9 0.0 copy-done.14
  685.9 8.0 fusion.17
  693.9 0.0 all-reduce.6.cloned.1.call-update
  693.9 0.0 all-gather.8.cloned.1.call-start
  693.9 1.5 copy-done.1
  695.4 2.3 convert_element_type.64
  697.8 188.0 %all-reduce.6.cloned.1.call-done = f32[256,4096]{0,1:T(8,128)} async-done(((f32[256,4096]{0,1:T(8,128)}), f32[256,4096]{0,1:T(8,128)}) %all-reduce.6.cloned.1.call-update) | async-done | bytes 4194320 | tf_op jit(solution)/shard_map/psum | solution.py:84
  885.7 2.6 multiply_reduce_fusion
  888.3 0.9 fusion.43
  889.2 0.0 copy-start.8
  889.2 0.3 fusion.45
  889.5 0.0 copy-start.4
  889.6 255.1 %all-reduce.10 = bf16[256,1024]{1,0:T(8,128)(2,1)S(1)} all-reduce(f32[256,1024]{1,0:T(8,128)S(1)} %fusion.45), channel_id=1, replica_groups=mesh['dp'=4,'expert'=64] {'expert'}, use_global_device_ids=true, to_apply=%region_15.16 | all-reduce | flops 262144 | bytes 1572864 | tf_op jit(solution)/shard_map/psum | solution.py:92
  1144.7 0.0 copy-start.13
  1144.7 1.5 convolution_convert_fusion
  1146.2 0.0 all-gather.8.cloned.1.call-update
  1146.2 0.0 reduce-scatter.5.cloned.1.call-start
  1146.3 30.1 %all-gather.8.cloned.1.call-done = bf16[736,1024]{1,0:T(8,128)(2,1)} async-done(((bf16[184,1024]{1,0:T(8,128)(2,1)}), bf16[736,1024]{1,0:T(8,128)(2,1)}) %all-gather.8.cloned.1.call-update) | async-done | bytes 1507344 | tf_op jit(solution)/shard_map/all_gather | solution.py:99
  1176.4 2.2 fusion.6
  1178.6 0.0 copy-done.8
  1178.7 0.0 copy-start.6
  1178.7 1.2 fusion.13
  1179.8 2.6 convolution_add_fusion
  1182.5 0.0 reduce-scatter.5.cloned.1.call-update
  1182.5 0.0 all-reduce.8.cloned.1.call-start
  1182.6 40.1 %reduce-scatter.5.cloned.1.call-done = f32[184,1024]{1,0:T(8,128)} async-done(((f32[736,1024]{1,0:T(8,128)}), f32[184,1024]{1,0:T(8,128)}) %reduce-scatter.5.cloned.1.call-update) | async-done | bytes 753680 | tf_op jit(solution)/shard_map/reduce_scatter | solution.py:111
  1222.7 2.8 fusion.29
  1225.5 0.0 all-reduce.8.cloned.1.call-update
  1225.5 0.2 fusion.4
  1225.7 246.2 %all-reduce = (f32[256]{0:T(256)S(1)}, f32[256,22]{0,1:T(8,128)}) all-reduce(f32[256]{0:T(256)S(1)} %get-tuple-element.5, f32[256,22]{0,1:T(8,128)S(1)} %broadcast_select_fusion), channel_id=1, replica_groups=mesh['dp'=4,'expert'=64] {'expert'}, use_global_device_ids=true, to_apply=%region_12.13 | all-reduce | flops 5888 | bytes 47104 | tf_op jit(solution)/shard_map/psum | solution.py:75
  1471.9 0.6 add_subtract_fusion
  1472.4 2.3 copy.25
  (31 shorter events, 0.1 us)
Async XLA Ops:
  7.2 40.6 %copy-start = (bf16[1,336,1024]{2,1,0:T(8,128)(2,1)S(1)}, bf16[1,336,1024]{2,1,0:T(8,128)(2,1)}, u32[]{:S(2)}) copy-start(bf16[1,336,1024]{2,1,0:T(8,128)(2,1)} %param.18) | copy-start | bytes 2064388
  7.2 38.6 %copy-start.5 = (bf16[1,1024,336]{1,2,0:T(8,128)(2,1)S(1)}, bf16[1,1024,336]{1,2,0:T(8,128)(2,1)}, u32[]{:S(2)}) copy-start(bf16[1,1024,336]{1,2,0:T(8,128)(2,1)} %param.17) | copy-start | bytes 2064388
  7.2 36.1 %all-gather.4.cloned.1.call-start = ((), (), s32[]{:S(2)}) async-start(), calls=%async_computation.2 | async-start | bytes 1884160 | tf_op jit(solution)/shard_map/all_gather | solution.py:44
  10.8 79.8 %reduce-scatter.3.cloned.1.call-start = ((), (), s32[]{:S(2)}) async-start(), calls=%async_computation.3 | async-start | bytes 3768320 | tf_op jit(solution)/shard_map/reduce_scatter | solution.py:51
  43.3 2.4 copy-start.12
  45.8 1.1 copy-start.3
  46.8 1.0 copy-start.15
  50.4 297.8 %copy-start.7 = (bf16[1024,64]{0,1:T(8,128)(2,1)S(1)}, bf16[1024,64]{0,1:T(8,128)(2,1)}, u32[]{:S(2)}) copy-start(bf16[1024,64]{0,1:T(8,128)(2,1)} %param.19) | copy-start | bytes 393220
  50.4 297.8 %copy-start.9 = (bf16[256,64]{0,1:T(8,128)(2,1)S(1)}, bf16[256,64]{0,1:T(8,128)(2,1)}, u32[]{:S(2)}) copy-start(bf16[256,64]{0,1:T(8,128)(2,1)} %param.13) | copy-start | bytes 98308
  50.4 298.8 %copy-start.10 = (bf16[4096]{0:T(1024)(128)(2,1)S(1)}, bf16[4096]{0:T(1024)(128)(2,1)}, u32[]{:S(2)}) copy-start(bf16[4096]{0:T(1024)(128)(2,1)} %param.20) | copy-start | bytes 24580
  50.4 298.8 %copy-start.11 = (s32[256]{0:T(256)S(1)}, s32[256]{0:T(256)}, u32[]{:S(2)}) copy-start(s32[256]{0:T(256)} %param.22) | copy-start | bytes 3076
  50.4 376.1 %all-gather.6.cloned.1.call-start = ((), (), s32[]{:S(2)}) async-start(), calls=%async_computation.4 | async-start | bytes 2129920 | tf_op jit(solution)/shard_map/all_gather | solution.py:61
  349.1 536.6 %all-reduce.6.cloned.1.call-start = ((), (), s32[]{:S(2)}) async-start(), calls=%async_computation.5 | async-start | bytes 8388608 | tf_op jit(solution)/shard_map/psum | solution.py:84
  428.7 257.2 %copy-start.14 = (f32[256]{0:T(256)S(1)}, f32[256]{0:T(256)}, u32[]{:S(2)}) copy-start(f32[256]{0:T(256)} %param.23) | copy-start | bytes 3076
  693.9 1.6 copy-start.1
  693.9 482.5 %all-gather.8.cloned.1.call-start = ((), (), s32[]{:S(2)}) async-start(), calls=%async_computation.6 | async-start | bytes 1884160 | tf_op jit(solution)/shard_map/all_gather | solution.py:99
  889.2 289.4 %copy-start.8 = (f32[256,64]{0,1:T(8,128)}, f32[256,64]{0,1:T(8,128)S(1)}, u32[]{:S(2)}) copy-start(f32[256,64]{0,1:T(8,128)S(1)} %fusion.43) | copy-start | bytes 196612
  889.5 289.1 %copy-start.4 = (f32[736,336]{0,1:T(8,128)S(1)}, f32[736,336]{0,1:T(8,128)}, u32[]{:S(2)}) copy-start(f32[736,336]{0,1:T(8,128)} %copy-done.3) | copy-start | bytes 2967556
  1144.7 33.9 %copy-start.13 = (bf16[1,1024,336]{1,2,0:T(8,128)(2,1)S(1)}, bf16[1,1024,336]{1,2,0:T(8,128)(2,1)}, u32[]{:S(2)}) copy-start(bf16[1,1024,336]{1,2,0:T(8,128)(2,1)} %param.16) | copy-start | bytes 2064388
  1146.2 76.5 %reduce-scatter.5.cloned.1.call-start = ((), (), s32[]{:S(2)}) async-start(), calls=%async_computation.7 | async-start | bytes 3768320 | tf_op jit(solution)/shard_map/reduce_scatter | solution.py:111
  1176.4 2.2 copy-start.16
  1178.7 1.2 copy-start.6
  1182.5 43.0 %copy-start.2 = (f32[256,1024]{1,0:T(8,128)S(1)}, f32[256,1024]{1,0:T(8,128)}, u32[]{:S(2)}) copy-start(f32[256,1024]{1,0:T(8,128)} %get-tuple-element.15) | copy-start | bytes 3145732
  1182.5 289.9 %all-reduce.8.cloned.1.call-start = ((), (), s32[]{:S(2)}) async-start(), calls=%async_computation.8 | async-start | bytes 2097152 | tf_op jit(solution)/shard_map/psum | solution.py:119
Sparse Core Ops, SparseCore 0:
  11.0 32.3 all-gather.3
  50.6 40.0 reduce-scatter.2
  349.3 77.2 all-gather.5
  694.0 191.6 all-reduce.5
  1146.4 29.9 all-gather.7
  1182.6 40.0 reduce-scatter.4
  1226.5 184.3 all-reduce.7
where the time goes:
time: 1490 us; the launch traced here: 1480 us
  blocking collectives  1010 us (68%)
  waiting for transfers between devices  408 us (27%)
  matrix products  36.6 us (2%)
    psum x2, blocking collectives, on_device(): row_total, target_logit = lax.psum((total_part, target_part), 'expert')  373 us
    psum x1, blocking collectives, on_device(): combined_grad = lax.psum(comb_part, 'expert').astype(jnp.bfloat16)  255 us
    psum x1, blocking collectives, on_device(): lax.psum(routed_out * gate_own[:, None], 'expert').astype(jnp.bfloat16)  255 us
    psum x1, waiting for transfers between devices, on_device(): full_grad = lax.psum(normed_grad, 'expert')  188 us
    pmax x1, blocking collectives, on_device(): row_peak = lax.pmax(top_part, 'expert')  124 us
    all_gather x1, waiting for transfers between devices, on_device(): hidden_all = lax.all_gather(hidden, 'expert', axis=1, tiled=True)  77.3 us
    reduce_scatter x1, waiting for transfers between devices, on_device(): lax.psum_scatter(jnp.dot(active, out_mat, preferred_element_type=jnp.floa...  40.2 us
    reduce_scatter x1, waiting for transfers between devices, on_device(): lax.psum_scatter(first_term + lax.dot_general(up_back, up_mat, contract_l...  40.1 us
  transfers between devices with their start and end apart: 7, of which 6 were waited for; matrix products, arithmetic and copies ran while one was open for 0% of the time, Pallas kernels for 0%

commit v1 on v0

v1 whole, which is shorter than its diff:
```python
import jax
import jax.numpy as jnp
from jax import lax
from jax.sharding import Mesh, PartitionSpec as P

norm_epsilon = 1e-05
plane = ("z", "y")
slab = ("z", "y", "c")
bf16 = jnp.bfloat16
f32 = jnp.float32


def dot(a, b, ca, cb):
    return lax.dot_general(a, b, (((ca,), (cb,)), ((), ())), preferred_element_type=f32)


def swap(x):
    return lax.ppermute(x, "c", [(0, 1), (1, 0)])


def deal(x, axes):
    return lax.all_to_all(x, axes, 0, 0, tiled=True)


def spread(x, axes):
    count = lax.axis_size(axes)
    return deal(jnp.broadcast_to(x[None], (count,) + x.shape), axes)


def on_device(
    latent,
    residual,
    gates,
    route_ids,
    w_gate,
    w_up,
    w_out,
    w_lift,
    norm_gain,
    w_vocab,
    targets,
    loss_cot,
):
    core = lax.axis_index("c")
    own_index = lax.axis_index(slab)
    places = lax.axis_size(plane)
    groups = lax.axis_size("dp")
    rows, width = latent.shape
    half = width // 2
    cols = residual.shape[1]
    model = w_vocab.shape[0]
    words = w_vocab.shape[1]
    chunk = rows // places
    first = core == 0

    def mine(x, axis):
        a, b = jnp.split(x, 2, axis)
        return jnp.where(first, a, b)

    def other(x, axis):
        a, b = jnp.split(x, 2, axis)
        return jnp.where(first, b, a)

    def joined(own, peer, axis):
        return jnp.where(
            first,
            jnp.concatenate([own, peer], axis),
            jnp.concatenate([peer, own], axis),
        )

    gate_mat, up_mat, out_mat = w_gate[0], w_up[0], w_out[0]
    chosen = route_ids == own_index
    gate_own = jnp.sum(jnp.where(chosen, gates, 0.0), axis=1)

    gate_groups = [gate_own] + [
        lax.ppermute(gate_own, "dp", [(i, (i + k) % groups) for i in range(groups)])
        for k in range(1, groups)
    ]
    position = lax.axis_index("dp")
    gate_ring = jnp.stack(gate_groups)
    gate_all = jnp.take(gate_ring, (position - jnp.arange(groups)) % groups, axis=0).reshape(-1)
    gate_peer = swap(gate_all)
    out_keep = mine(out_mat, 1)
    out_peer = swap(other(out_mat, 1))

    lat_own = spread(mine(latent, 1), "dp").reshape(groups * rows, half)
    lat_all = joined(lat_own, swap(lat_own), 1)
    gate_pre = dot(lat_all, gate_mat, 1, 0)
    up_pre = dot(lat_all, up_mat, 1, 0)
    active = (jax.nn.silu(gate_pre) * up_pre).astype(bf16)
    active_peer = swap(active)
    part = dot(active, out_keep, 1, 0) * gate_all[:, None]
    part = part + dot(active_peer, out_peer, 1, 0) * gate_peer[:, None]
    summed = jnp.sum(deal(part, "dp").reshape(groups, rows, half), axis=0)
    summed, gate_mat, up_mat, out_mat = lax.optimization_barrier(
        (summed, gate_mat, up_mat, out_mat)
    )
    gate_full = lax.all_gather(gate_mat, "dp")
    up_full = lax.all_gather(up_mat, "dp")
    out_full = lax.all_gather(out_mat, "dp")

    comb_rows = jnp.sum(deal(summed, plane).reshape(places, chunk, half), axis=0).astype(bf16)
    comb_own = spread(comb_rows, plane).reshape(rows, half)
    combined = joined(comb_own, swap(comb_own), 1)
    lifted_t = dot(w_lift, combined, 0, 1)
    hidden_t = (residual.T.astype(f32) + lifted_t).astype(bf16)
    hid_own = spread(hidden_t, plane)
    hid_peer = swap(hid_own)
    hidden_all = joined(hid_own[:, None], hid_peer[:, None], 1).reshape(model, rows)
    hidden_float = hidden_all.astype(f32)
    scale_inv = lax.rsqrt(jnp.mean(hidden_float * hidden_float, axis=0) + norm_epsilon)
    gain_float = norm_gain.astype(f32)
    normed_t = (hidden_float * scale_inv[None, :] * gain_float[:, None]).astype(bf16)
    logits = dot(normed_t, w_vocab, 0, 0)

    word_range = jnp.arange(words, dtype=jnp.int32)
    is_target = targets[:, None] - own_index * words == word_range[None, :]
    target_part = jnp.sum(jnp.where(is_target, logits, 0.0), axis=1)
    peak_part = jnp.max(logits, axis=1)
    below = logits - peak_part[:, None]
    weight = jnp.exp(below)
    total_part = jnp.sum(weight, axis=1)
    lean_part = jnp.sum(weight * below, axis=1)
    stats = jnp.stack([peak_part, total_part, lean_part, target_part]).reshape(-1, 128)
    stats = spread(stats, slab).reshape(-1, 4, rows)
    row_peak = jnp.max(stats[:, 0], axis=0)
    gap = stats[:, 0] - row_peak[None, :]
    share = jnp.exp(gap)
    row_total = jnp.sum(share * stats[:, 1], axis=0)
    lean = jnp.sum(share * (stats[:, 2] + gap * stats[:, 1]), axis=0)
    target_logit = jnp.sum(stats[:, 3], axis=0)
    row_loss = row_peak + jnp.log(row_total) - target_logit
    inner = loss_cot * (lean / row_total - (target_logit - row_peak))

    probs = jnp.exp(logits - row_peak[:, None]) / row_total[:, None]
    logit_grad = (loss_cot[:, None] * (probs - is_target.astype(f32))).astype(bf16)
    grad_t = dot(w_vocab, logit_grad, 1, 1).reshape(places, 2, cols, rows)
    keep_t = jnp.where(first, grad_t[:, 0], grad_t[:, 1])
    send_t = jnp.where(first, grad_t[:, 1], grad_t[:, 0]).astype(bf16)
    keep_t = (keep_t + swap(send_t).astype(f32)).astype(bf16)
    normed_grad = jnp.sum(deal(keep_t, plane).astype(f32), axis=0)
    gain_own = lax.dynamic_slice_in_dim(gain_float, own_index * cols, cols, 0)
    d_res_t = (
        scale_inv[None, :] * (normed_grad * gain_own[:, None])
        - hidden_t.astype(f32) * (scale_inv**2 * (inner / model))[None, :]
    )
    d_residual = d_res_t.T
    d_res_bf = d_res_t.astype(bf16)
    lift_keep = mine(w_lift, 0)
    lift_peer = swap(other(w_lift, 0))
    cg_part = dot(d_res_bf, lift_keep, 0, 1) + dot(swap(d_res_bf), lift_peer, 0, 1)
    cg_rows = deal(cg_part.astype(bf16), plane).astype(f32)
    cg_rows = jnp.sum(cg_rows.reshape(places, chunk, half), axis=0).astype(bf16)
    cg_own = spread(cg_rows, plane).reshape(rows, half)
    comb_grad = joined(cg_own, swap(cg_own), 1)

    gate_pre = jnp.einsum("tl,qlf->qtf", latent, gate_full, preferred_element_type=f32)
    up_pre = jnp.einsum("tl,qlf->qtf", latent, up_full, preferred_element_type=f32)
    sig = jax.nn.sigmoid(gate_pre)
    active = (gate_pre * sig * up_pre).astype(bf16)
    routed_grad = (comb_grad.astype(f32) * gate_own[:, None]).astype(bf16)
    act_grad = jnp.einsum("tl,qfl->qtf", routed_grad, out_full, preferred_element_type=f32)
    gate_term = jnp.sum(act_grad * active.astype(f32), axis=(0, 2))
    gate_term = gate_term / jnp.where(gate_own > 0, gate_own, 1.0)
    gate_back = (act_grad * up_pre * sig * (1.0 + gate_pre * (1.0 - sig))).astype(bf16)
    up_back = (act_grad * gate_pre * sig).astype(bf16)
    block = jnp.einsum("qtf,qlf->tl", gate_back, gate_full, preferred_element_type=f32)
    block = block + jnp.einsum("qtf,qlf->tl", up_back, up_full, preferred_element_type=f32)
    gate_grad = jnp.where(chosen, gate_term[:, None], 0.0)
    gate_grad = jnp.pad(gate_grad, ((0, 0), (0, 128 - gate_grad.shape[1])))
    keep = jnp.concatenate([mine(block, 1), gate_grad], axis=1)
    send = jnp.concatenate([other(block, 1), gate_grad], axis=1).astype(bf16)
    keep = (keep + swap(send).astype(f32)).astype(bf16)
    tail = jnp.sum(deal(keep, plane).astype(f32).reshape(places, chunk, -1), axis=0).astype(bf16)
    tail = spread(tail, plane).reshape(rows, -1)
    d_latent = joined(tail[:, :half], swap(tail[:, :half]), 1).astype(f32)
    d_gates = tail[:, half : half + gates.shape[1]].astype(f32)
    return (row_loss, d_residual, d_latent, d_gates)


def solution(mesh):
    fine = Mesh(mesh.devices.reshape(mesh.devices.shape[0], 8, 4, 2), ("dp", "z", "y", "c"))
    in_specs = (
        P("dp", None),
        P("dp", slab),
        P("dp", None),
        P("dp", None),
        P(slab, None, "dp"),
        P(slab, None, "dp"),
        P(slab, "dp", None),
        P(None, slab),
        P(),
        P(None, slab),
        P("dp"),
        P("dp"),
    )
    out_specs = (P("dp"), P("dp", slab), P("dp", None), P("dp", None))
    return jax.shard_map(
        on_device, mesh=fine, in_specs=in_specs, out_specs=out_specs, check_vma=False
    )
```

time: 1490 us -> 336 us (0.23)
  blocking collectives: 1010 us -> 162 us
  waiting for transfers between devices: 408 us -> 56 us
  starting transfers between devices: 0.29 us -> 42.9 us
    psum x4 -> x0, blocking collectives: 883 us -> none  [the longest x2 373 us: on_device(): row_total, target_logit = lax.psum((total_part, target_part), 'expert')]
    psum x2 -> x0, waiting for transfers between devices: 188 us -> none  [the longest x1 188 us: on_device(): full_grad = lax.psum(normed_grad, 'expert')]
    all_to_all x0 -> x8, blocking collectives: none -> 162 us  [deal(): return lax.all_to_all(x, axes, 0, 0, tiled=True)]
    all_gather x3, waiting for transfers between devices: 140 us -> 0.02 us  [the longest x1 0.02 us: on_device(): up_full = lax.all_gather(up_mat, 'dp')]
    pmax x1 -> x0, blocking collectives: 124 us -> none  [on_device(): row_peak = lax.pmax(top_part, 'expert')]
    reduce_scatter x2 -> x0, waiting for transfers between devices: 80.3 us -> none  [the longest x1 40.2 us: on_device(): lax.psum_scatter(jnp.dot(active, out_mat, preferred_element_type=jnp.floa...]
    all_to_all x0 -> x3, waiting for transfers between devices: none -> 46.5 us  [deal(): return lax.all_to_all(x, axes, 0, 0, tiled=True)]
    ppermute x0 -> x15, starting transfers between devices: none -> 22.9 us  [the longest x12 20.7 us: swap(): return lax.ppermute(x, 'c', [(0, 1), (1, 0)])]
  transfers between devices with their start and end apart: 7 -> 21, of which waited for: 6 -> 9; matrix products, arithmetic and copies ran while one was open for 0% -> 14% of each run, Pallas kernels for 0% -> 0%
where the time goes in v1:
time: 336 us; the launch traced here: 334 us
  blocking collectives  162 us (48%)
  waiting for transfers between devices  56 us (17%)
  starting transfers between devices  42.9 us (13%)
  matrix products  35.3 us (11%)
  other arithmetic  14.9 us (4%)
  between operations  14.2 us (4%)
  local copies, waits for them, and re-layouts  9.1 us (3%)
    all_to_all x8, blocking collectives, deal(): return lax.all_to_all(x, axes, 0, 0, tiled=True)  162 us
    all_to_all x3, waiting for transfers between devices, deal(): return lax.all_to_all(x, axes, 0, 0, tiled=True)  46.5 us
    dot_general x9, matrix products, dot(): lax.dot_general(a, b, (((ca,), (cb,)), ((), ())), preferred_element_type=...  22.9 us
    ppermute x12, starting transfers between devices, swap(): return lax.ppermute(x, 'c', [(0, 1), (1, 0)])  20.7 us
    all_to_all x3, starting transfers between devices, deal(): return lax.all_to_all(x, axes, 0, 0, tiled=True)  19.9 us
    ppermute x12, waiting for transfers between devices, swap(): return lax.ppermute(x, 'c', [(0, 1), (1, 0)])  8.06 us
  transfers between devices with their start and end apart: 21, of which 9 were waited for; matrix products, arithmetic and copies ran while one was open for 14% of the time, Pallas kernels for 0%

profile of v1, /device:TPU:1, one launch (start us, length us, event | category | flops | bytes accessed | tf_op | source)
XLA Modules:
  0.0 334.5 jit_solution(4589189604598202725)
XLA Ops:
  7.2 1.1 slice_select_fusion.1
  8.4 18.9 %all_to_all.71 = bf16[4,256,512]{2,1,0:T(8,128)(2,1)S(1)} all-to-all(bf16[4,256,512]{2,1,0:T(8,128)(2,1)S(1)} %broadcast_in_dim.45), channel_id=1, replica_groups=mesh['dp'=4,'z'=8,'y'=4,'c'=2] {'dp'}, dimensions={0} | all-to-all | bytes 2097152 | tf_op jit(solution)/shard_map/all_to_all | solution.py:22
  27.3 1.9 collective-permute-start
  29.6 1.0 collective-permute-start.3
  30.5 1.2 collective-permute-start.2
  31.8 0.7 collective-permute-start.5
  32.5 2.6 fusion.62
  35.1 2.8 multiply_convert_fusion.3
  38.0 0.6 gather_fusion
  38.7 0.5 collective-permute-start.6
  39.2 0.7 fusion.63
  40.1 1.7 multiply_add_fusion
  41.9 30.2 %all_to_all.72 = f32[4,256,512]{2,1,0:T(8,128)S(1)} all-to-all(f32[4,256,512]{2,1,0:T(8,128)S(1)} %bitcast.131), channel_id=1, replica_groups=mesh['dp'=4,'z'=8,'y'=4,'c'=2] {'dp'}, dimensions={0} | all-to-all | bytes 4194304 | tf_op jit(solution)/shard_map/all_to_all | solution.py:22
  72.1 1.0 reduce_sum.133
  73.1 11.3 %all-to-all-start.2 = ((f32[32,8,512]{2,1,0:T(8,128)}), f32[32,8,512]{2,1,0:T(8,128)S(1)}, u32[]{:S(2)}, u32[]{:S(2)}) async-start(f32[32,8,512]{2,1,0:T(8,128)} %bitcast.10), calls=%async_computation.2 | async-start | bytes 1048576 | tf_op jit(solution)/shard_map/all_to_all | solution.py:22
  84.5 0.7 all-gather.9.cloned.1.call-update
  85.2 14.6 %all-to-all-done.2 = f32[32,8,512]{2,1,0:T(8,128)S(1)} async-done(((f32[32,8,512]{2,1,0:T(8,128)}), f32[32,8,512]{2,1,0:T(8,128)S(1)}, u32[]{:S(2)}, u32[]{:S(2)}) %all-to-all-start.2) | async-done | bytes 524320 | tf_op jit(solution)/shard_map/all_to_all | solution.py:22
  99.9 16.3 %all_to_all.73 = bf16[32,8,512]{2,1,0:T(8,128)(2,1)S(1)} all-to-all(bf16[32,8,512]{2,1,0:T(8,128)(2,1)S(1)} %broadcast_in_dim.50), channel_id=1, replica_groups=mesh['dp'=4,'z'=8,'y'=4,'c'=2] {'z','y'}, dimensions={0} | all-to-all | bytes 524288 | tf_op jit(solution)/shard_map/all_to_all | solution.py:22
  116.2 3.8 %collective-permute-start.7 = (bf16[256,512]{1,0:T(8,128)(2,1)S(1)}, bf16[256,512]{1,0:T(8,128)(2,1)S(1)}, u32[]{:S(2)}, u32[]{:S(2)}) collective-permute-start(bf16[256,512]{1,0:T(8,128)(2,1)S(1)} %bitcast.147), channel_id=1, source_target_pairs={{0,1},{1,0},{2,3},{3,2},{4,5},{5,4},{6,7},{7,6},{8,9},{9,8},{10,11... | collective-permute-start | bytes 786440 | tf_op jit(solution)/shard_map/ppermute | solution.py:18
  120.0 1.2 collective-permute-done.7
  121.1 0.3 fusion.33
  121.6 29.4 %all_to_all.74 = bf16[32,64,256]{2,1,0:T(8,128)(2,1)S(1)} all-to-all(bf16[32,64,256]{2,1,0:T(8,128)(2,1)S(1)} %broadcast_in_dim.51), channel_id=1, replica_groups=mesh['dp'=4,'z'=8,'y'=4,'c'=2] {'z','y'}, dimensions={0} | all-to-all | bytes 2097152 | tf_op jit(solution)/shard_map/all_to_all | solution.py:22
  151.0 2.7 collective-permute-start.8
  153.7 2.2 collective-permute-done.8
  155.9 0.3 fusion.14
  156.2 1.0 multiply_reduce_fusion
  157.2 1.0 fusion.1
  158.2 6.3 %fusion.89 = (f32[256]{0:T(256)S(1)}, f32[256,1024]{1,0:T(8,128)S(1)}) fusion(bf16[4096,256]{1,0:T(8,128)(2,1)S(1)} %fusion.1, bf16[4096,1024]{1,0:T(8,128)(2,1)} %param.21), kind=kOutput, calls=%fused_computation.145 | convolution fusion | flops 2147745536 | bytes 11535360 | tf_op jit(solution)/shard_map/dot_general | solution.py:14
  164.5 0.6 exponential_reduce_fusion
  165.1 18.7 %all_to_all.75 = f32[64,8,128]{2,1,0:T(8,128)S(1)} all-to-all(f32[64,8,128]{2,1,0:T(8,128)S(1)} %broadcast_in_dim.100), channel_id=1, replica_groups=mesh['dp'=4,'z'=8,'y'=4,'c'=2] {'z','y','c'}, dimensions={0} | all-to-all | bytes 524288 | tf_op jit(solution)/shard_map/all_to_all | solution.py:22
  183.9 0.2 slice_reduce_fusion.1
  184.2 8.0 %convolution_bitcast_fusion = f32[4096,256]{0,1:T(8,128)} fusion(bf16[4096,1024]{1,0:T(8,128)(2,1)} %param.21, f32[256,1024]{1,0:T(8,128)S(1)} %get-tuple-element.43, f32[256]{0:T(256)S(1)} %get-tuple-element.34, f32[256]{0:T(256)S(1)} %get-tuple-element.31, f32[256]{0:T(256)S(1)} %copy-done.9, s32[256]{0:T(256)S(1)} %broadcast_subtract_fusion), kind=kOutput, calls=%fused_computation.1 | convolution fusion | flops 2149318656 | bytes 13635584 | tf_op jit(solution)/shard_map/dot_general | solution.py:14
  192.1 5.6 %copy.49 = f32[4096,256]{1,0:T(8,128)} copy(f32[4096,256]{0,1:T(8,128)} %convolution_bitcast_fusion) | data formatting | bytes 8388608 | tf_op jit(solution)/shard_map/dot_general | solution.py:14
  197.7 2.4 fusion.35
  200.2 0.4 collective-permute-start.9
  200.5 2.4 collective-permute-done.9
  202.9 3.8 %fusion.15 = bf16[32,64,256]{2,1,0:T(8,128)(2,1)} fusion(bf16[32,64,256]{2,1,0:T(8,128)(2,1)S(1)} %collective-permute-done.9, f32[32,2,64,256]{3,2,1,0:T(8,128)} %bitcast.128, pred[]{:T(512)S(6)} %eq.24), kind=kLoop, calls=%fused_computation.22 | loop fusion | flops 2097152 | bytes 6291457 | tf_op jit(solution)/shard_map/convert_element_type | solution.py:140
  206.7 3.9 %all-to-all-start.6 = ((bf16[32,64,256]{2,1,0:T(8,128)(2,1)}), bf16[32,64,256]{2,1,0:T(8,128)(2,1)S(1)}, u32[]{:S(2)}, u32[]{:S(2)}) async-start(bf16[32,64,256]{2,1,0:T(8,128)(2,1)} %fusion.15), calls=%async_computation.6 | async-start | bytes 2097152 | tf_op jit(solution)/shard_map/all_to_all | solution.py:22
  210.7 0.7 all-gather.7.cloned.1.call-update
  211.4 0.7 collective-permute-start.11
  212.2 0.6 multiply_multiply_fusion.1
  212.8 24.2 %all-to-all-done.6 = bf16[32,64,256]{2,1,0:T(8,128)(2,1)S(1)} async-done(((bf16[32,64,256]{2,1,0:T(8,128)(2,1)}), bf16[32,64,256]{2,1,0:T(8,128)(2,1)S(1)}, u32[]{:S(2)}, u32[]{:S(2)}) %all-to-all-start.6) | async-done | bytes 1048608 | tf_op jit(solution)/shard_map/all_to_all | solution.py:22
  237.2 2.8 collective-permute-start.10
  240.0 0.2 fusion.72
  240.2 0.6 collective-permute-done.10
  240.8 0.2 fusion.32
  241.1 16.7 %all_to_all.76 = bf16[32,8,512]{2,1,0:T(8,128)(2,1)S(1)} all-to-all(bf16[32,8,512]{2,1,0:T(8,128)(2,1)S(1)} %fusion.32), channel_id=1, replica_groups=mesh['dp'=4,'z'=8,'y'=4,'c'=2] {'z','y'}, dimensions={0} | all-to-all | bytes 524288 | tf_op jit(solution)/shard_map/all_to_all | solution.py:22
  257.9 0.7 broadcast_in_dim.101
  258.6 4.6 %all-to-all-start.8 = ((bf16[32,8,512]{2,1,0:T(8,128)(2,1)}), bf16[32,8,512]{2,1,0:T(8,128)(2,1)S(1)}, u32[]{:S(2)}, u32[]{:S(2)}) async-start(bf16[32,8,512]{2,1,0:T(8,128)(2,1)} %broadcast_in_dim.101), calls=%async_computation.8 | async-start | bytes 524288 | tf_op jit(solution)/shard_map/all_to_all | solution.py:22
  263.2 2.7 fusion.16
  265.9 7.8 %all-to-all-done.8 = bf16[32,8,512]{2,1,0:T(8,128)(2,1)S(1)} async-done(((bf16[32,8,512]{2,1,0:T(8,128)(2,1)}), bf16[32,8,512]{2,1,0:T(8,128)(2,1)S(1)}, u32[]{:S(2)}, u32[]{:S(2)}) %all-to-all-start.8) | async-done | bytes 262176 | tf_op jit(solution)/shard_map/all_to_all | solution.py:22
  273.7 3.4 %collective-permute-start.12 = (bf16[256,512]{1,0:T(8,128)(2,1)S(1)}, bf16[256,512]{1,0:T(8,128)(2,1)S(1)}, u32[]{:S(2)}, u32[]{:S(2)}) collective-permute-start(bf16[256,512]{1,0:T(8,128)(2,1)S(1)} %bitcast.145), channel_id=1, source_target_pairs={{0,1},{1,0},{2,3},{3,2},{4,5},{5,4},{6,7},{7,6},{8,9},{9,8},{10,11... | collective-permute-start | bytes 786440 | tf_op jit(solution)/shard_map/ppermute | solution.py:18
  277.1 3.8 %fusion.19 = f32[4,256,336]{1,2,0:T(8,128)} fusion(bf16[42,4,8,1024]{3,2,1,0:T(8,128)(2,1)} %bitcast.161, bf16[256,1024]{1,0:T(8,128)(2,1)S(1)} %copy-done.3), kind=kOutput, calls=%fused_computation.29 | convolution fusion | flops 704643072 | bytes 4653056 | tf_op jit(solution)/shard_map/tl,qlf->qtf/dot_general | solution.py:157
  280.9 3.5 %multiply_reduce_fusion.1 = (f32[256]{0:T(256)S(1)}, f32[4,256,336]{1,2,0:T(8,128)S(1)}) fusion(f32[4,256,336]{1,2,0:T(8,128)S(1)} %fusion.16, f32[4,256,336]{1,2,0:T(8,128)} %fusion.19, bf16[4,336,1024]{2,1,0:T(8,128)(2,1)} %bitcast.163, bf16[256,512]{1,0:T(8,128)(2,1)S(1)} %collective-permute-done.12, bf16[256,512]{1,0:T(8,128)(2,1)S(1)} %bitcast.146, ...), kind=kOutput, calls=%fused_computation.31 | convolution fusion | flops 710885120 | bytes 7407617 | tf_op jit(solution)/shard_map/tl,qfl->qtf/dot_general | solution.py:162
  284.6 1.1 fusion.22
  285.6 0.7 copy-done.11
  286.3 1.4 fusion.28
  288.0 1.5 collective-permute-done.13
  289.6 16.3 %all_to_all.77 = bf16[32,8,640]{2,1,0:T(8,128)(2,1)S(1)} all-to-all(bf16[32,8,640]{2,1,0:T(8,128)(2,1)S(1)} %fusion.66), channel_id=1, replica_groups=mesh['dp'=4,'z'=8,'y'=4,'c'=2] {'z','y'}, dimensions={0} | all-to-all | bytes 655360 | tf_op jit(solution)/shard_map/all_to_all | solution.py:22
  306.1 15.6 %all_to_all.78 = bf16[32,8,640]{2,1,0:T(8,128)(2,1)S(1)} all-to-all(bf16[32,8,640]{2,1,0:T(8,128)(2,1)S(1)} %broadcast_in_dim.104), channel_id=1, replica_groups=mesh['dp'=4,'z'=8,'y'=4,'c'=2] {'z','y'}, dimensions={0} | all-to-all | bytes 655360 | tf_op jit(solution)/shard_map/all_to_all | solution.py:22
  321.7 3.8 %collective-permute-start.14 = (bf16[256,512]{1,0:T(8,128)(2,1)S(1)}, bf16[256,512]{1,0:T(8,128)(2,1)S(1)}, u32[]{:S(2)}, u32[]{:S(2)}) collective-permute-start(bf16[256,512]{1,0:T(8,128)(2,1)S(1)} %slice.45), channel_id=1, source_target_pairs={{0,1},{1,0},{2,3},{3,2},{4,5},{5,4},{6,7},{7,6},{8,9},{9,8},{10,11... | collective-permute-start | bytes 786440 | tf_op jit(solution)/shard_map/ppermute | solution.py:18
  325.4 0.7 bitcast_subtract_fusion
  326.1 0.7 copy.54
  326.8 1.1 fusion.51
  (86 shorter events, 2.5 us)
Async XLA Ops:
  7.2 22.0 %copy-start.5 = (f32[256,22]{0,1:T(8,128)S(1)}, f32[256,22]{0,1:T(8,128)}, u32[]{:S(2)}) copy-start(f32[256,22]{0,1:T(8,128)} %param.14) | copy-start | bytes 67588
  7.2 22.1 %copy-start.6 = (s32[256,22]{0,1:T(8,128)S(1)}, s32[256,22]{0,1:T(8,128)}, u32[]{:S(2)}) copy-start(s32[256,22]{0,1:T(8,128)} %param.15) | copy-start | bytes 67588
  8.3 23.4 %copy-start = (bf16[1,336,1024]{2,1,0:T(8,128)(2,1)S(1)}, bf16[1,336,1024]{2,1,0:T(8,128)(2,1)}, u32[]{:S(2)}) copy-start(bf16[1,336,1024]{2,1,0:T(8,128)(2,1)} %param.18) | copy-start | bytes 2064388
  8.4 24.1 %copy-start.2 = (bf16[1,1024,336]{1,2,0:T(8,128)(2,1)S(1)}, bf16[1,1024,336]{1,2,0:T(8,128)(2,1)}, u32[]{:S(2)}) copy-start(bf16[1,1024,336]{1,2,0:T(8,128)(2,1)} %param.16) | copy-start | bytes 2064388
  27.3 5.2 %collective-permute-start = (bf16[1024,512]{1,0:T(8,128)(2,1)S(1)}, bf16[1024,512]{1,0:T(8,128)(2,1)}, u32[]{:S(2)}, u32[]{:S(2)}) collective-permute-start(bf16[1024,512]{1,0:T(8,128)(2,1)S(1)} %bitcast.139), channel_id=1, source_target_pairs={{0,1},{1,0},{2,3},{3,2},{4,5},{5,4},{6,7},{7,6},{8,9},{9,8},{10,11... | collective-permute-start | bytes 3145736 | tf_op jit(solution)/shard_map/ppermute | solution.py:18
  29.6 8.4 %collective-permute-start.3 = (f32[256]{0:T(256)S(1)}, f32[256]{0:T(256)S(1)}, u32[]{:S(2)}, u32[]{:S(2)}) collective-permute-start(f32[256]{0:T(256)S(1)} %get-tuple-element.35), channel_id=1, source_target_pairs={{0,192},{64,0},{128,64},{192,128},{1,193},{65,1},{129,65},{193,129... | collective-permute-start | bytes 3080 | tf_op jit(solution)/shard_map/ppermute | solution.py:76
  30.5 7.5 %collective-permute-start.2 = (f32[256]{0:T(256)S(1)}, f32[256]{0:T(256)S(1)}, u32[]{:S(2)}, u32[]{:S(2)}) collective-permute-start(f32[256]{0:T(256)S(1)} %get-tuple-element.35), channel_id=1, source_target_pairs={{0,128},{64,192},{128,0},{192,64},{1,129},{65,193},{129,1},{193,65... | collective-permute-start | bytes 3080 | tf_op jit(solution)/shard_map/ppermute | solution.py:76
  31.7 6.3 %collective-permute-start.1 = (f32[256]{0:T(256)S(1)}, f32[256]{0:T(256)S(1)}, u32[]{:S(2)}, u32[]{:S(2)}) collective-permute-start(f32[256]{0:T(256)S(1)} %get-tuple-element.35), channel_id=1, source_target_pairs={{0,64},{64,128},{128,192},{192,0},{1,65},{65,129},{129,193},{193,1... | collective-permute-start | bytes 3080 | tf_op jit(solution)/shard_map/ppermute | solution.py:76
  31.8 8.4 %collective-permute-start.5 = (bf16[336,512]{1,0:T(8,128)(2,1)S(1)}, bf16[336,512]{1,0:T(8,128)(2,1)}, u32[]{:S(2)}, u32[]{:S(2)}) collective-permute-start(bf16[336,512]{1,0:T(8,128)(2,1)S(1)} %broadcast_select_fusion), channel_id=1, source_target_pairs={{0,1},{1,0},{2,3},{3,2},{4,5},{5,4},{6,7},{7,6},{8,9},{9,8},{10,11... | collective-permute-start | bytes 1032200 | tf_op jit(solution)/shard_map/ppermute | solution.py:18
  32.4 2.7 copy-start.1
  37.9 2.2 collective-permute-start.4
  38.7 1.4 collective-permute-start.6
  73.1 48.0 %copy-start.4 = (bf16[1024,64]{0,1:T(8,128)(2,1)S(1)}, bf16[1024,64]{0,1:T(8,128)(2,1)}, u32[]{:S(2)}) copy-start(bf16[1024,64]{0,1:T(8,128)(2,1)} %param.19) | copy-start | bytes 393220
  73.1 48.0 %copy-start.12 = (bf16[256,64]{0,1:T(8,128)(2,1)S(1)}, bf16[256,64]{0,1:T(8,128)(2,1)}, u32[]{:S(2)}) copy-start(bf16[256,64]{0,1:T(8,128)(2,1)} %param.13) | copy-start | bytes 98308
  73.1 26.7 %all-to-all-start.2 = ((f32[32,8,512]{2,1,0:T(8,128)}), f32[32,8,512]{2,1,0:T(8,128)S(1)}, u32[]{:S(2)}, u32[]{:S(2)}) async-start(f32[32,8,512]{2,1,0:T(8,128)} %bitcast.10), calls=%async_computation.2 | async-start | bytes 1048576 | tf_op jit(solution)/shard_map/all_to_all | solution.py:22
  84.5 178.7 %all-gather.9.cloned.1.call-start = ((), (), s32[]{:S(2)}) async-start(), calls=%async_computation.12 | async-start | bytes 3440640 | tf_op jit(solution)/shard_map/all_gather | solution.py:99
  85.2 191.9 %all-gather.11.cloned.1.call-start = ((), (), s32[]{:S(2)}) async-start(), calls=%async_computation.13 | async-start | bytes 3440640 | tf_op jit(solution)/shard_map/all_gather | solution.py:98
  116.2 4.9 %collective-permute-start.7 = (bf16[256,512]{1,0:T(8,128)(2,1)S(1)}, bf16[256,512]{1,0:T(8,128)(2,1)S(1)}, u32[]{:S(2)}, u32[]{:S(2)}) collective-permute-start(bf16[256,512]{1,0:T(8,128)(2,1)S(1)} %bitcast.147), channel_id=1, source_target_pairs={{0,1},{1,0},{2,3},{3,2},{4,5},{5,4},{6,7},{7,6},{8,9},{9,8},{10,11... | collective-permute-start | bytes 786440 | tf_op jit(solution)/shard_map/ppermute | solution.py:18
  121.4 32.2 %copy-start.7 = (bf16[4096]{0:T(1024)(128)(2,1)S(1)}, bf16[4096]{0:T(1024)(128)(2,1)}, u32[]{:S(2)}) copy-start(bf16[4096]{0:T(1024)(128)(2,1)} %param.20) | copy-start | bytes 24580
  121.4 32.2 %copy-start.8 = (s32[256]{0:T(256)S(1)}, s32[256]{0:T(256)}, u32[]{:S(2)}) copy-start(s32[256]{0:T(256)} %param.22) | copy-start | bytes 3076
  151.0 5.0 %collective-permute-start.8 = (bf16[32,64,256]{2,1,0:T(8,128)(2,1)S(1)}, bf16[32,64,256]{2,1,0:T(8,128)(2,1)S(1)}, u32[]{:S(2)}, u32[]{:S(2)}) collective-permute-start(bf16[32,64,256]{2,1,0:T(8,128)(2,1)S(1)} %all_to_all.74), channel_id=1, source_target_pairs={{0,1},{1,0},{2,3},{3,2},{4,5},{5,4},{6,7},{7,6},{8,9},{9,8},{10,11... | collective-permute-start | bytes 3145736 | tf_op jit(solution)/shard_map/ppermute | solution.py:18
  164.5 19.7 %copy-start.9 = (f32[256]{0:T(256)S(1)}, f32[256]{0:T(256)}, u32[]{:S(2)}) copy-start(f32[256]{0:T(256)} %param.23) | copy-start | bytes 3076
  200.2 2.7 collective-permute-start.9
  206.7 30.3 %all-to-all-start.6 = ((bf16[32,64,256]{2,1,0:T(8,128)(2,1)}), bf16[32,64,256]{2,1,0:T(8,128)(2,1)S(1)}, u32[]{:S(2)}, u32[]{:S(2)}) async-start(bf16[32,64,256]{2,1,0:T(8,128)(2,1)} %fusion.15), calls=%async_computation.6 | async-start | bytes 2097152 | tf_op jit(solution)/shard_map/all_to_all | solution.py:22
  210.7 70.2 %all-gather.7.cloned.1.call-start = ((), (), s32[]{:S(2)}) async-start(), calls=%async_computation.11 | async-start | bytes 3440640 | tf_op jit(solution)/shard_map/all_gather | solution.py:100
  211.4 28.8 %collective-permute-start.11 = (bf16[512,64]{0,1:T(8,128)(2,1)S(1)}, bf16[512,64]{0,1:T(8,128)(2,1)S(1)}, u32[]{:S(2)}, u32[]{:S(2)}) collective-permute-start(bf16[512,64]{0,1:T(8,128)(2,1)S(1)} %broadcast_select_fusion.2), channel_id=1, source_target_pairs={{0,1},{1,0},{2,3},{3,2},{4,5},{5,4},{6,7},{7,6},{8,9},{9,8},{10,11... | collective-permute-start | bytes 196616 | tf_op jit(solution)/shard_map/ppermute | solution.py:18
  212.8 50.4 %copy-start.3 = (bf16[256,1024]{1,0:T(8,128)(2,1)S(1)}, bf16[256,1024]{1,0:T(8,128)(2,1)}, u32[]{:S(2)}) copy-start(bf16[256,1024]{1,0:T(8,128)(2,1)} %param.12) | copy-start | bytes 1572868
  237.2 3.6 %collective-permute-start.10 = (bf16[64,256]{1,0:T(8,128)(2,1)S(1)}, bf16[64,256]{1,0:T(8,128)(2,1)S(1)}, u32[]{:S(2)}, u32[]{:S(2)}) collective-permute-start(bf16[64,256]{1,0:T(8,128)(2,1)S(1)} %subtract_convert_fusion), channel_id=1, source_target_pairs={{0,1},{1,0},{2,3},{3,2},{4,5},{5,4},{6,7},{7,6},{8,9},{9,8},{10,11... | collective-permute-start | bytes 98312 | tf_op jit(solution)/shard_map/ppermute | solution.py:18
  258.6 15.1 %all-to-all-start.8 = ((bf16[32,8,512]{2,1,0:T(8,128)(2,1)}), bf16[32,8,512]{2,1,0:T(8,128)(2,1)S(1)}, u32[]{:S(2)}, u32[]{:S(2)}) async-start(bf16[32,8,512]{2,1,0:T(8,128)(2,1)} %broadcast_in_dim.101), calls=%async_computation.8 | async-start | bytes 524288 | tf_op jit(solution)/shard_map/all_to_all | solution.py:22
  273.7 7.2 %collective-permute-start.12 = (bf16[256,512]{1,0:T(8,128)(2,1)S(1)}, bf16[256,512]{1,0:T(8,128)(2,1)S(1)}, u32[]{:S(2)}, u32[]{:S(2)}) collective-permute-start(bf16[256,512]{1,0:T(8,128)(2,1)S(1)} %bitcast.145), channel_id=1, source_target_pairs={{0,1},{1,0},{2,3},{3,2},{4,5},{5,4},{6,7},{7,6},{8,9},{9,8},{10,11... | collective-permute-start | bytes 786440 | tf_op jit(solution)/shard_map/ppermute | solution.py:18
  280.9 3.7 %copy-start.10 = (bf16[4096,336]{0,1:T(8,128)(2,1)S(1)}, bf16[4096,336]{0,1:T(8,128)(2,1)}, u32[]{:S(2)}) copy-start(bf16[4096,336]{0,1:T(8,128)(2,1)} %all-gather.9.cloned.1.call-done) | copy-start | bytes 8257540
  280.9 3.7 %copy-start.13 = (f32[4,256,336]{1,2,0:T(8,128)S(1)}, f32[4,256,336]{1,2,0:T(8,128)}, u32[]{:S(2)}) copy-start(f32[4,256,336]{1,2,0:T(8,128)} %fusion.19) | copy-start | bytes 4128772
  284.5 1.8 copy-start.11
  287.8 1.7 collective-permute-start.13
  321.7 5.2 %collective-permute-start.14 = (bf16[256,512]{1,0:T(8,128)(2,1)S(1)}, bf16[256,512]{1,0:T(8,128)(2,1)S(1)}, u32[]{:S(2)}, u32[]{:S(2)}) collective-permute-start(bf16[256,512]{1,0:T(8,128)(2,1)S(1)} %slice.45), channel_id=1, source_target_pairs={{0,1},{1,0},{2,3},{3,2},{4,5},{5,4},{6,7},{7,6},{8,9},{9,8},{10,11... | collective-permute-start | bytes 786440 | tf_op jit(solution)/shard_map/ppermute | solution.py:18
Sparse Core Ops, SparseCore 0:
  87.1 39.1 all-gather.8
  153.8 33.4 all-gather.10
  213.3 38.1 all-gather.6

commit v2 on v1

--- a/solution.py
+++ b/solution.py
@@ -44,7 +44,6 @@
     core = lax.axis_index("c")
     own_index = lax.axis_index(slab)
     places = lax.axis_size(plane)
-    groups = lax.axis_size("dp")
     rows, width = latent.shape
     half = width // 2
     cols = residual.shape[1]
@@ -72,32 +71,20 @@
     chosen = route_ids == own_index
     gate_own = jnp.sum(jnp.where(chosen, gates, 0.0), axis=1)
 
-    gate_groups = [gate_own] + [
-        lax.ppermute(gate_own, "dp", [(i, (i + k) % groups) for i in range(groups)])
-        for k in range(1, groups)
-    ]
-    position = lax.axis_index("dp")
-    gate_ring = jnp.stack(gate_groups)
-    gate_all = jnp.take(gate_ring, (position - jnp.arange(groups)) % groups, axis=0).reshape(-1)
-    gate_peer = swap(gate_all)
-    out_keep = mine(out_mat, 1)
-    out_peer = swap(other(out_mat, 1))
+    out_full = lax.all_gather(out_mat, "dp")
 
-    lat_own = spread(mine(latent, 1), "dp").reshape(groups * rows, half)
-    lat_all = joined(lat_own, swap(lat_own), 1)
-    gate_pre = dot(lat_all, gate_mat, 1, 0)
-    up_pre = dot(lat_all, up_mat, 1, 0)
-    active = (jax.nn.silu(gate_pre) * up_pre).astype(bf16)
-    active_peer = swap(active)
-    part = dot(active, out_keep, 1, 0) * gate_all[:, None]
-    part = part + dot(active_peer, out_peer, 1, 0) * gate_peer[:, None]
-    summed = jnp.sum(deal(part, "dp").reshape(groups, rows, half), axis=0)
-    summed, gate_mat, up_mat, out_mat = lax.optimization_barrier(
-        (summed, gate_mat, up_mat, out_mat)
-    )
+    lat_own = spread(mine(latent, 1), "dp")
+    lat_all = joined(lat_own, swap(lat_own), 2)
+    gate_part = jnp.einsum("gtl,lf->gtf", lat_all, gate_mat, preferred_element_type=f32)
+    up_part = jnp.einsum("gtl,lf->gtf", lat_all, up_mat, preferred_element_type=f32)
+    active = (jax.nn.silu(gate_part) * up_part).astype(bf16)
+    active = deal(active, "dp")
+    active, gate_mat, up_mat = lax.optimization_barrier((active, gate_mat, up_mat))
     gate_full = lax.all_gather(gate_mat, "dp")
     up_full = lax.all_gather(up_mat, "dp")
-    out_full = lax.all_gather(out_mat, "dp")
+    part = jnp.einsum("qtf,qfl->tl", active, out_full, preferred_element_type=f32)
+    part = part * gate_own[:, None]
+    summed = mine(part, 1) + swap(other(part, 1))
 
     comb_rows = jnp.sum(deal(summed, plane).reshape(places, chunk, half), axis=0).astype(bf16)
     comb_own = spread(comb_rows, plane).reshape(rows, half)
@@ -157,7 +144,6 @@
     gate_pre = jnp.einsum("tl,qlf->qtf", latent, gate_full, preferred_element_type=f32)
     up_pre = jnp.einsum("tl,qlf->qtf", latent, up_full, preferred_element_type=f32)
     sig = jax.nn.sigmoid(gate_pre)
-    active = (gate_pre * sig * up_pre).astype(bf16)
     routed_grad = (comb_grad.astype(f32) * gate_own[:, None]).astype(bf16)
     act_grad = jnp.einsum("tl,qfl->qtf", routed_grad, out_full, preferred_element_type=f32)
     gate_term = jnp.sum(act_grad * active.astype(f32), axis=(0, 2))

time: 336 us -> 332 us (0.988)
  waiting for transfers between devices: 56 us -> 71.8 us
  starting transfers between devices: 42.9 us -> 33.4 us
  blocking collectives: 162 us -> 153 us
    all_to_all x3, waiting for transfers between devices: 46.5 us -> 56 us  [deal(): return lax.all_to_all(x, axes, 0, 0, tiled=True)]
    all_to_all x8, blocking collectives: 162 us -> 153 us  [deal(): return lax.all_to_all(x, axes, 0, 0, tiled=True)]
    dot_general x9 -> x5, matrix products: 22.9 us -> 15 us  [dot(): lax.dot_general(a, b, (((ca,), (cb,)), ((), ())), preferred_element_type=...]
    all_to_all x3, starting transfers between devices: 19.9 us -> 13.5 us  [deal(): return lax.all_to_all(x, axes, 0, 0, tiled=True)]
    dot_general x1, matrix products: 1.39 us -> 6.82 us  [on_device(): jnp.einsum('qtf,qlf->tl', gate_back, gate_full, preferred_element_type=f32)]
    ppermute x12 -> x10, waiting for transfers between devices: 8.06 us -> 11.7 us  [swap(): return lax.ppermute(x, 'c', [(0, 1), (1, 0)])]
    ppermute x12 -> x10, starting transfers between devices: 20.7 us -> 19.6 us  [swap(): return lax.ppermute(x, 'c', [(0, 1), (1, 0)])]
  transfers between devices with their start and end apart: 21 -> 16, of which waited for: 9 -> 11; matrix products, arithmetic and copies ran while one was open for 14% -> 10% of each run, Pallas kernels for 0% -> 0%
where the time goes in v2:
time: 332 us; the launch traced here: 331 us
  blocking collectives  153 us (46%)
  waiting for transfers between devices  71.8 us (22%)
  matrix products  37 us (11%)
  starting transfers between devices  33.4 us (10%)
  other arithmetic  14.1 us (4%)
  between operations  14.1 us (4%)
  local copies, waits for them, and re-layouts  7.85 us (2%)
    all_to_all x8, blocking collectives, deal(): return lax.all_to_all(x, axes, 0, 0, tiled=True)  153 us
    all_to_all x3, waiting for transfers between devices, deal(): return lax.all_to_all(x, axes, 0, 0, tiled=True)  56 us
    ppermute x10, starting transfers between devices, swap(): return lax.ppermute(x, 'c', [(0, 1), (1, 0)])  19.6 us
    dot_general x5, matrix products, dot(): lax.dot_general(a, b, (((ca,), (cb,)), ((), ())), preferred_element_type=...  15 us
    all_to_all x3, starting transfers between devices, deal(): return lax.all_to_all(x, axes, 0, 0, tiled=True)  13.5 us
    ppermute x10, waiting for transfers between devices, swap(): return lax.ppermute(x, 'c', [(0, 1), (1, 0)])  11.7 us
    dot_general x1, matrix products, on_device(): jnp.einsum('qtf,qlf->tl', gate_back, gate_full, preferred_element_type=f32)  6.82 us
  transfers between devices with their start and end apart: 16, of which 11 were waited for; matrix products, arithmetic and copies ran while one was open for 10% of the time, Pallas kernels for 0%

profile of v2, /device:TPU:1, one launch (start us, length us, event | category | flops | bytes accessed | tf_op | source)
XLA Modules:
  0.0 331.3 jit_solution(6971624338408280426)
XLA Ops:
  7.2 0.7 all-gather.6.cloned.1.call-update
  7.9 1.1 slice_select_fusion.2
  9.1 18.8 %all_to_all.67 = bf16[4,256,512]{2,1,0:T(8,128)(2,1)S(1)} all-to-all(bf16[4,256,512]{2,1,0:T(8,128)(2,1)S(1)} %broadcast_in_dim.35), channel_id=1, replica_groups=mesh['dp'=4,'z'=8,'y'=4,'c'=2] {'dp'}, dimensions={0} | all-to-all | bytes 2097152 | tf_op jit(solution)/shard_map/all_to_all | solution.py:22
  27.9 1.9 collective-permute-start
  29.8 2.3 collective-permute-done
  32.1 1.2 fusion.55
  33.4 2.0 multiply_convert_fusion.1
  35.4 3.5 %all-to-all-start.1 = ((bf16[4,256,336]{1,2,0:T(8,128)(2,1)}), bf16[4,256,336]{1,2,0:T(8,128)(2,1)S(1)}, u32[]{:S(2)}, u32[]{:S(2)}) async-start(bf16[4,256,336]{1,2,0:T(8,128)(2,1)} %multiply_convert_fusion.1), calls=%async_computation.1 | async-start | bytes 1376256 | tf_op jit(solution)/shard_map/all_to_all | solution.py:22
  39.2 18.5 %all-to-all-done.1 = bf16[4,256,336]{1,2,0:T(8,128)(2,1)S(1)} async-done(((bf16[4,256,336]{1,2,0:T(8,128)(2,1)}), bf16[4,256,336]{1,2,0:T(8,128)(2,1)S(1)}, u32[]{:S(2)}, u32[]{:S(2)}) %all-to-all-start.1) | async-done | bytes 688160 | tf_op jit(solution)/shard_map/all_to_all | solution.py:22
  57.7 2.1 all-gather.6.cloned.1.call-done
  59.8 2.8 fusion.37
  62.7 0.8 collective-permute-start.1
  63.5 1.5 collective-permute-done.1
  65.0 0.1 add_bitcast_fusion
  65.2 26.4 %all_to_all.68 = f32[32,8,512]{2,1,0:T(8,128)S(1)} all-to-all(f32[32,8,512]{2,1,0:T(8,128)S(1)} %add_bitcast_fusion), channel_id=1, replica_groups=mesh['dp'=4,'z'=8,'y'=4,'c'=2] {'z','y'}, dimensions={0} | all-to-all | bytes 1048576 | tf_op jit(solution)/shard_map/all_to_all | solution.py:22
  91.7 15.2 %all_to_all.69 = bf16[32,8,512]{2,1,0:T(8,128)(2,1)S(1)} all-to-all(bf16[32,8,512]{2,1,0:T(8,128)(2,1)S(1)} %broadcast_in_dim.37), channel_id=1, replica_groups=mesh['dp'=4,'z'=8,'y'=4,'c'=2] {'z','y'}, dimensions={0} | all-to-all | bytes 524288 | tf_op jit(solution)/shard_map/all_to_all | solution.py:22
  106.9 3.8 %collective-permute-start.2 = (bf16[256,512]{1,0:T(8,128)(2,1)S(1)}, bf16[256,512]{1,0:T(8,128)(2,1)S(1)}, u32[]{:S(2)}, u32[]{:S(2)}) collective-permute-start(bf16[256,512]{1,0:T(8,128)(2,1)S(1)} %bitcast.156), channel_id=1, source_target_pairs={{0,1},{1,0},{2,3},{3,2},{4,5},{5,4},{6,7},{7,6},{8,9},{9,8},{10,11... | collective-permute-start | bytes 786440 | tf_op jit(solution)/shard_map/ppermute | solution.py:18
  110.6 1.2 collective-permute-done.2
  111.8 0.3 fusion.46
  112.2 29.4 %all_to_all.70 = bf16[32,64,256]{2,1,0:T(8,128)(2,1)S(1)} all-to-all(bf16[32,64,256]{2,1,0:T(8,128)(2,1)S(1)} %broadcast_in_dim.38), channel_id=1, replica_groups=mesh['dp'=4,'z'=8,'y'=4,'c'=2] {'z','y'}, dimensions={0} | all-to-all | bytes 2097152 | tf_op jit(solution)/shard_map/all_to_all | solution.py:22
  141.7 2.7 collective-permute-start.3
  144.3 2.3 collective-permute-done.3
  146.6 0.3 fusion.14
  146.9 0.9 multiply_reduce_fusion
  147.8 1.0 fusion.1
  148.8 5.8 %fusion.99 = (f32[256]{0:T(256)S(1)}, f32[256,1024]{1,0:T(8,128)S(1)}) fusion(bf16[4096,256]{1,0:T(8,128)(2,1)S(1)} %fusion.1, bf16[4096,1024]{1,0:T(8,128)(2,1)} %param.21), kind=kOutput, calls=%fused_computation.128 | convolution fusion | flops 2147745536 | bytes 11535360 | tf_op jit(solution)/shard_map/dot_general | solution.py:14
  154.7 0.6 exponential_reduce_fusion
  155.3 0.7 broadcast_in_dim.44
  156.0 6.1 %all-to-all-start.5 = ((f32[64,8,128]{2,1,0:T(8,128)}), f32[64,8,128]{2,1,0:T(8,128)S(1)}, u32[]{:S(2)}, u32[]{:S(2)}) async-start(f32[64,8,128]{2,1,0:T(8,128)} %broadcast_in_dim.44), calls=%async_computation.5 | async-start | bytes 524288 | tf_op jit(solution)/shard_map/all_to_all | solution.py:22
  162.1 0.2 all-gather.10.cloned.1.call-start
  162.4 0.5 all-gather.10.cloned.1.call-update
  162.9 12.4 %all-to-all-done.5 = f32[64,8,128]{2,1,0:T(8,128)S(1)} async-done(((f32[64,8,128]{2,1,0:T(8,128)}), f32[64,8,128]{2,1,0:T(8,128)S(1)}, u32[]{:S(2)}, u32[]{:S(2)}) %all-to-all-start.5) | async-done | bytes 262176 | tf_op jit(solution)/shard_map/all_to_all | solution.py:22
  175.3 0.1 reshape.81
  175.4 0.2 slice_reduce_fusion.1
  175.7 8.4 %convolution_bitcast_fusion = f32[4096,256]{0,1:T(8,128)} fusion(bf16[4096,1024]{1,0:T(8,128)(2,1)} %param.21, f32[256,1024]{1,0:T(8,128)S(1)} %get-tuple-element.45, f32[256]{0:T(256)S(1)} %get-tuple-element.36, f32[256]{0:T(256)S(1)} %get-tuple-element.33, f32[256]{0:T(256)S(1)} %copy-done.8, s32[256]{0:T(256)S(1)} %broadcast_subtract_fusion), kind=kOutput, calls=%fused_computation | convolution fusion | flops 2149318656 | bytes 13635584 | tf_op jit(solution)/shard_map/dot_general | solution.py:14
  184.1 5.6 %copy.57 = f32[4096,256]{1,0:T(8,128)} copy(f32[4096,256]{0,1:T(8,128)} %convolution_bitcast_fusion) | data formatting | bytes 8388608 | tf_op jit(solution)/shard_map/dot_general | solution.py:14
  189.8 2.5 fusion.48
  192.2 0.4 collective-permute-start.4
  192.6 2.3 collective-permute-done.4
  195.0 3.9 %fusion.15 = bf16[32,64,256]{2,1,0:T(8,128)(2,1)} fusion(bf16[32,64,256]{2,1,0:T(8,128)(2,1)S(1)} %collective-permute-done.4, f32[32,2,64,256]{3,2,1,0:T(8,128)} %bitcast.144, pred[]{:T(512)S(6)} %eq.22), kind=kLoop, calls=%fused_computation.21 | loop fusion | flops 2097152 | bytes 6291457 | tf_op jit(solution)/shard_map/convert_element_type | solution.py:127
  198.9 3.9 %all-to-all-start.6 = ((bf16[32,64,256]{2,1,0:T(8,128)(2,1)}), bf16[32,64,256]{2,1,0:T(8,128)(2,1)S(1)}, u32[]{:S(2)}, u32[]{:S(2)}) async-start(bf16[32,64,256]{2,1,0:T(8,128)(2,1)} %fusion.15), calls=%async_computation.6 | async-start | bytes 2097152 | tf_op jit(solution)/shard_map/all_to_all | solution.py:22
  202.8 0.7 all-gather.8.cloned.1.call-update
  203.6 0.5 collective-permute-start.6
  204.1 0.6 multiply_multiply_fusion.1
  204.7 25.2 %all-to-all-done.6 = bf16[32,64,256]{2,1,0:T(8,128)(2,1)S(1)} async-done(((bf16[32,64,256]{2,1,0:T(8,128)(2,1)}), bf16[32,64,256]{2,1,0:T(8,128)(2,1)S(1)}, u32[]{:S(2)}, u32[]{:S(2)}) %all-to-all-start.6) | async-done | bytes 1048608 | tf_op jit(solution)/shard_map/all_to_all | solution.py:22
  229.9 0.2 convert_reduce_fusion
  230.1 2.3 collective-permute-start.5
  232.4 0.2 fusion.87
  232.7 0.6 collective-permute-done.5
  233.3 0.2 fusion.45
  233.6 16.4 %all_to_all.71 = bf16[32,8,512]{2,1,0:T(8,128)(2,1)S(1)} all-to-all(bf16[32,8,512]{2,1,0:T(8,128)(2,1)S(1)} %fusion.45), channel_id=1, replica_groups=mesh['dp'=4,'z'=8,'y'=4,'c'=2] {'z','y'}, dimensions={0} | all-to-all | bytes 524288 | tf_op jit(solution)/shard_map/all_to_all | solution.py:22
  250.0 15.0 %all_to_all.72 = bf16[32,8,512]{2,1,0:T(8,128)(2,1)S(1)} all-to-all(bf16[32,8,512]{2,1,0:T(8,128)(2,1)S(1)} %broadcast_in_dim.45), channel_id=1, replica_groups=mesh['dp'=4,'z'=8,'y'=4,'c'=2] {'z','y'}, dimensions={0} | all-to-all | bytes 524288 | tf_op jit(solution)/shard_map/all_to_all | solution.py:22
  265.0 3.3 collective-permute-start.7
  268.3 2.9 fusion.22
  271.2 2.1 multiply_reduce_fusion.1
  273.5 4.3 %fusion.31 = f32[256,1024]{1,0:T(8,128)} fusion(bf16[42,4,8,1024]{3,2,1,0:T(8,128)(2,1)} %bitcast.164, f32[4,256,336]{1,2,0:T(8,128)} %get-tuple-element.47, f32[4,256,336]{1,2,0:T(8,128)S(1)} %fusion.22), kind=kOutput, calls=%fused_computation.36 | convolution fusion | flops 706707456 | bytes 6553600 | tf_op jit(solution)/shard_map/qtf,qlf->tl/dot_general | solution.py:154
  277.7 6.8 %fusion.41 = f32[256,1024]{1,0:T(8,128)S(1)} fusion(f32[256,1024]{1,0:T(8,128)} %fusion.31, bf16[42,4,8,1024]{3,2,1,0:T(8,128)(2,1)} %bitcast.163, f32[4,256,336]{1,2,0:T(8,128)} %copy-done.11, f32[4,256,336]{1,2,0:T(8,128)} %get-tuple-element.47, bf16[42,4,8,1024]{3,2,1,0:T(8,128)(2,1)} %bitcast.165, bf16[256,1024]{1,0:T(8,128)(2,1)S(1)} %copy-done.2), kind=kOutput, calls=%fused_computation.41 | convolution fusion | flops 1412988928 | bytes 10878976 | tf_op jit(solution)/shard_map/qtf,qlf->tl/dot_general | solution.py:153
  284.9 1.5 collective-permute-done.8
  286.5 16.3 %all_to_all.73 = bf16[32,8,640]{2,1,0:T(8,128)(2,1)S(1)} all-to-all(bf16[32,8,640]{2,1,0:T(8,128)(2,1)S(1)} %fusion.83), channel_id=1, replica_groups=mesh['dp'=4,'z'=8,'y'=4,'c'=2] {'z','y'}, dimensions={0} | all-to-all | bytes 655360 | tf_op jit(solution)/shard_map/all_to_all | solution.py:22
  302.9 15.6 %all_to_all.74 = bf16[32,8,640]{2,1,0:T(8,128)(2,1)S(1)} all-to-all(bf16[32,8,640]{2,1,0:T(8,128)(2,1)S(1)} %broadcast_in_dim.52), channel_id=1, replica_groups=mesh['dp'=4,'z'=8,'y'=4,'c'=2] {'z','y'}, dimensions={0} | all-to-all | bytes 655360 | tf_op jit(solution)/shard_map/all_to_all | solution.py:22
  318.5 3.8 %collective-permute-start.9 = (bf16[256,512]{1,0:T(8,128)(2,1)S(1)}, bf16[256,512]{1,0:T(8,128)(2,1)S(1)}, u32[]{:S(2)}, u32[]{:S(2)}) collective-permute-start(bf16[256,512]{1,0:T(8,128)(2,1)S(1)} %slice.43), channel_id=1, source_target_pairs={{0,1},{1,0},{2,3},{3,2},{4,5},{5,4},{6,7},{7,6},{8,9},{9,8},{10,11... | collective-permute-start | bytes 786440 | tf_op jit(solution)/shard_map/ppermute | solution.py:18
  322.3 0.7 bitcast_subtract_fusion
  323.0 0.7 copy.62
  323.7 1.1 fusion.72
  (63 shorter events, 1.8 us)
Async XLA Ops:
  7.2 52.6 %all-gather.6.cloned.1.call-start = ((), (), s32[]{:S(2)}) async-start(), calls=%async_computation.11 | async-start | bytes 3440640 | tf_op jit(solution)/shard_map/all_gather | solution.py:74
  7.9 24.2 %copy-start = (bf16[1,1024,336]{1,2,0:T(8,128)(2,1)S(1)}, bf16[1,1024,336]{1,2,0:T(8,128)(2,1)}, u32[]{:S(2)}) copy-start(bf16[1,1024,336]{1,2,0:T(8,128)(2,1)} %param.16) | copy-start | bytes 2064388
  27.9 5.5 %copy-start.1 = (bf16[1,1024,336]{1,2,0:T(8,128)(2,1)S(1)}, bf16[1,1024,336]{1,2,0:T(8,128)(2,1)}, u32[]{:S(2)}) copy-start(bf16[1,1024,336]{1,2,0:T(8,128)(2,1)} %param.17) | copy-start | bytes 2064388
  27.9 4.2 %collective-permute-start = (bf16[4,256,512]{2,1,0:T(8,128)(2,1)S(1)}, bf16[4,256,512]{2,1,0:T(8,128)(2,1)S(1)}, u32[]{:S(2)}, u32[]{:S(2)}) collective-permute-start(bf16[4,256,512]{2,1,0:T(8,128)(2,1)S(1)} %all_to_all.67), channel_id=1, source_target_pairs={{0,1},{1,0},{2,3},{3,2},{4,5},{5,4},{6,7},{7,6},{8,9},{9,8},{10,11... | collective-permute-start | bytes 3145736 | tf_op jit(solution)/shard_map/ppermute | solution.py:18
  33.3 5.5 %copy-start.4 = (f32[256,22]{0,1:T(8,128)S(1)}, f32[256,22]{0,1:T(8,128)}, u32[]{:S(2)}) copy-start(f32[256,22]{0,1:T(8,128)} %param.14) | copy-start | bytes 67588
  33.4 5.6 %copy-start.5 = (s32[256,22]{0,1:T(8,128)S(1)}, s32[256,22]{0,1:T(8,128)}, u32[]{:S(2)}) copy-start(s32[256,22]{0,1:T(8,128)} %param.15) | copy-start | bytes 67588
  35.4 22.3 %all-to-all-start.1 = ((bf16[4,256,336]{1,2,0:T(8,128)(2,1)}), bf16[4,256,336]{1,2,0:T(8,128)(2,1)S(1)}, u32[]{:S(2)}, u32[]{:S(2)}) async-start(bf16[4,256,336]{1,2,0:T(8,128)(2,1)} %multiply_convert_fusion.1), calls=%async_computation.1 | async-start | bytes 1376256 | tf_op jit(solution)/shard_map/all_to_all | solution.py:22
  62.7 49.1 %copy-start.3 = (bf16[1024,64]{0,1:T(8,128)(2,1)S(1)}, bf16[1024,64]{0,1:T(8,128)(2,1)}, u32[]{:S(2)}) copy-start(bf16[1024,64]{0,1:T(8,128)(2,1)} %param.19) | copy-start | bytes 393220
  62.7 49.1 %copy-start.10 = (bf16[256,64]{0,1:T(8,128)(2,1)S(1)}, bf16[256,64]{0,1:T(8,128)(2,1)}, u32[]{:S(2)}) copy-start(bf16[256,64]{0,1:T(8,128)(2,1)} %param.13) | copy-start | bytes 98308
  62.7 2.3 collective-permute-start.1
  106.9 4.9 %collective-permute-start.2 = (bf16[256,512]{1,0:T(8,128)(2,1)S(1)}, bf16[256,512]{1,0:T(8,128)(2,1)S(1)}, u32[]{:S(2)}, u32[]{:S(2)}) collective-permute-start(bf16[256,512]{1,0:T(8,128)(2,1)S(1)} %bitcast.156), channel_id=1, source_target_pairs={{0,1},{1,0},{2,3},{3,2},{4,5},{5,4},{6,7},{7,6},{8,9},{9,8},{10,11... | collective-permute-start | bytes 786440 | tf_op jit(solution)/shard_map/ppermute | solution.py:18
  112.1 32.2 %copy-start.6 = (bf16[4096]{0:T(1024)(128)(2,1)S(1)}, bf16[4096]{0:T(1024)(128)(2,1)}, u32[]{:S(2)}) copy-start(bf16[4096]{0:T(1024)(128)(2,1)} %param.20) | copy-start | bytes 24580
  112.1 32.2 %copy-start.7 = (s32[256]{0:T(256)S(1)}, s32[256]{0:T(256)}, u32[]{:S(2)}) copy-start(s32[256]{0:T(256)} %param.22) | copy-start | bytes 3076
  141.7 5.0 %collective-permute-start.3 = (bf16[32,64,256]{2,1,0:T(8,128)(2,1)S(1)}, bf16[32,64,256]{2,1,0:T(8,128)(2,1)S(1)}, u32[]{:S(2)}, u32[]{:S(2)}) collective-permute-start(bf16[32,64,256]{2,1,0:T(8,128)(2,1)S(1)} %all_to_all.70), channel_id=1, source_target_pairs={{0,1},{1,0},{2,3},{3,2},{4,5},{5,4},{6,7},{7,6},{8,9},{9,8},{10,11... | collective-permute-start | bytes 3145736 | tf_op jit(solution)/shard_map/ppermute | solution.py:18
  154.7 21.0 %copy-start.8 = (f32[256]{0:T(256)S(1)}, f32[256]{0:T(256)}, u32[]{:S(2)}) copy-start(f32[256]{0:T(256)} %param.23) | copy-start | bytes 3076
  156.0 19.3 %all-to-all-start.5 = ((f32[64,8,128]{2,1,0:T(8,128)}), f32[64,8,128]{2,1,0:T(8,128)S(1)}, u32[]{:S(2)}, u32[]{:S(2)}) async-start(f32[64,8,128]{2,1,0:T(8,128)} %broadcast_in_dim.44), calls=%async_computation.5 | async-start | bytes 524288 | tf_op jit(solution)/shard_map/all_to_all | solution.py:22
  162.1 106.1 %all-gather.10.cloned.1.call-start = ((), (), s32[]{:S(2)}) async-start(), calls=%async_computation.13 | async-start | bytes 3440640 | tf_op jit(solution)/shard_map/all_gather | solution.py:83
  192.2 2.7 collective-permute-start.4
  198.9 31.0 %all-to-all-start.6 = ((bf16[32,64,256]{2,1,0:T(8,128)(2,1)}), bf16[32,64,256]{2,1,0:T(8,128)(2,1)S(1)}, u32[]{:S(2)}, u32[]{:S(2)}) async-start(bf16[32,64,256]{2,1,0:T(8,128)(2,1)} %fusion.15), calls=%async_computation.6 | async-start | bytes 2097152 | tf_op jit(solution)/shard_map/all_to_all | solution.py:22
  202.8 70.6 %all-gather.8.cloned.1.call-start = ((), (), s32[]{:S(2)}) async-start(), calls=%async_computation.12 | async-start | bytes 3440640 | tf_op jit(solution)/shard_map/all_gather | solution.py:84
  203.6 29.1 %collective-permute-start.6 = (bf16[512,64]{0,1:T(8,128)(2,1)S(1)}, bf16[512,64]{0,1:T(8,128)(2,1)S(1)}, u32[]{:S(2)}, u32[]{:S(2)}) collective-permute-start(bf16[512,64]{0,1:T(8,128)(2,1)S(1)} %broadcast_select_fusion.1), channel_id=1, source_target_pairs={{0,1},{1,0},{2,3},{3,2},{4,5},{5,4},{6,7},{7,6},{8,9},{9,8},{10,11... | collective-permute-start | bytes 196616 | tf_op jit(solution)/shard_map/ppermute | solution.py:18
  204.7 63.6 %copy-start.2 = (bf16[256,1024]{1,0:T(8,128)(2,1)S(1)}, bf16[256,1024]{1,0:T(8,128)(2,1)}, u32[]{:S(2)}) copy-start(bf16[256,1024]{1,0:T(8,128)(2,1)} %param.12) | copy-start | bytes 1572868
  230.1 3.2 collective-permute-start.5
  265.0 6.2 %collective-permute-start.7 = (bf16[256,512]{1,0:T(8,128)(2,1)S(1)}, bf16[256,512]{1,0:T(8,128)(2,1)S(1)}, u32[]{:S(2)}, u32[]{:S(2)}) collective-permute-start(bf16[256,512]{1,0:T(8,128)(2,1)S(1)} %bitcast.154), channel_id=1, source_target_pairs={{0,1},{1,0},{2,3},{3,2},{4,5},{5,4},{6,7},{7,6},{8,9},{9,8},{10,11... | collective-permute-start | bytes 786440 | tf_op jit(solution)/shard_map/ppermute | solution.py:18
  268.3 2.9 copy-start.9
  271.1 2.3 copy-start.11
  284.6 1.7 collective-permute-start.8
  318.5 5.2 %collective-permute-start.9 = (bf16[256,512]{1,0:T(8,128)(2,1)S(1)}, bf16[256,512]{1,0:T(8,128)(2,1)S(1)}, u32[]{:S(2)}, u32[]{:S(2)}) collective-permute-start(bf16[256,512]{1,0:T(8,128)(2,1)S(1)} %slice.43), channel_id=1, source_target_pairs={{0,1},{1,0},{2,3},{3,2},{4,5},{5,4},{6,7},{7,6},{8,9},{9,8},{10,11... | collective-permute-start | bytes 786440 | tf_op jit(solution)/shard_map/ppermute | solution.py:18
Sparse Core Ops, SparseCore 0:
  9.8 49.9 all-gather.5
  164.8 37.9 all-gather.9
  205.4 38.1 all-gather.7

commit v3 on v2

v3 whole, which is shorter than its diff:
```python
import jax
import jax.numpy as jnp
from jax import lax
from jax.experimental import pallas as pl
from jax.experimental.pallas import tpu as pltpu
from jax.sharding import Mesh, PartitionSpec as P

norm_epsilon = 1e-05
plane = ("z", "y")
slab = ("z", "y", "c")
bf16 = jnp.bfloat16
f32 = jnp.float32


def dot(a, b, ca, cb):
    return lax.dot_general(a, b, (((ca,), (cb,)), ((), ())), preferred_element_type=f32)


def swap(x):
    return lax.ppermute(x, "c", [(0, 1), (1, 0)])


def deal(x, axes):
    return lax.all_to_all(x, axes, 0, 0, tiled=True)


def spread(x, axes):
    count = lax.axis_size(axes)
    return deal(jnp.broadcast_to(x[None], (count,) + x.shape), axes)


def compiler_params():
    return pltpu.CompilerParams(vmem_limit_bytes=44 << 20)


def head_kernel(core, own, peer, gain, words, target, logits, stats, block, scale):
    step = pl.program_id(0)
    last = pl.num_programs(0) - 1
    per = gain.shape[2]
    cols = gain.shape[1]
    half = own.shape[0] // per

    @pl.when(step == 0)
    def _():
        def add(i, total):
            a = own[i].astype(f32)
            b = peer[i].astype(f32)
            return total + a * a + b * b

        total = lax.fori_loop(0, own.shape[0], add, jnp.zeros(own.shape[1:], f32), unroll=4)
        mean = jnp.sum(total, axis=0, keepdims=True) / (2 * own.shape[0] * cols) + norm_epsilon
        guess = lax.rsqrt(mean)
        scale[...] = guess * (1.5 - 0.5 * mean * guess * guess)
        logits[...] = jnp.zeros_like(logits)

    def fill(source, base):
        for j in range(per):
            h = source[base + j].astype(f32) * scale[...]
            h = h * gain[0, :, j : j + 1]
            block[j * cols : (j + 1) * cols, :] = h.astype(bf16)

    @pl.when(step < half)
    def _():
        fill(own, step * per)

    @pl.when(step >= half)
    def _():
        fill(peer, (step - half) * per)

    rhs = words[...].reshape(per * cols, -1)
    logits[...] += lax.dot_general(
        block[...], rhs, (((0,), (0,)), ((), ())), preferred_element_type=f32
    )

    @pl.when(step == last)
    def _():
        values = logits[...]
        peak = jnp.max(values, axis=1, keepdims=True)
        below = values - peak
        weight = jnp.exp(below)
        total = jnp.sum(weight, axis=1, keepdims=True)
        lean = jnp.sum(weight * below, axis=1, keepdims=True)
        at = lax.broadcasted_iota(jnp.int32, values.shape, 1) == target[...]
        hit = jnp.sum(jnp.where(at, values, 0.0), axis=1, keepdims=True)
        lane = lax.broadcasted_iota(jnp.int32, (values.shape[0], 128), 1)
        packed = jnp.where(lane == 0, peak, jnp.where(lane == 1, total, 0.0))
        packed = jnp.where(lane == 2, lean, jnp.where(lane == 3, hit, packed))
        row = lax.broadcasted_iota(jnp.int32, stats.shape, 0)
        stats[...] = jnp.where(row == 4, scale[...], packed.T[: stats.shape[0]])


def loss_kernel(core, stats, logits, target, cot, words, grad, send, rows):
    @pl.when(pl.program_id(0) == 0)
    def _():
        peaks = stats[:, 0, :]
        peak = jnp.max(peaks, axis=0, keepdims=True)
        gap = peaks - peak
        share = jnp.exp(gap)
        totals = stats[:, 1, :]
        total = jnp.sum(share * totals, axis=0, keepdims=True)
        lean = jnp.sum(share * (stats[:, 2, :] + gap * totals), axis=0, keepdims=True)
        hit = jnp.sum(stats[:, 3, :], axis=0, keepdims=True)
        inverse = 1.0 / total
        inner = cot[...] * (lean * inverse - (hit - peak))
        row = lax.broadcasted_iota(jnp.int32, (128, peak.shape[1]), 0)
        packed = jnp.where(row == 0, peak, jnp.where(row == 1, inverse, 0.0))
        packed = jnp.where(row == 2, cot[...], packed)
        col = packed.T
        top = lax.broadcasted_iota(jnp.int32, rows.shape, 0)
        loss = peak + jnp.log(total) - hit
        rows[...] = jnp.where(top == 0, loss, jnp.where(top == 1, inner, 0.0))
        probs = jnp.exp(logits[...] - col[:, 0:1]) * col[:, 1:2]
        at = lax.broadcasted_iota(jnp.int32, probs.shape, 1) == target[...]
        grad[...] = (col[:, 2:3] * (probs - jnp.where(at, 1.0, 0.0))).astype(bf16)

    lhs = words[...].reshape(-1, words.shape[3])
    out = lax.dot_general(lhs, grad[...], (((1,), (1,)), ((), ())), preferred_element_type=f32)
    send[...] = out.reshape(send.shape).astype(send.dtype)


def keep_kernel(core, grad, words, keep):
    lhs = words[...].reshape(-1, words.shape[3])
    out = lax.dot_general(lhs, grad[...], (((1,), (1,)), ((), ())), preferred_element_type=f32)
    keep[...] = out.reshape(keep.shape)


def whole(shape):
    return pl.BlockSpec(shape, lambda i, core: (0,) * len(shape))


def call_head(core, own, peer, gain, words, target):
    rows, count = own.shape[2], words.shape[3]
    steps, cols, per = gain.shape
    half = steps // 2

    def part(i, core):
        return (i % half, jnp.where(i < half, core[0], 1 - core[0]), 0, 0)

    return pl.pallas_call(
        head_kernel,
        grid_spec=pltpu.PrefetchScalarGridSpec(
            num_scalar_prefetch=1,
            grid=(steps,),
            in_specs=[
                whole(own.shape),
                whole(peer.shape),
                pl.BlockSpec((1, cols, per), lambda i, core: (i, 0, 0)),
                pl.BlockSpec((per, 1, cols, count), part),
                whole(target.shape),
            ],
            out_specs=[whole((rows, count)), whole((8, rows))],
            scratch_shapes=[
                pltpu.VMEM((per * cols, rows), bf16),
                pltpu.VMEM((1, rows), f32),
            ],
        ),
        out_shape=[
            jax.ShapeDtypeStruct((rows, count), f32),
            jax.ShapeDtypeStruct((8, rows), f32),
        ],
        compiler_params=compiler_params(),
        name="head",
    )(core, own, peer, gain, words, target)


def call_loss(core, stats, logits, target, cot, words, per):
    places, _, cols, count = words.shape
    rows = logits.shape[0]
    return pl.pallas_call(
        loss_kernel,
        grid_spec=pltpu.PrefetchScalarGridSpec(
            num_scalar_prefetch=1,
            grid=(places // per,),
            in_specs=[
                whole(stats.shape),
                whole(logits.shape),
                whole(target.shape),
                whole(cot.shape),
                pl.BlockSpec((per, 1, cols, count), lambda i, core: (i, 1 - core[0], 0, 0)),
            ],
            out_specs=[
                whole((rows, count)),
                pl.BlockSpec((per, cols, rows), lambda i, core: (i, 0, 0)),
                whole((8, rows)),
            ],
        ),
        out_shape=[
            jax.ShapeDtypeStruct((rows, count), bf16),
            jax.ShapeDtypeStruct((places, cols, rows), bf16),
            jax.ShapeDtypeStruct((8, rows), f32),
        ],
        compiler_params=compiler_params(),
        name="loss",
    )(core, stats, logits, target, cot, words)


def call_keep(core, grad, words, per):
    places, _, cols, count = words.shape
    rows = grad.shape[0]
    return pl.pallas_call(
        keep_kernel,
        grid_spec=pltpu.PrefetchScalarGridSpec(
            num_scalar_prefetch=1,
            grid=(places // per,),
            in_specs=[
                whole(grad.shape),
                pl.BlockSpec((per, 1, cols, count), lambda i, core: (i, core[0], 0, 0)),
            ],
            out_specs=pl.BlockSpec((per, cols, rows), lambda i, core: (i, 0, 0)),
        ),
        out_shape=jax.ShapeDtypeStruct((places, cols, rows), f32),
        compiler_params=compiler_params(),
        cost_estimate=pl.CostEstimate(
            flops=places * cols * rows * count * 2,
            bytes_accessed=places * cols * count * 2,
            transcendentals=0,
        ),
        name="keep",
    )(core, grad, words)


def expert_kernel(
    core, own, peer, latent, active, marks, gate_w, up_w, out_w, keep, send, routed, block, term
):
    step = pl.program_id(0)
    half = own.shape[1]
    gate = jnp.sum(marks[...], axis=1, keepdims=True)

    @pl.when(step == 0)
    def _():
        a = (own[...].astype(f32) * gate).astype(bf16)
        b = (peer[...].astype(f32) * gate).astype(bf16)

        @pl.when(core[0] == 0)
        def _():
            routed[:, :half] = a
            routed[:, half:] = b

        @pl.when(core[0] != 0)
        def _():
            routed[:, :half] = b
            routed[:, half:] = a

        block[...] = jnp.zeros_like(block)
        term[...] = jnp.zeros_like(term)

    def over_last(x, w):
        return lax.dot_general(x, w, (((1,), (1,)), ((), ())), preferred_element_type=f32)

    gate_pre = over_last(latent[...], gate_w[0])
    up_pre = over_last(latent[...], up_w[0])
    act_grad = over_last(routed[...], out_w[0])
    sig = 1.0 / (1.0 + jnp.exp(-gate_pre))
    term[...] += jnp.sum(act_grad * active[0].astype(f32), axis=1, keepdims=True)
    gate_back = (act_grad * up_pre * sig * (1.0 + gate_pre * (1.0 - sig))).astype(bf16)
    up_back = (act_grad * gate_pre * sig).astype(bf16)
    block[...] += jnp.dot(gate_back, gate_w[0], preferred_element_type=f32) + jnp.dot(
        up_back, up_w[0], preferred_element_type=f32
    )

    @pl.when(step == pl.num_programs(0) - 1)
    def _():
        share = term[...] / jnp.where(gate > 0, gate, 1.0)
        gate_grad = jnp.where(marks[...] > 0, share, 0.0)
        keep[:, half:] = gate_grad
        send[:, half:] = gate_grad.astype(bf16)

        @pl.when(core[0] == 0)
        def _():
            keep[:, :half] = block[:, :half]
            send[:, :half] = block[:, half:].astype(bf16)

        @pl.when(core[0] != 0)
        def _():
            keep[:, :half] = block[:, half:]
            send[:, :half] = block[:, :half].astype(bf16)


def call_expert(core, own, peer, latent, active, marks, gate_w, up_w, out_w):
    rows, width = latent.shape
    quarters, units, _ = gate_w.shape
    lanes = own.shape[1] + marks.shape[1]

    def part(shape):
        return pl.BlockSpec((1,) + shape, lambda i, core: (i, 0, 0))

    return pl.pallas_call(
        expert_kernel,
        grid_spec=pltpu.PrefetchScalarGridSpec(
            num_scalar_prefetch=1,
            grid=(quarters,),
            in_specs=[
                whole(own.shape),
                whole(peer.shape),
                whole(latent.shape),
                part((rows, units)),
                whole(marks.shape),
                part((units, width)),
                part((units, width)),
                part((units, width)),
            ],
            out_specs=[whole((rows, lanes)), whole((rows, lanes))],
            scratch_shapes=[
                pltpu.VMEM((rows, width), bf16),
                pltpu.VMEM((rows, width), f32),
                pltpu.VMEM((rows, 1), f32),
            ],
        ),
        out_shape=[
            jax.ShapeDtypeStruct((rows, lanes), f32),
            jax.ShapeDtypeStruct((rows, lanes), bf16),
        ],
        compiler_params=compiler_params(),
        name="expert",
    )(core, own, peer, latent, active, marks, gate_w, up_w, out_w)


def on_device(
    latent,
    residual,
    gates,
    route_ids,
    w_gate,
    w_up,
    w_out,
    w_lift,
    norm_gain,
    w_vocab,
    targets,
    loss_cot,
):
    core = lax.axis_index("c")
    own_index = lax.axis_index(slab)
    places = lax.axis_size(plane)
    rows, width = latent.shape
    half = width // 2
    cols = residual.shape[1]
    model = w_vocab.shape[0]
    words = w_vocab.shape[1]
    chunk = rows // places
    first = core == 0

    def mine(x, axis):
        a, b = jnp.split(x, 2, axis)
        return jnp.where(first, a, b)

    def other(x, axis):
        a, b = jnp.split(x, 2, axis)
        return jnp.where(first, b, a)

    def joined(own, peer, axis):
        return jnp.where(
            first,
            jnp.concatenate([own, peer], axis),
            jnp.concatenate([peer, own], axis),
        )

    gate_mat, up_mat, out_mat = w_gate[0], w_up[0], w_out[0]
    chosen = route_ids == own_index
    gate_own = jnp.sum(jnp.where(chosen, gates, 0.0), axis=1)

    out_full = lax.all_gather(out_mat, "dp")

    lat_own = spread(mine(latent, 1), "dp")
    lat_all = joined(lat_own, swap(lat_own), 2)
    gate_part = jnp.einsum("gtl,lf->gtf", lat_all, gate_mat, preferred_element_type=f32)
    up_part = jnp.einsum("gtl,lf->gtf", lat_all, up_mat, preferred_element_type=f32)
    active = (jax.nn.silu(gate_part) * up_part).astype(bf16)
    active = deal(active, "dp")
    active, gate_mat, up_mat = lax.optimization_barrier((active, gate_mat, up_mat))
    gate_full = lax.all_gather(gate_mat.T, "dp")
    up_full = lax.all_gather(up_mat.T, "dp")
    part = jnp.einsum("qtf,qfl->tl", active, out_full, preferred_element_type=f32)
    part = part * gate_own[:, None]
    summed = mine(part, 1) + swap(other(part, 1))

    comb_rows = jnp.sum(deal(summed, plane).reshape(places, chunk, half), axis=0).astype(bf16)
    comb_own = spread(comb_rows, plane).reshape(rows, half)
    combined = joined(comb_own, swap(comb_own), 1)
    lifted_t = dot(w_lift, combined, 0, 1)
    hidden_t = (residual.T.astype(f32) + lifted_t).astype(bf16)
    hid_own = spread(hidden_t, plane)
    hid_peer = swap(hid_own)
    per = 8
    steps = places // per
    core_id = core.astype(jnp.int32)[None]
    gain_float = norm_gain.astype(f32)
    gain_parts = gain_float.reshape(steps, per, 2, cols)
    gain_parts = jnp.concatenate(
        [
            jnp.where(first, gain_parts[:, :, 0], gain_parts[:, :, 1]),
            jnp.where(first, gain_parts[:, :, 1], gain_parts[:, :, 0]),
        ]
    ).transpose(0, 2, 1)
    target = (targets - own_index * words)[:, None]
    vocab = w_vocab.reshape(places, 2, cols, words)
    logits, stats = call_head(core_id, hid_own, hid_peer, gain_parts, vocab, target)
    scale_inv = stats[4]
    stats_all = spread(stats, slab)
    grad, send_t, row_out = call_loss(
        core_id, stats_all, logits, target, loss_cot[None], vocab, per
    )
    row_loss = row_out[0]
    inner = row_out[1]
    keep_t = call_keep(core_id, grad, vocab, per)
    keep_t = (keep_t + swap(send_t).astype(f32)).astype(bf16)
    normed_grad = jnp.sum(deal(keep_t, plane).astype(f32), axis=0)
    gain_own = lax.dynamic_slice_in_dim(gain_float, own_index * cols, cols, 0)
    d_res_t = (
        scale_inv[None, :] * (normed_grad * gain_own[:, None])
        - hidden_t.astype(f32) * (scale_inv**2 * (inner / model))[None, :]
    )
    d_residual = d_res_t.T
    d_res_bf = d_res_t.astype(bf16)
    lift_keep = mine(w_lift, 0)
    lift_peer = swap(other(w_lift, 0))
    cg_part = dot(d_res_bf, lift_keep, 0, 1) + dot(swap(d_res_bf), lift_peer, 0, 1)
    cg_rows = deal(cg_part.astype(bf16), plane).astype(f32)
    cg_rows = jnp.sum(cg_rows.reshape(places, chunk, half), axis=0).astype(bf16)
    cg_own = spread(cg_rows, plane).reshape(rows, half)
    marks = jnp.where(chosen, gates, 0.0)
    marks = jnp.pad(marks, ((0, 0), (0, 128 - marks.shape[1])))
    keep, send = call_expert(
        core_id, cg_own, swap(cg_own), latent, active, marks, gate_full, up_full, out_full
    )
    keep = (keep + swap(send).astype(f32)).astype(bf16)
    tail = jnp.sum(deal(keep, plane).astype(f32).reshape(places, chunk, -1), axis=0).astype(bf16)
    tail = spread(tail, plane).reshape(rows, -1)
    d_latent = joined(tail[:, :half], swap(tail[:, :half]), 1).astype(f32)
    d_gates = tail[:, half : half + gates.shape[1]].astype(f32)
    return (row_loss, d_residual, d_latent, d_gates)


def solution(mesh):
    fine = Mesh(mesh.devices.reshape(mesh.devices.shape[0], 8, 4, 2), ("dp", "z", "y", "c"))
    in_specs = (
        P("dp", None),
        P("dp", slab),
        P("dp", None),
        P("dp", None),
        P(slab, None, "dp"),
        P(slab, None, "dp"),
        P(slab, "dp", None),
        P(None, slab),
        P(),
        P(None, slab),
        P("dp"),
        P("dp"),
    )
    out_specs = (P("dp"), P("dp", slab), P("dp", None), P("dp", None))
    return jax.shard_map(
        on_device, mesh=fine, in_specs=in_specs, out_specs=out_specs, check_vma=False
    )
```

time: 332 us -> 325 us (0.979)
  matrix products: 37 us -> 6.77 us
  Pallas kernels: 0 us -> 26.6 us
  waiting for transfers between devices: 71.8 us -> 83.9 us
  other arithmetic: 14.1 us -> 6.96 us
  blocking collectives: 153 us -> 147 us
    pallas_call x0 -> x4, Pallas kernels: none -> 26.6 us  [the longest x1 9.48 us: call_head(): pl.pallas_call(head_kernel, grid_spec=pltpu.PrefetchScalarGridSpec(num_sc...]
    dot_general x4 -> x0, matrix products: 16 us -> none  [the longest x1 6.82 us: on_device(): jnp.einsum('qtf,qlf->tl', gate_back, gate_full, preferred_element_type=f32)]
    all_to_all x3, waiting for transfers between devices: 56 us -> 71 us  [deal(): return lax.all_to_all(x, axes, 0, 0, tiled=True)]
    dot_general x5 -> x3, matrix products: 15 us -> 0.77 us  [dot(): lax.dot_general(a, b, (((ca,), (cb,)), ((), ())), preferred_element_type=...]
    all_to_all x8, blocking collectives: 153 us -> 147 us  [deal(): return lax.all_to_all(x, axes, 0, 0, tiled=True)]
    dot_general x1 -> x0, local copies, waits for them, and re-layouts: 5.63 us -> none  [dot(): lax.dot_general(a, b, (((ca,), (cb,)), ((), ())), preferred_element_type=...]
    convert_element_type x4 -> x0, other arithmetic: 3.76 us -> none  [the longest x1 2.47 us: on_device(): send_t = jnp.where(first, grad_t[:, 1], grad_t[:, 0]).astype(bf16)]
    unnamed x27, local copies, waits for them, and re-layouts: 0.98 us -> 4.53 us
  transfers between devices with their start and end apart: 16 -> 16, of which waited for: 11 -> 11; matrix products, arithmetic and copies ran while one was open for 10% -> 3% of each run, Pallas kernels for 0% -> 6%
where the time goes in v3:
time: 325 us; the launch traced here: 324 us
  blocking collectives  147 us (45%)
  waiting for transfers between devices  83.9 us (26%)
  starting transfers between devices  31.3 us (10%)
  Pallas kernels  26.6 us (8%)
  between operations  14.1 us (4%)
  other arithmetic  6.96 us (2%)
  matrix products  6.77 us (2%)
  local copies, waits for them, and re-layouts  6.61 us (2%)
    all_to_all x8, blocking collectives, deal(): return lax.all_to_all(x, axes, 0, 0, tiled=True)  147 us
    all_to_all x3, waiting for transfers between devices, deal(): return lax.all_to_all(x, axes, 0, 0, tiled=True)  71 us
    ppermute x10, starting transfers between devices, swap(): return lax.ppermute(x, 'c', [(0, 1), (1, 0)])  18.9 us
    all_to_all x3, starting transfers between devices, deal(): return lax.all_to_all(x, axes, 0, 0, tiled=True)  12.3 us
    pallas_call x1, Pallas kernels, call_head(): pl.pallas_call(head_kernel, grid_spec=pltpu.PrefetchScalarGridSpec(num_sc...  9.48 us
    ppermute x10, waiting for transfers between devices, swap(): return lax.ppermute(x, 'c', [(0, 1), (1, 0)])  9.44 us
    pallas_call x1, Pallas kernels, call_expert(): pl.pallas_call(expert_kernel, grid_spec=pltpu.PrefetchScalarGridSpec(num_...  8.51 us
  transfers between devices with their start and end apart: 16, of which 11 were waited for; matrix products, arithmetic and copies ran while one was open for 3% of the time, Pallas kernels for 6%

profile of v3, /device:TPU:1, one launch (start us, length us, event | category | flops | bytes accessed | tf_op | source)
XLA Modules:
  0.0 323.7 jit_solution(11246659932573210960)
XLA Ops:
  7.2 0.7 all-gather.6.cloned.1.call-update
  7.9 1.1 slice_select_fusion.1
  9.1 18.8 %all_to_all.67 = bf16[4,256,512]{2,1,0:T(8,128)(2,1)S(1)} all-to-all(bf16[4,256,512]{2,1,0:T(8,128)(2,1)S(1)} %broadcast_in_dim.24), channel_id=1, replica_groups=mesh['dp'=4,'z'=8,'y'=4,'c'=2] {'dp'}, dimensions={0} | all-to-all | bytes 2097152 | tf_op jit(solution)/shard_map/all_to_all | solution.py:24
  27.9 1.9 collective-permute-start
  29.8 2.3 collective-permute-done
  32.1 1.2 fusion.8
  33.4 2.0 multiply_convert_fusion
  35.4 3.5 %all-to-all-start.1 = ((bf16[4,256,336]{1,2,0:T(8,128)(2,1)}), bf16[4,256,336]{1,2,0:T(8,128)(2,1)S(1)}, u32[]{:S(2)}, u32[]{:S(2)}) async-start(bf16[4,256,336]{1,2,0:T(8,128)(2,1)} %multiply_convert_fusion), calls=%async_computation.1 | async-start | bytes 1376256 | tf_op jit(solution)/shard_map/all_to_all | solution.py:24
  38.9 0.1 copy.35
  39.0 0.1 copy.34
  39.1 0.1 fusion.26
  39.2 18.5 %all-to-all-done.1 = bf16[4,256,336]{1,2,0:T(8,128)(2,1)S(1)} async-done(((bf16[4,256,336]{1,2,0:T(8,128)(2,1)}), bf16[4,256,336]{1,2,0:T(8,128)(2,1)S(1)}, u32[]{:S(2)}, u32[]{:S(2)}) %all-to-all-start.1) | async-done | bytes 688160 | tf_op jit(solution)/shard_map/all_to_all | solution.py:24
  57.7 2.1 all-gather.6.cloned.1.call-done.out_w
  59.8 2.8 fusion
  62.6 0.1 slice_select_fusion
  62.7 0.8 collective-permute-start.1
  63.5 1.5 collective-permute-done.1
  65.0 0.1 add_bitcast_fusion
  65.2 26.4 %all_to_all.68 = f32[32,8,512]{2,1,0:T(8,128)S(1)} all-to-all(f32[32,8,512]{2,1,0:T(8,128)S(1)} %add_bitcast_fusion), channel_id=1, replica_groups=mesh['dp'=4,'z'=8,'y'=4,'c'=2] {'z','y'}, dimensions={0} | all-to-all | bytes 1048576 | tf_op jit(solution)/shard_map/all_to_all | solution.py:24
  91.7 15.2 %all_to_all.69 = bf16[32,8,512]{2,1,0:T(8,128)(2,1)S(1)} all-to-all(bf16[32,8,512]{2,1,0:T(8,128)(2,1)S(1)} %broadcast_in_dim.26), channel_id=1, replica_groups=mesh['dp'=4,'z'=8,'y'=4,'c'=2] {'z','y'}, dimensions={0} | all-to-all | bytes 524288 | tf_op jit(solution)/shard_map/all_to_all | solution.py:24
  106.9 3.8 %collective-permute-start.2 = (bf16[256,512]{1,0:T(8,128)(2,1)S(1)}, bf16[256,512]{1,0:T(8,128)(2,1)S(1)}, u32[]{:S(2)}, u32[]{:S(2)}) collective-permute-start(bf16[256,512]{1,0:T(8,128)(2,1)S(1)} %bitcast.61), channel_id=1, source_target_pairs={{0,1},{1,0},{2,3},{3,2},{4,5},{5,4},{6,7},{7,6},{8,9},{9,8},{10,11... | collective-permute-start | bytes 786440 | tf_op jit(solution)/shard_map/ppermute | solution.py:20
  110.6 1.2 collective-permute-done.2
  111.8 0.3 fusion.3
  112.1 1.1 broadcast_in_dim.27
  113.2 3.9 %all-to-all-start.4 = ((bf16[32,64,256]{2,1,0:T(8,128)(2,1)}), bf16[32,64,256]{2,1,0:T(8,128)(2,1)S(1)}, u32[]{:S(2)}, u32[]{:S(2)}) async-start(bf16[32,64,256]{2,1,0:T(8,128)(2,1)} %broadcast_in_dim.27), calls=%async_computation.4 | async-start | bytes 2097152 | tf_op jit(solution)/shard_map/all_to_all | solution.py:24
  117.2 0.7 all-gather.8.cloned.1.call-update
  117.9 26.4 %all-to-all-done.4.own = bf16[32,64,256]{2,1,0:T(8,128)(2,1)S(1)} async-done(((bf16[32,64,256]{2,1,0:T(8,128)(2,1)}), bf16[32,64,256]{2,1,0:T(8,128)(2,1)S(1)}, u32[]{:S(2)}, u32[]{:S(2)}) %all-to-all-start.4) | async-done | bytes 1048608 | tf_op jit(solution)/shard_map/all_to_all | solution.py:24
  144.3 2.1 collective-permute-start.3
  146.5 0.1 reshape.52
  146.6 0.1 copy.36
  146.8 0.1 copy.37.target
  146.9 1.8 collective-permute-done.3.peer
  148.8 9.5 %head.1 = (f32[256,1024]{1,0:T(8,128)S(1)}, f32[8,256]{1,0:T(8,128)S(1)}) custom-call(s32[1]{0:T(128)} %bitcast.core, bf16[32,64,256]{2,1,0:T(8,128)(2,1)S(1)} %all-to-all-done.4.own, bf16[32,64,256]{2,1,0:T(8,128)(2,1)S(1)} %collective-permute-done.3.peer, f32[8,64,8]{2,1,0:T(8,128)S(1)} %bitcast.51, bf16[32,2,64,1024]{3,2,1,0:T(8,128)(2,1)} %bitcast.53, ...), custom_call_target="tpu_custom_call" | custom-call | tf_op jit(solution)/shard_map/head/pallas_call | solution.py:139
  158.3 23.3 %all_to_all.70.stats = f32[64,8,256]{2,1,0:T(8,128)S(1)} all-to-all(f32[64,8,256]{2,1,0:T(8,128)S(1)} %broadcast_in_dim.29), channel_id=1, replica_groups=mesh['dp'=4,'z'=8,'y'=4,'c'=2] {'z','y','c'}, dimensions={0} | all-to-all | bytes 1048576 | tf_op jit(solution)/shard_map/all_to_all | solution.py:24
  181.6 4.6 %loss.1 = (bf16[256,1024]{1,0:T(8,128)(2,1)S(1)}, bf16[32,64,256]{2,1,0:T(8,128)(2,1)S(1)}, f32[8,256]{1,0:T(8,128)S(1)}) custom-call(s32[1]{0:T(128)} %bitcast.core, f32[64,8,256]{2,1,0:T(8,128)S(1)} %all_to_all.70.stats, f32[256,1024]{1,0:T(8,128)S(1)} %get-tuple-element.16.logits, s32[256,1]{1,0:T(8,128)S(1)} %copy.37.target, f32[1,256]{1,0:T(1,128)S(1)} %bitcast.52, ...), custom_call_target="tpu_custom_call" | custom-call | tf_op jit(solution)/shard_map/loss/pallas_call | solution.py:169
  186.3 0.5 collective-permute-start.4
  186.8 4.0 %keep.1 = f32[32,64,256]{2,1,0:T(8,128)S(1)} custom-call(s32[1]{0:T(128)} %bitcast.core, bf16[256,1024]{1,0:T(8,128)(2,1)S(1)} %get-tuple-element.18.grad, bf16[32,2,64,1024]{3,2,1,0:T(8,128)(2,1)} %bitcast.55), custom_call_target="tpu_custom_call" | custom-call | flops 1073741824 | bytes 4194304 | tf_op jit(solution)/shard_map/keep/pallas_call | solution.py:200
  190.8 2.6 add_convert_fusion
  193.4 4.9 %all-to-all-start.6 = ((bf16[32,64,256]{2,1,0:T(8,128)(2,1)}), bf16[32,64,256]{2,1,0:T(8,128)(2,1)S(1)}, u32[]{:S(2)}, u32[]{:S(2)}) async-start(bf16[32,64,256]{2,1,0:T(8,128)(2,1)} %add_convert_fusion), calls=%async_computation.6 | async-start | bytes 2097152 | tf_op jit(solution)/shard_map/all_to_all | solution.py:24
  198.3 0.6 collective-permute-start.6
  198.9 0.6 fusion.27
  199.5 26.1 %all-to-all-done.6 = bf16[32,64,256]{2,1,0:T(8,128)(2,1)S(1)} async-done(((bf16[32,64,256]{2,1,0:T(8,128)(2,1)}), bf16[32,64,256]{2,1,0:T(8,128)(2,1)S(1)}, u32[]{:S(2)}, u32[]{:S(2)}) %all-to-all-start.6) | async-done | bytes 1048608 | tf_op jit(solution)/shard_map/all_to_all | solution.py:24
  225.6 0.2 convert_reduce_fusion
  225.8 0.1 subtract_convert_fusion
  225.9 1.7 collective-permute-start.5
  227.6 0.2 fusion.18
  227.9 0.6 collective-permute-done.5
  228.5 0.2 fusion.2
  228.7 16.7 %all_to_all.71 = bf16[32,8,512]{2,1,0:T(8,128)(2,1)S(1)} all-to-all(bf16[32,8,512]{2,1,0:T(8,128)(2,1)S(1)} %fusion.2), channel_id=1, replica_groups=mesh['dp'=4,'z'=8,'y'=4,'c'=2] {'z','y'}, dimensions={0} | all-to-all | bytes 524288 | tf_op jit(solution)/shard_map/all_to_all | solution.py:24
  245.5 15.0 %all_to_all.72 = bf16[32,8,512]{2,1,0:T(8,128)(2,1)S(1)} all-to-all(bf16[32,8,512]{2,1,0:T(8,128)(2,1)S(1)} %broadcast_in_dim.31), channel_id=1, replica_groups=mesh['dp'=4,'z'=8,'y'=4,'c'=2] {'z','y'}, dimensions={0} | all-to-all | bytes 524288 | tf_op jit(solution)/shard_map/all_to_all | solution.py:24
  260.5 3.3 %collective-permute-start.7 = (bf16[256,512]{1,0:T(8,128)(2,1)S(1)}, bf16[256,512]{1,0:T(8,128)(2,1)S(1)}, u32[]{:S(2)}, u32[]{:S(2)}) collective-permute-start(bf16[256,512]{1,0:T(8,128)(2,1)S(1)} %bitcast.49), channel_id=1, source_target_pairs={{0,1},{1,0},{2,3},{3,2},{4,5},{5,4},{6,7},{7,6},{8,9},{9,8},{10,11... | collective-permute-start | bytes 786440 | tf_op jit(solution)/shard_map/ppermute | solution.py:20
  263.8 0.4 copy.39.active
  264.2 0.7 collective-permute-done.7.peer
  265.0 1.8 copy-done
  266.7 1.8 copy-done.1
  268.5 8.5 %expert.1 = (f32[256,640]{1,0:T(8,128)S(1)}, bf16[256,640]{1,0:T(8,128)(2,1)S(1)}) custom-call(s32[1]{0:T(128)} %bitcast.core, bf16[256,512]{1,0:T(8,128)(2,1)S(1)} %bitcast.50, bf16[256,512]{1,0:T(8,128)(2,1)S(1)} %collective-permute-done.7.peer, bf16[256,1024]{1,0:T(8,128)(2,1)S(1)} %copy-done.2, bf16[4,256,336]{2,1,0:T(8,128)(2,1)S(1)} %copy.39.active, ...), custom_call_target="tpu_custom_call" | custom-call | tf_op jit(solution)/shard_map/expert/pallas_call | solution.py:287
  277.0 0.4 collective-permute-start.8
  277.5 1.3 collective-permute-done.8
  278.8 16.1 %all_to_all.73 = bf16[32,8,640]{2,1,0:T(8,128)(2,1)S(1)} all-to-all(bf16[32,8,640]{2,1,0:T(8,128)(2,1)S(1)} %fusion.17), channel_id=1, replica_groups=mesh['dp'=4,'z'=8,'y'=4,'c'=2] {'z','y'}, dimensions={0} | all-to-all | bytes 655360 | tf_op jit(solution)/shard_map/all_to_all | solution.py:24
  295.0 15.8 %all_to_all.74 = bf16[32,8,640]{2,1,0:T(8,128)(2,1)S(1)} all-to-all(bf16[32,8,640]{2,1,0:T(8,128)(2,1)S(1)} %broadcast_in_dim.62), channel_id=1, replica_groups=mesh['dp'=4,'z'=8,'y'=4,'c'=2] {'z','y'}, dimensions={0} | all-to-all | bytes 655360 | tf_op jit(solution)/shard_map/all_to_all | solution.py:24
  310.8 3.8 %collective-permute-start.9 = (bf16[256,512]{1,0:T(8,128)(2,1)S(1)}, bf16[256,512]{1,0:T(8,128)(2,1)S(1)}, u32[]{:S(2)}, u32[]{:S(2)}) collective-permute-start(bf16[256,512]{1,0:T(8,128)(2,1)S(1)} %slice.33), channel_id=1, source_target_pairs={{0,1},{1,0},{2,3},{3,2},{4,5},{5,4},{6,7},{7,6},{8,9},{9,8},{10,11... | collective-permute-start | bytes 786440 | tf_op jit(solution)/shard_map/ppermute | solution.py:20
  314.6 0.7 bitcast_subtract_fusion
  315.3 0.7 copy.40
  316.0 1.1 fusion.15
  (48 shorter events, 0.8 us)
Async XLA Ops:
  7.2 52.6 %all-gather.6.cloned.1.call-start = ((), (), s32[]{:S(2)}) async-start(), calls=%async_computation.11 | async-start | bytes 3440640 | tf_op jit(solution)/shard_map/all_gather | solution.py:362
  7.9 24.2 %copy-start.4 = (bf16[1,1024,336]{1,2,0:T(8,128)(2,1)S(1)}, bf16[1,1024,336]{1,2,0:T(8,128)(2,1)}, u32[]{:S(2)}) copy-start(bf16[1,1024,336]{1,2,0:T(8,128)(2,1)} %param.16) | copy-start | bytes 2064388
  27.9 5.4 %copy-start.5 = (bf16[1,1024,336]{1,2,0:T(8,128)(2,1)S(1)}, bf16[1,1024,336]{1,2,0:T(8,128)(2,1)}, u32[]{:S(2)}) copy-start(bf16[1,1024,336]{1,2,0:T(8,128)(2,1)} %param.17) | copy-start | bytes 2064388
  27.9 4.2 %collective-permute-start = (bf16[4,256,512]{2,1,0:T(8,128)(2,1)S(1)}, bf16[4,256,512]{2,1,0:T(8,128)(2,1)S(1)}, u32[]{:S(2)}, u32[]{:S(2)}) collective-permute-start(bf16[4,256,512]{2,1,0:T(8,128)(2,1)S(1)} %all_to_all.67), channel_id=1, source_target_pairs={{0,1},{1,0},{2,3},{3,2},{4,5},{5,4},{6,7},{7,6},{8,9},{9,8},{10,11... | collective-permute-start | bytes 3145736 | tf_op jit(solution)/shard_map/ppermute | solution.py:20
  33.3 5.5 %copy-start.7 = (f32[256,22]{0,1:T(8,128)S(1)}, f32[256,22]{0,1:T(8,128)}, u32[]{:S(2)}) copy-start(f32[256,22]{0,1:T(8,128)} %param.14) | copy-start | bytes 67588
  33.3 5.7 %copy-start.8 = (s32[256,22]{0,1:T(8,128)S(1)}, s32[256,22]{0,1:T(8,128)}, u32[]{:S(2)}) copy-start(s32[256,22]{0,1:T(8,128)} %param.15) | copy-start | bytes 67588
  35.4 22.3 %all-to-all-start.1 = ((bf16[4,256,336]{1,2,0:T(8,128)(2,1)}), bf16[4,256,336]{1,2,0:T(8,128)(2,1)S(1)}, u32[]{:S(2)}, u32[]{:S(2)}) async-start(bf16[4,256,336]{1,2,0:T(8,128)(2,1)} %multiply_convert_fusion), calls=%async_computation.1 | async-start | bytes 1376256 | tf_op jit(solution)/shard_map/all_to_all | solution.py:24
  62.7 49.1 %copy-start.6 = (bf16[1024,64]{0,1:T(8,128)(2,1)S(1)}, bf16[1024,64]{0,1:T(8,128)(2,1)}, u32[]{:S(2)}) copy-start(bf16[1024,64]{0,1:T(8,128)(2,1)} %param.19) | copy-start | bytes 393220
  62.7 49.1 %copy-start.11 = (bf16[256,64]{0,1:T(8,128)(2,1)S(1)}, bf16[256,64]{0,1:T(8,128)(2,1)}, u32[]{:S(2)}) copy-start(bf16[256,64]{0,1:T(8,128)(2,1)} %param.13) | copy-start | bytes 98308
  62.7 2.3 collective-permute-start.1
  106.9 4.9 %collective-permute-start.2 = (bf16[256,512]{1,0:T(8,128)(2,1)S(1)}, bf16[256,512]{1,0:T(8,128)(2,1)S(1)}, u32[]{:S(2)}, u32[]{:S(2)}) collective-permute-start(bf16[256,512]{1,0:T(8,128)(2,1)S(1)} %bitcast.61), channel_id=1, source_target_pairs={{0,1},{1,0},{2,3},{3,2},{4,5},{5,4},{6,7},{7,6},{8,9},{9,8},{10,11... | collective-permute-start | bytes 786440 | tf_op jit(solution)/shard_map/ppermute | solution.py:20
  112.1 34.4 %copy-start.9 = (bf16[4096]{0:T(1024)(128)(2,1)S(1)}, bf16[4096]{0:T(1024)(128)(2,1)}, u32[]{:S(2)}) copy-start(bf16[4096]{0:T(1024)(128)(2,1)} %param.20) | copy-start | bytes 24580
  112.1 34.6 %copy-start.10 = (s32[256]{0:T(256)S(1)}, s32[256]{0:T(256)}, u32[]{:S(2)}) copy-start(s32[256]{0:T(256)} %param.22) | copy-start | bytes 3076
  113.2 31.1 %all-to-all-start.4 = ((bf16[32,64,256]{2,1,0:T(8,128)(2,1)}), bf16[32,64,256]{2,1,0:T(8,128)(2,1)S(1)}, u32[]{:S(2)}, u32[]{:S(2)}) async-start(bf16[32,64,256]{2,1,0:T(8,128)(2,1)} %broadcast_in_dim.27), calls=%async_computation.4 | async-start | bytes 2097152 | tf_op jit(solution)/shard_map/all_to_all | solution.py:24
  117.1 147.0 %all-gather.8.cloned.1.call-start = ((), (), s32[]{:S(2)}) async-start(), calls=%async_computation.12 | async-start | bytes 3440640 | tf_op jit(solution)/shard_map/all_gather | solution.py:371
  117.9 146.3 %all-gather.10.cloned.1.call-start = ((), (), s32[]{:S(2)}) async-start(), calls=%async_computation.13 | async-start | bytes 3440640 | tf_op jit(solution)/shard_map/all_gather | solution.py:372
  144.3 4.4 %collective-permute-start.3 = (bf16[32,64,256]{2,1,0:T(8,128)(2,1)S(1)}, bf16[32,64,256]{2,1,0:T(8,128)(2,1)S(1)}, u32[]{:S(2)}, u32[]{:S(2)}) collective-permute-start(bf16[32,64,256]{2,1,0:T(8,128)(2,1)S(1)} %all-to-all-done.4.own), channel_id=1, source_target_pairs={{0,1},{1,0},{2,3},{3,2},{4,5},{5,4},{6,7},{7,6},{8,9},{9,8},{10,11... | collective-permute-start | bytes 3145736 | tf_op jit(solution)/shard_map/ppermute | solution.py:20
  148.7 32.9 %copy-start.3 = (f32[256]{0:T(256)S(1)}, f32[256]{0:T(256)}, u32[]{:S(2)}) copy-start(f32[256]{0:T(256)} %param.23) | copy-start | bytes 3076
  186.3 4.5 %collective-permute-start.4 = (bf16[32,64,256]{2,1,0:T(8,128)(2,1)S(1)}, bf16[32,64,256]{2,1,0:T(8,128)(2,1)}, u32[]{:S(2)}, u32[]{:S(2)}) collective-permute-start(bf16[32,64,256]{2,1,0:T(8,128)(2,1)S(1)} %get-tuple-element.19), channel_id=1, source_target_pairs={{0,1},{1,0},{2,3},{3,2},{4,5},{5,4},{6,7},{7,6},{8,9},{9,8},{10,11... | collective-permute-start | bytes 3145736 | tf_op jit(solution)/shard_map/ppermute | solution.py:20
  193.4 32.2 %all-to-all-start.6 = ((bf16[32,64,256]{2,1,0:T(8,128)(2,1)}), bf16[32,64,256]{2,1,0:T(8,128)(2,1)S(1)}, u32[]{:S(2)}, u32[]{:S(2)}) async-start(bf16[32,64,256]{2,1,0:T(8,128)(2,1)} %add_convert_fusion), calls=%async_computation.6 | async-start | bytes 2097152 | tf_op jit(solution)/shard_map/all_to_all | solution.py:24
  198.3 29.6 %collective-permute-start.6 = (bf16[512,64]{0,1:T(8,128)(2,1)S(1)}, bf16[512,64]{0,1:T(8,128)(2,1)S(1)}, u32[]{:S(2)}, u32[]{:S(2)}) collective-permute-start(bf16[512,64]{0,1:T(8,128)(2,1)S(1)} %broadcast_select_fusion), channel_id=1, source_target_pairs={{0,1},{1,0},{2,3},{3,2},{4,5},{5,4},{6,7},{7,6},{8,9},{9,8},{10,11... | collective-permute-start | bytes 196616 | tf_op jit(solution)/shard_map/ppermute | solution.py:20
  225.9 2.6 collective-permute-start.5
  227.9 37.1 %copy-start.2 = (bf16[256,1024]{1,0:T(8,128)(2,1)S(1)}, bf16[256,1024]{1,0:T(8,128)(2,1)}, u32[]{:S(2)}) copy-start(bf16[256,1024]{1,0:T(8,128)(2,1)} %latent.1) | copy-start | bytes 1572868
  260.5 4.5 %collective-permute-start.7 = (bf16[256,512]{1,0:T(8,128)(2,1)S(1)}, bf16[256,512]{1,0:T(8,128)(2,1)S(1)}, u32[]{:S(2)}, u32[]{:S(2)}) collective-permute-start(bf16[256,512]{1,0:T(8,128)(2,1)S(1)} %bitcast.49), channel_id=1, source_target_pairs={{0,1},{1,0},{2,3},{3,2},{4,5},{5,4},{6,7},{7,6},{8,9},{9,8},{10,11... | collective-permute-start | bytes 786440 | tf_op jit(solution)/shard_map/ppermute | solution.py:20
  265.0 1.8 copy-start
  266.7 1.8 copy-start.1
  277.0 1.7 collective-permute-start.8
  310.8 5.2 %collective-permute-start.9 = (bf16[256,512]{1,0:T(8,128)(2,1)S(1)}, bf16[256,512]{1,0:T(8,128)(2,1)S(1)}, u32[]{:S(2)}, u32[]{:S(2)}) collective-permute-start(bf16[256,512]{1,0:T(8,128)(2,1)S(1)} %slice.33), channel_id=1, source_target_pairs={{0,1},{1,0},{2,3},{3,2},{4,5},{5,4},{6,7},{7,6},{8,9},{9,8},{10,11... | collective-permute-start | bytes 786440 | tf_op jit(solution)/shard_map/ppermute | solution.py:20
Sparse Core Ops, SparseCore 0:
  9.8 49.9 all-gather.5
  119.8 38.0 all-gather.7
  186.9 33.1 all-gather.9

commit v4 on v2

v4 whole, which is shorter than its diff:
```python
import jax
import jax.numpy as jnp
from jax import lax
from jax.experimental import pallas as pl
from jax.experimental.pallas import tpu as pltpu
from jax.sharding import Mesh, PartitionSpec as P

norm_epsilon = 1e-05
plane = ("z", "y")
slab = ("z", "y", "c")
bf16 = jnp.bfloat16
f32 = jnp.float32


def dot(a, b, ca, cb):
    return lax.dot_general(a, b, (((ca,), (cb,)), ((), ())), preferred_element_type=f32)


def swap(x):
    return lax.ppermute(x, "c", [(0, 1), (1, 0)])


def deal(x, axes):
    return lax.all_to_all(x, axes, 0, 0, tiled=True)


def spread(x, axes):
    count = lax.axis_size(axes)
    return deal(jnp.broadcast_to(x[None], (count,) + x.shape), axes)


def limit(mib):
    return pltpu.CompilerParams(vmem_limit_bytes=mib << 20)


def over_last(x, w):
    return lax.dot_general(x, w, (((1,), (1,)), ((), ())), preferred_element_type=f32)


def head_kernel(core, own, peer, gain, words, target, logits, stats, scale):
    step = pl.program_id(0)
    last = pl.num_programs(0) - 1
    rows, wide = own.shape
    span = gain.shape[2]
    half = wide // span

    @pl.when(step == 0)
    def _():
        total = jnp.zeros((rows, 128), f32)
        for k in range(wide // 128):
            a = own[:, k * 128 : (k + 1) * 128].astype(f32)
            b = peer[:, k * 128 : (k + 1) * 128].astype(f32)
            total = total + a * a + b * b
        mean = jnp.sum(total, axis=1, keepdims=True) / (2 * wide) + norm_epsilon
        guess = lax.rsqrt(mean)
        guess = guess * (1.5 - 0.5 * mean * guess * guess)
        scale[...] = jnp.broadcast_to(guess, scale.shape)

    def add(source, index):
        h = source[:, pl.ds(pl.multiple_of(index * span, span), span)].astype(f32)
        h = (h * scale[:, 0:1] * gain[0]).astype(bf16)
        rhs = words[...].reshape(span, -1)
        part = jnp.dot(h, rhs, preferred_element_type=f32)

        @pl.when(step == 0)
        def _():
            logits[...] = part

        @pl.when(step > 0)
        def _():
            logits[...] += part

    @pl.when(step < half)
    def _():
        add(own, step)

    @pl.when(step >= half)
    def _():
        add(peer, step - half)

    @pl.when(step == last)
    def _():
        values = logits[...]
        peak = jnp.max(values, axis=1, keepdims=True)
        below = values - peak
        weight = jnp.exp(below)
        total = jnp.sum(weight, axis=1, keepdims=True)
        lean = jnp.sum(weight * below, axis=1, keepdims=True)
        at = lax.broadcasted_iota(jnp.int32, values.shape, 1) == target[...]
        hit = jnp.sum(jnp.where(at, values, 0.0), axis=1, keepdims=True)
        lane = lax.broadcasted_iota(jnp.int32, (rows, 128), 1)
        packed = jnp.where(lane == 0, peak, jnp.where(lane == 1, total, 0.0))
        packed = jnp.where(lane == 2, lean, jnp.where(lane == 3, hit, packed))
        packed = packed.T
        stats[0:4, :] = packed[0:4, 0:128]
        stats[4:8, :] = packed[0:4, 128:256]


def loss_kernel(core, stats, logits, target, cot, scale, words, grad, send, loss, marks):
    @pl.when(pl.program_id(0) == 0)
    def _():
        def stat(k):
            return jnp.concatenate([stats[:, k, :], stats[:, k + 4, :]], axis=1)

        peaks = stat(0)
        peak = jnp.max(peaks, axis=0, keepdims=True)
        gap = peaks - peak
        share = jnp.exp(gap)
        totals = stat(1)
        total = jnp.sum(share * totals, axis=0, keepdims=True)
        lean = jnp.sum(share * (stat(2) + gap * totals), axis=0, keepdims=True)
        hit = jnp.sum(stat(3), axis=0, keepdims=True)
        inverse = 1.0 / total
        inner = cot[...] * (lean * inverse - (hit - peak))
        row = lax.broadcasted_iota(jnp.int32, (128, peak.shape[1]), 0)
        packed = jnp.where(row == 0, peak, jnp.where(row == 1, inverse, 0.0))
        packed = jnp.where(row == 2, cot[...], jnp.where(row == 3, inner, packed))
        col = packed.T
        loss[...] = jnp.broadcast_to(peak + jnp.log(total) - hit, loss.shape)
        lane = lax.broadcasted_iota(jnp.int32, marks.shape, 1)
        marks[...] = jnp.where(lane == 0, scale[...], col[:, 3:4])
        probs = jnp.exp(logits[...] - col[:, 0:1]) * col[:, 1:2]
        at = lax.broadcasted_iota(jnp.int32, probs.shape, 1) == target[...]
        grad[...] = (col[:, 2:3] * (probs - jnp.where(at, 1.0, 0.0))).astype(bf16)

    rhs = words[...].reshape(-1, words.shape[3])
    send[...] = over_last(grad[...], rhs).astype(send.dtype)


def keep_kernel(core, grad, words, keep):
    keep[...] = over_last(grad[...], words[...].reshape(-1, words.shape[3]))


def lower_kernel(place, parts, hidden, gain, marks, lift, chunks, partial):
    total = jnp.sum(parts[...].astype(f32), axis=0)
    scale = marks[:, 0:1]
    inner = marks[:, 1:2]
    model = 2 * hidden.shape[1]
    d_res = scale * (total * gain[...])
    d_res = d_res - hidden[...].astype(f32) * (scale * scale * (inner / model))
    high = d_res.astype(bf16)
    low = (d_res - high.astype(f32)).astype(bf16)
    cols = chunks.shape[2] // 2
    for k in range(chunks.shape[0]):
        chunks[k, :, :cols] = high[:, k * cols : (k + 1) * cols]
        chunks[k, :, cols:] = low[:, k * cols : (k + 1) * cols]
    partial[...] = jnp.dot(high, lift[...], preferred_element_type=f32)


def expert_kernel(
    core, own, peer, latent, marks, gate_w, up_w, out_w, keep, send, routed, block, term
):
    step = pl.program_id(0)
    half = own.shape[1]
    width = latent.shape[1]
    gate = jnp.sum(marks[...], axis=1, keepdims=True)

    @pl.when(step == 0)
    def _():
        a = (own[...].astype(f32) * gate).astype(bf16)
        b = (peer[...].astype(f32) * gate).astype(bf16)

        @pl.when(core[0] == 0)
        def _():
            routed[:, :half] = a
            routed[:, half:] = b

        @pl.when(core[0] != 0)
        def _():
            routed[:, :half] = b
            routed[:, half:] = a

        block[...] = jnp.zeros_like(block)
        term[...] = jnp.zeros_like(term)

    gate_mat = gate_w[...].reshape(-1, width)
    up_mat = up_w[...].reshape(-1, width)
    out_mat = out_w[...].reshape(-1, width)
    gate_pre = over_last(latent[...], gate_mat)
    up_pre = over_last(latent[...], up_mat)
    act_grad = over_last(routed[...], out_mat)
    sig = 1.0 / (1.0 + jnp.exp(-gate_pre))
    active = (gate_pre * sig * up_pre).astype(bf16).astype(f32)
    term[...] += jnp.sum(act_grad * active, axis=1, keepdims=True)
    gate_back = (act_grad * up_pre * sig * (1.0 + gate_pre * (1.0 - sig))).astype(bf16)
    up_back = (act_grad * gate_pre * sig).astype(bf16)
    block[...] += jnp.dot(gate_back, gate_mat, preferred_element_type=f32) + jnp.dot(
        up_back, up_mat, preferred_element_type=f32
    )

    @pl.when(step == pl.num_programs(0) - 1)
    def _():
        share = term[...] / jnp.where(gate > 0, gate, 1.0)
        gate_grad = jnp.where(marks[...] > 0, share, 0.0)
        keep[:, half:] = gate_grad
        send[:, half:] = gate_grad.astype(bf16)

        @pl.when(core[0] == 0)
        def _():
            keep[:, :half] = block[:, :half]
            send[:, :half] = block[:, half:].astype(bf16)

        @pl.when(core[0] != 0)
        def _():
            keep[:, :half] = block[:, half:]
            send[:, :half] = block[:, :half].astype(bf16)


def whole(shape):
    return pl.BlockSpec(shape, lambda i, core: (0,) * len(shape))


def call(kernel, name, scalar, args, in_specs, out_specs, out_shape, steps, mib, scratch=(), cost=None):
    return pl.pallas_call(
        kernel,
        grid_spec=pltpu.PrefetchScalarGridSpec(
            num_scalar_prefetch=1,
            grid=(steps,),
            in_specs=in_specs,
            out_specs=out_specs,
            scratch_shapes=list(scratch),
        ),
        out_shape=out_shape,
        compiler_params=limit(mib),
        cost_estimate=cost,
        name=name,
    )(scalar, *args)


def struct(shape, dtype):
    return jax.ShapeDtypeStruct(shape, dtype)


def call_head(core, own, peer, gain, words, target):
    rows = own.shape[0]
    places, _, cols, count = words.shape
    steps, _, span = gain.shape
    half = steps // 2

    def part(i, core):
        return (i % half, jnp.where(i < half, core[0], 1 - core[0]), 0, 0)

    return call(
        head_kernel,
        "head",
        core,
        (own, peer, gain, words, target),
        [
            whole(own.shape),
            whole(peer.shape),
            pl.BlockSpec((1, 1, span), lambda i, core: (i, 0, 0)),
            pl.BlockSpec((span // cols, 1, cols, count), part),
            whole(target.shape),
        ],
        [whole((rows, count)), whole((8, 128)), whole((rows, 128))],
        [struct((rows, count), f32), struct((8, 128), f32), struct((rows, 128), f32)],
        steps,
        24,
    )


def call_loss(core, stats, logits, target, cot, scale, words, per):
    places, _, cols, count = words.shape
    rows = logits.shape[0]
    return call(
        loss_kernel,
        "loss",
        core,
        (stats, logits, target, cot, scale, words),
        [
            whole(stats.shape),
            whole(logits.shape),
            whole(target.shape),
            whole(cot.shape),
            whole(scale.shape),
            pl.BlockSpec((per, 1, cols, count), lambda i, core: (i, 1 - core[0], 0, 0)),
        ],
        [
            whole((rows, count)),
            pl.BlockSpec((rows, per * cols), lambda i, core: (0, i)),
            whole((8, rows)),
            whole((rows, 128)),
        ],
        [
            struct((rows, count), bf16),
            struct((rows, places * cols), bf16),
            struct((8, rows), f32),
            struct((rows, 128), f32),
        ],
        places // per,
        24,
    )


def call_keep(core, grad, words, per):
    places, _, cols, count = words.shape
    rows = grad.shape[0]
    return call(
        keep_kernel,
        "keep",
        core,
        (grad, words),
        [
            whole(grad.shape),
            pl.BlockSpec((per, 1, cols, count), lambda i, core: (i, core[0], 0, 0)),
        ],
        pl.BlockSpec((rows, per * cols), lambda i, core: (0, i)),
        struct((rows, places * cols), f32),
        places // per,
        24,
        cost=pl.CostEstimate(
            flops=places * cols * rows * count * 2,
            bytes_accessed=places * cols * count * 2,
            transcendentals=0,
        ),
    )


def call_lower(place, parts, hidden, gain, marks, lift):
    places, chunk, wide = parts.shape
    width = lift.shape[1]
    cols = wide // places
    return call(
        lower_kernel,
        "lower",
        place,
        (parts, hidden, gain, marks, lift),
        [
            whole(parts.shape),
            whole(hidden.shape),
            whole(gain.shape),
            pl.BlockSpec((chunk, 128), lambda i, place: (place[0], 0)),
            whole(lift.shape),
        ],
        [whole((places, chunk, 2 * cols)), whole((chunk, width))],
        [struct((places, chunk, 2 * cols), bf16), struct((chunk, width), f32)],
        1,
        24,
    )


def call_expert(core, own, peer, latent, marks, weights):
    rows, width = latent.shape
    quarters, _, units, _ = weights.shape
    lanes = own.shape[1] + marks.shape[1]
    per = 2

    def part(k):
        return pl.BlockSpec((per, 1, units, width), lambda i, core: (i, k, 0, 0))

    return call(
        expert_kernel,
        "expert",
        core,
        (own, peer, latent, marks, weights, weights, weights),
        [
            whole(own.shape),
            whole(peer.shape),
            whole(latent.shape),
            whole(marks.shape),
            part(0),
            part(1),
            part(2),
        ],
        [whole((rows, lanes)), whole((rows, lanes))],
        [struct((rows, lanes), f32), struct((rows, lanes), bf16)],
        quarters // per,
        56,
        scratch=[
            pltpu.VMEM((rows, width), bf16),
            pltpu.VMEM((rows, width), f32),
            pltpu.VMEM((rows, 1), f32),
        ],
    )


def on_device(
    latent,
    residual,
    gates,
    route_ids,
    w_gate,
    w_up,
    w_out,
    w_lift,
    norm_gain,
    w_vocab,
    targets,
    loss_cot,
):
    core = lax.axis_index("c")
    own_index = lax.axis_index(slab)
    place = lax.axis_index(plane)
    places = lax.axis_size(plane)
    groups = lax.axis_size("dp")
    rows, width = latent.shape
    half = width // 2
    cols = residual.shape[1]
    words = w_vocab.shape[1]
    chunk = rows // places
    wide = places * cols
    first = core == 0

    def mine(x, axis):
        a, b = jnp.split(x, 2, axis)
        return jnp.where(first, a, b)

    def other(x, axis):
        a, b = jnp.split(x, 2, axis)
        return jnp.where(first, b, a)

    def joined(own, peer, axis):
        return jnp.where(
            first,
            jnp.concatenate([own, peer], axis),
            jnp.concatenate([peer, own], axis),
        )

    gate_mat, up_mat, out_mat = w_gate[0], w_up[0], w_out[0]
    lift_wide = lax.all_gather(w_lift.T, plane, axis=0, tiled=True)

    chosen = route_ids == own_index
    gate_own = jnp.sum(jnp.where(chosen, gates, 0.0), axis=1)
    high = lax.reduce_precision(gate_own, 8, 7)
    middle = lax.reduce_precision(gate_own - high, 8, 7)
    low = gate_own - high - middle
    gate_rows = jnp.concatenate([high, middle, low, jnp.zeros_like(low)]).reshape(-1, half)
    extra = jnp.pad(gate_rows.astype(bf16), ((0, 16 - gate_rows.shape[0]), (0, 0)))
    out_keep = mine(out_mat, 1)
    out_peer = swap(other(out_mat, 1))

    lat_own = spread(jnp.concatenate([mine(latent, 1), extra]), "dp")
    lat_peer = swap(lat_own)

    def gate_of(x):
        parts = x[:, rows : rows + gate_rows.shape[0]].reshape(groups, -1).astype(f32)
        parts = parts.reshape(groups, -1, rows)
        return (parts[:, 0] + parts[:, 1] + parts[:, 2]).reshape(-1)

    gate_all, gate_peer = gate_of(lat_own), gate_of(lat_peer)
    lat_all = joined(lat_own[:, :rows], lat_peer[:, :rows], 2).reshape(-1, width)
    gate_part = dot(lat_all, gate_mat, 1, 0)
    up_part = dot(lat_all, up_mat, 1, 0)
    active = (jax.nn.silu(gate_part) * up_part).astype(bf16)
    active_peer = swap(active)
    part = dot(active, out_keep, 1, 0) * gate_all[:, None]
    part = part + dot(active_peer, out_peer, 1, 0) * gate_peer[:, None]
    summed = jnp.sum(deal(part, "dp").reshape(groups, rows, half), axis=0)

    summed = summed.reshape(places, chunk, half)
    carried = residual.reshape(places, chunk, cols).astype(f32)
    carried = jnp.pad(carried, ((0, 0), (0, 0), (0, 128 - cols)))
    dealt = deal(jnp.concatenate([summed, carried], axis=2), plane)
    comb_own = jnp.sum(dealt[:, :, :half], axis=0).astype(bf16)
    res_rows = dealt[:, :, half : half + cols].transpose(1, 0, 2).reshape(chunk, wide)
    comb_own, gate_mat, up_mat, out_mat = lax.optimization_barrier(
        (comb_own, gate_mat, up_mat, out_mat)
    )
    weights = lax.all_gather(jnp.stack([gate_mat.T, up_mat.T, out_mat]), "dp")

    combined = joined(comb_own, swap(comb_own), 1)
    hidden = (res_rows + dot(combined, lift_wide, 1, 1)).astype(bf16)
    hid_own = spread(hidden, plane).reshape(rows, wide)

    per = 16
    steps = places // per
    core_id = core.astype(jnp.int32)[None]
    gain_sides = norm_gain.astype(f32).reshape(places, 2, cols)
    gain_own = jnp.where(first, gain_sides[:, 0], gain_sides[:, 1]).reshape(steps, 1, -1)
    gain_peer = jnp.where(first, gain_sides[:, 1], gain_sides[:, 0]).reshape(steps, 1, -1)
    target = (targets - own_index * words)[:, None]
    vocab = w_vocab.reshape(places, 2, cols, words)
    logits, stats, scale = call_head(
        core_id, hid_own, swap(hid_own), jnp.concatenate([gain_own, gain_peer]), vocab, target
    )
    stats_all = spread(stats, slab)
    grad, send, loss, marks = call_loss(
        core_id, stats_all, logits, target, loss_cot[None], scale, vocab, 8
    )
    row_loss = loss[0]
    keep = call_keep(core_id, grad, vocab, 8)
    keep = (keep + swap(send).astype(f32)).astype(bf16)
    parts = deal(keep.reshape(places, chunk, wide), plane)
    chunks, partial = call_lower(
        place.astype(jnp.int32)[None], parts, hidden, gain_own.reshape(1, wide), marks, lift_wide
    )
    cg_rows = (mine(partial, 1) + swap(other(partial, 1))).astype(bf16)
    cg_rows = jnp.broadcast_to(cg_rows[None], (places, chunk, half))
    dealt = deal(jnp.concatenate([cg_rows, chunks], axis=2), plane)
    cg_own = dealt[:, :, :half].reshape(rows, half)
    d_residual = dealt[:, :, half : half + cols].astype(f32) + dealt[:, :, half + cols :].astype(f32)
    d_residual = d_residual.reshape(rows, cols)

    gate_marks = jnp.where(chosen, gates, 0.0)
    gate_marks = jnp.pad(gate_marks, ((0, 0), (0, 128 - gate_marks.shape[1])))
    keep, send = call_expert(core_id, cg_own, swap(cg_own), latent, gate_marks, weights)
    keep = (keep + swap(send).astype(f32)).astype(bf16)
    tail = jnp.sum(deal(keep, plane).astype(f32).reshape(places, chunk, -1), axis=0).astype(bf16)
    tail = spread(tail, plane).reshape(rows, -1)
    d_latent = joined(tail[:, :half], swap(tail[:, :half]), 1).astype(f32)
    d_gates = tail[:, half : half + gates.shape[1]].astype(f32)
    return (row_loss, d_residual, d_latent, d_gates)


def solution(mesh):
    fine = Mesh(mesh.devices.reshape(mesh.devices.shape[0], 8, 4, 2), ("dp", "z", "y", "c"))
    in_specs = (
        P("dp", None),
        P("dp", slab),
        P("dp", None),
        P("dp", None),
        P(slab, None, "dp"),
        P(slab, None, "dp"),
        P(slab, "dp", None),
        P(None, slab),
        P(),
        P(None, slab),
        P("dp"),
        P("dp"),
    )
    out_specs = (P("dp"), P("dp", slab), P("dp", None), P("dp", None))
    return jax.shard_map(
        on_device, mesh=fine, in_specs=in_specs, out_specs=out_specs, check_vma=False
    )
```

time: 332 us -> 310 us (0.934)
  matrix products: 37 us -> 8.66 us
  Pallas kernels: 0 us -> 21.5 us
  blocking collectives: 153 us -> 138 us
  local copies, waits for them, and re-layouts: 7.85 us -> 17.8 us
  starting transfers between devices: 33.4 us -> 28.3 us
  other arithmetic: 14.1 us -> 9.01 us
    dot_general x7 -> x0, matrix products: 22 us -> none  [the longest x1 6.82 us: on_device(): jnp.einsum('qtf,qlf->tl', gate_back, gate_full, preferred_element_type=f32)]
    pallas_call x0 -> x5, Pallas kernels: none -> 21.5 us  [call(): pl.pallas_call(kernel, grid_spec=pltpu.PrefetchScalarGridSpec(num_scalar_...]
    all_to_all x8 -> x6, blocking collectives: 153 us -> 138 us  [deal(): return lax.all_to_all(x, axes, 0, 0, tiled=True)]
    unnamed x27 -> x35, local copies, waits for them, and re-layouts: 0.98 us -> 13 us
    all_to_all x3, waiting for transfers between devices: 56 us -> 63.3 us  [deal(): return lax.all_to_all(x, axes, 0, 0, tiled=True)]
    convert_element_type x6 -> x3, other arithmetic: 7.71 us -> 0.78 us  [the longest x2 0.77 us: gate_of(): parts = x[:, rows:rows + gate_rows.shape[0]].reshape(groups, -1).astype(f32)]
    dot_general x5, matrix products: 15 us -> 8.66 us  [dot(): lax.dot_general(a, b, (((ca,), (cb,)), ((), ())), preferred_element_type=...]
    dot_general x1 -> x0, local copies, waits for them, and re-layouts: 5.63 us -> none  [dot(): lax.dot_general(a, b, (((ca,), (cb,)), ((), ())), preferred_element_type=...]
  transfers between devices with their start and end apart: 16 -> 15, of which waited for: 11 -> 10; matrix products, arithmetic and copies ran while one was open for 10% -> 7% of each run, Pallas kernels for 0% -> 4%
where the time goes in v4:
time: 310 us; the launch traced here: 309 us
  blocking collectives  138 us (45%)
  waiting for transfers between devices  70.7 us (23%)
  starting transfers between devices  28.3 us (9%)
  Pallas kernels  21.5 us (7%)
  local copies, waits for them, and re-layouts  17.8 us (6%)
  between operations  14.5 us (5%)
  other arithmetic  9.01 us (3%)
  matrix products  8.66 us (3%)
    all_to_all x6, blocking collectives, deal(): return lax.all_to_all(x, axes, 0, 0, tiled=True)  138 us
    all_to_all x3, waiting for transfers between devices, deal(): return lax.all_to_all(x, axes, 0, 0, tiled=True)  63.3 us
    pallas_call x5, Pallas kernels, call(): pl.pallas_call(kernel, grid_spec=pltpu.PrefetchScalarGridSpec(num_scalar_...  21.5 us
    ppermute x10, starting transfers between devices, swap(): return lax.ppermute(x, 'c', [(0, 1), (1, 0)])  15.8 us
    unnamed x35, local copies, waits for them, and re-layouts  13 us
    all_to_all x3, starting transfers between devices, deal(): return lax.all_to_all(x, axes, 0, 0, tiled=True)  12.5 us
    dot_general x5, matrix products, dot(): lax.dot_general(a, b, (((ca,), (cb,)), ((), ())), preferred_element_type=...  8.66 us
    ppermute x10, waiting for transfers between devices, swap(): return lax.ppermute(x, 'c', [(0, 1), (1, 0)])  6.78 us
  transfers between devices with their start and end apart: 15, of which 10 were waited for; matrix products, arithmetic and copies ran while one was open for 7% of the time, Pallas kernels for 4%

profile of v4, /device:TPU:1, one launch (start us, length us, event | category | flops | bytes accessed | tf_op | source)
XLA Modules:
  0.0 308.5 jit_solution(12179861521085791953)
XLA Ops:
  7.2 0.7 all-gather.4.cloned.1.call-update
  7.9 0.8 copy.30
  8.8 0.8 copy.29
  9.6 0.7 fusion.27
  10.3 1.1 slice_select_fusion
  11.5 19.3 %all_to_all.53 = bf16[4,272,512]{2,1,0:T(8,128)(2,1)S(1)} all-to-all(bf16[4,272,512]{2,1,0:T(8,128)(2,1)S(1)} %broadcast_in_dim.53), channel_id=1, replica_groups=mesh['dp'=4,'z'=8,'y'=4,'c'=2] {'dp'}, dimensions={0} | all-to-all | bytes 2228224 | tf_op jit(solution)/shard_map/all_to_all | solution.py:24
  30.8 2.2 collective-permute-start
  33.3 2.5 collective-permute-done
  35.8 1.3 slice.84
  37.1 1.2 fusion.5
  38.4 1.3 multiply_convert_fusion
  39.6 0.5 collective-permute-start.1
  40.1 0.8 slice_convert_fusion.1
  40.9 0.7 fusion.6
  41.6 0.2 collective-permute-done.1
  41.8 2.1 multiply_add_fusion
  43.9 3.7 %all-to-all-start.1 = ((f32[4,256,512]{2,1,0:T(8,128)}), f32[4,256,512]{2,1,0:T(8,128)S(1)}, u32[]{:S(2)}, u32[]{:S(2)}) async-start(f32[4,256,512]{2,1,0:T(8,128)} %bitcast.8), calls=%async_computation.1 | async-start | bytes 4194304 | tf_op jit(solution)/shard_map/all_to_all | solution.py:24
  47.7 0.1 copy.31
  47.9 25.9 %all-to-all-done.1 = f32[4,256,512]{2,1,0:T(8,128)S(1)} async-done(((f32[4,256,512]{2,1,0:T(8,128)}), f32[4,256,512]{2,1,0:T(8,128)S(1)}, u32[]{:S(2)}, u32[]{:S(2)}) %all-to-all-start.1) | async-done | bytes 2097184 | tf_op jit(solution)/shard_map/all_to_all | solution.py:24
  73.7 0.2 reduce_sum.40
  74.1 33.6 %all_to_all.54 = f32[32,8,640]{2,1,0:T(8,128)S(1)} all-to-all(f32[32,8,640]{2,1,0:T(8,128)S(1)} %pad_maximum_fusion.1), channel_id=1, replica_groups=mesh['dp'=4,'z'=8,'y'=4,'c'=2] {'z','y'}, dimensions={0} | all-to-all | bytes 1310720 | tf_op jit(solution)/shard_map/all_to_all | solution.py:24
  107.7 1.6 pad_maximum_fusion
  109.3 1.2 collective-permute-start.3
  110.7 0.7 collective-permute-done.3
  111.3 3.4 %fusion.hidden = bf16[8,2048]{1,0:T(8,128)(2,1)S(1)} fusion(f32[8,2048]{1,0:T(8,128)S(1)} %reshape.164, bf16[2048,1024]{1,0:T(8,128)(2,1)} %all-gather.4.cloned.1.call-done.lift, bf16[8,512]{1,0:T(8,128)(2,1)S(1)} %collective-permute-done.3, bf16[8,512]{1,0:T(8,128)(2,1)S(1)} %slice_reduce_fusion, pred[]{:T(512)S(6)} %eq.9), kind=kOutput, calls=%fused_computation.1 | convolution fusion | flops 33660928 | bytes 4308993 | tf_op jit(solution)/shard_map/dot_general | solution.py:16
  114.7 0.1 broadcast_in_dim.54
  114.8 31.7 %all_to_all.55 = bf16[32,8,2048]{2,1,0:T(8,128)(2,1)S(1)} all-to-all(bf16[32,8,2048]{2,1,0:T(8,128)(2,1)S(1)} %broadcast_in_dim.54), channel_id=1, replica_groups=mesh['dp'=4,'z'=8,'y'=4,'c'=2] {'z','y'}, dimensions={0} | all-to-all | bytes 2097152 | tf_op jit(solution)/shard_map/all_to_all | solution.py:24
  146.5 2.6 collective-permute-start.4
  149.2 0.5 broadcast.53
  149.7 0.7 fusion.26
  150.7 0.1 copy.33.target
  150.8 0.6 collective-permute-done.4.peer
  151.4 3.5 %copy-done = bf16[4096,1024]{1,0:T(8,128)(2,1)S(1)} copy-done((bf16[4096,1024]{1,0:T(8,128)(2,1)S(1)}, bf16[4096,1024]{1,0:T(8,128)(2,1)}, u32[]{:S(2)}) %copy-start) | copy-done | bytes 8388632
  154.9 5.2 %head.1 = (f32[256,1024]{1,0:T(8,128)S(1)}, f32[8,128]{1,0:T(8,128)S(1)}, f32[256,128]{1,0:T(8,128)S(1)}) custom-call(s32[1]{0:T(128)} %bitcast.core, bf16[256,2048]{1,0:T(8,128)(2,1)S(1)} %bitcast.50, bf16[256,2048]{1,0:T(8,128)(2,1)S(1)} %collective-permute-done.4.peer, f32[4,1,1024]{2,1,0:T(1,128)S(1)} %pad_maximum_fusion.3.gain, ...), custom_call_target="tpu_custom_call" | custom-call | tf_op jit(solution)/shard_map/head/pallas_call | solution.py:214
  160.1 19.3 %all_to_all.56.stats = f32[64,8,128]{2,1,0:T(8,128)S(1)} all-to-all(f32[64,8,128]{2,1,0:T(8,128)S(1)} %broadcast_in_dim.56), channel_id=1, replica_groups=mesh['dp'=4,'z'=8,'y'=4,'c'=2] {'z','y','c'}, dimensions={0} | all-to-all | bytes 524288 | tf_op jit(solution)/shard_map/all_to_all | solution.py:24
  179.4 3.4 %copy-done.1 = bf16[4096,1024]{1,0:T(8,128)(2,1)S(1)} copy-done((bf16[4096,1024]{1,0:T(8,128)(2,1)S(1)}, bf16[4096,1024]{1,0:T(8,128)(2,1)}, u32[]{:S(2)}) %copy-start.1) | copy-done | bytes 8388632
  182.8 3.0 loss.1
  185.8 0.3 collective-permute-start.5
  186.2 2.4 keep.1
  188.6 1.3 fusion.1
  189.8 4.0 %all-to-all-start.5 = ((bf16[32,8,2048]{2,1,0:T(8,128)(2,1)}), bf16[32,8,2048]{2,1,0:T(8,128)(2,1)S(1)}, u32[]{:S(2)}, u32[]{:S(2)}) async-start(bf16[32,8,2048]{2,1,0:T(8,128)(2,1)} %fusion.1), calls=%async_computation.5 | async-start | bytes 2097152 | tf_op jit(solution)/shard_map/all_to_all | solution.py:24
  193.9 26.7 %all-to-all-done.5.parts = bf16[32,8,2048]{2,1,0:T(8,128)(2,1)S(1)} async-done(((bf16[32,8,2048]{2,1,0:T(8,128)(2,1)}), bf16[32,8,2048]{2,1,0:T(8,128)(2,1)S(1)}, u32[]{:S(2)}, u32[]{:S(2)}) %all-to-all-start.5) | async-done | bytes 1048608 | tf_op jit(solution)/shard_map/all_to_all | solution.py:24
  220.7 2.2 copy-done.2
  222.8 0.8 lower.1
  223.7 2.3 collective-permute-start.6
  225.9 0.8 collective-permute-done.6
  226.8 17.9 %all_to_all.57 = bf16[32,8,640]{2,1,0:T(8,128)(2,1)S(1)} all-to-all(bf16[32,8,640]{2,1,0:T(8,128)(2,1)S(1)} %pad_maximum_fusion.2), channel_id=1, replica_groups=mesh['dp'=4,'z'=8,'y'=4,'c'=2] {'z','y'}, dimensions={0} | all-to-all | bytes 655360 | tf_op jit(solution)/shard_map/all_to_all | solution.py:24
  244.7 2.5 collective-permute-start.7
  247.2 0.7 pad.18.marks
  247.9 0.5 collective-permute-done.7.peer
  248.4 0.7 copy-done.11
  249.1 10.1 %expert.1 = (f32[256,640]{1,0:T(8,128)}, bf16[256,640]{1,0:T(8,128)(2,1)}) custom-call(s32[1]{0:T(128)} %bitcast.core, bf16[256,512]{1,0:T(8,128)(2,1)} %copy-done.5, bf16[256,512]{1,0:T(8,128)(2,1)} %copy-done.11, bf16[256,1024]{1,0:T(8,128)(2,1)} %latent.1, f32[256,128]{1,0:T(8,128)} %pad.18.marks, bf16[4,3,336,1024]{3,2,1,0:T(8,128)(2,1)} %bitcast.52, ...), custom_call_target="tpu_custom_call" | custom-call | tf_op jit(solution)/shard_map/expert/pallas_call | solution.py:214
  259.2 0.4 collective-permute-start.8
  259.5 1.5 collective-permute-done.8
  261.0 1.1 fusion.9
  262.2 16.3 %all_to_all.58 = bf16[32,8,640]{2,1,0:T(8,128)(2,1)S(1)} all-to-all(bf16[32,8,640]{2,1,0:T(8,128)(2,1)S(1)} %fusion.9), channel_id=1, replica_groups=mesh['dp'=4,'z'=8,'y'=4,'c'=2] {'z','y'}, dimensions={0} | all-to-all | bytes 655360 | tf_op jit(solution)/shard_map/all_to_all | solution.py:24
  278.5 0.8 broadcast_in_dim.60
  279.3 4.8 %all-to-all-start.8 = ((bf16[32,8,640]{2,1,0:T(8,128)(2,1)}), bf16[32,8,640]{2,1,0:T(8,128)(2,1)S(1)}, u32[]{:S(2)}, u32[]{:S(2)}) async-start(bf16[32,8,640]{2,1,0:T(8,128)(2,1)} %broadcast_in_dim.60), calls=%async_computation.8 | async-start | bytes 655360 | tf_op jit(solution)/shard_map/all_to_all | solution.py:24
  284.0 0.6 slice.77
  284.6 10.7 %all-to-all-done.8 = bf16[32,8,640]{2,1,0:T(8,128)(2,1)S(1)} async-done(((bf16[32,8,640]{2,1,0:T(8,128)(2,1)}), bf16[32,8,640]{2,1,0:T(8,128)(2,1)S(1)}, u32[]{:S(2)}, u32[]{:S(2)}) %all-to-all-start.8) | async-done | bytes 327712 | tf_op jit(solution)/shard_map/all_to_all | solution.py:24
  295.3 3.8 %collective-permute-start.9 = (bf16[256,512]{1,0:T(8,128)(2,1)S(1)}, bf16[256,512]{1,0:T(8,128)(2,1)S(1)}, u32[]{:S(2)}, u32[]{:S(2)}) collective-permute-start(bf16[256,512]{1,0:T(8,128)(2,1)S(1)} %slice.100), channel_id=1, source_target_pairs={{0,1},{1,0},{2,3},{3,2},{4,5},{5,4},{6,7},{7,6},{8,9},{9,8},{10,11... | collective-permute-start | bytes 786440 | tf_op jit(solution)/shard_map/ppermute | solution.py:20
  299.1 0.7 copy.35
  299.9 0.7 copy.36
  300.6 1.1 fusion.3
  (70 shorter events, 1.5 us)
Async XLA Ops:
  7.2 104.2 %all-gather.4.cloned.1.call-start = ((), (), s32[]{:S(2)}) async-start(), calls=%async_computation.9 | async-start | bytes 4325376 | tf_op jit(solution)/shard_map/all_gather | solution.py:420
  11.4 21.7 %copy-start.4 = (bf16[1,336,1024]{2,1,0:T(8,128)(2,1)S(1)}, bf16[1,336,1024]{2,1,0:T(8,128)(2,1)}, u32[]{:S(2)}) copy-start(bf16[1,336,1024]{2,1,0:T(8,128)(2,1)} %param.18) | copy-start | bytes 2064388
  30.8 5.0 %collective-permute-start = (bf16[4,272,512]{2,1,0:T(8,128)(2,1)S(1)}, bf16[4,272,512]{2,1,0:T(8,128)(2,1)}, u32[]{:S(2)}, u32[]{:S(2)}) collective-permute-start(bf16[4,272,512]{2,1,0:T(8,128)(2,1)S(1)} %all_to_all.53), channel_id=1, source_target_pairs={{0,1},{1,0},{2,3},{3,2},{4,5},{5,4},{6,7},{7,6},{8,9},{9,8},{10,11... | collective-permute-start | bytes 3342344 | tf_op jit(solution)/shard_map/ppermute | solution.py:20
  33.1 8.5 %collective-permute-start.2 = (bf16[336,512]{1,0:T(8,128)(2,1)S(1)}, bf16[336,512]{1,0:T(8,128)(2,1)S(1)}, u32[]{:S(2)}, u32[]{:S(2)}) collective-permute-start(bf16[336,512]{1,0:T(8,128)(2,1)S(1)} %broadcast_select_fusion), channel_id=1, source_target_pairs={{0,1},{1,0},{2,3},{3,2},{4,5},{5,4},{6,7},{7,6},{8,9},{9,8},{10,11... | collective-permute-start | bytes 1032200 | tf_op jit(solution)/shard_map/ppermute | solution.py:20
  33.2 3.9 %copy-start.6 = (bf16[1,1024,336]{1,2,0:T(8,128)(2,1)S(1)}, bf16[1,1024,336]{1,2,0:T(8,128)(2,1)}, u32[]{:S(2)}) copy-start(bf16[1,1024,336]{1,2,0:T(8,128)(2,1)} %param.16) | copy-start | bytes 2064388
  37.1 1.2 copy-start.8
  39.6 2.2 collective-permute-start.1
  43.9 3.8 %copy-start.12 = (bf16[256,64]{0,1:T(8,128)(2,1)S(1)}, bf16[256,64]{0,1:T(8,128)(2,1)}, u32[]{:S(2)}) copy-start(bf16[256,64]{0,1:T(8,128)(2,1)} %param.13) | copy-start | bytes 98308
  43.9 29.8 %all-to-all-start.1 = ((f32[4,256,512]{2,1,0:T(8,128)}), f32[4,256,512]{2,1,0:T(8,128)S(1)}, u32[]{:S(2)}, u32[]{:S(2)}) async-start(f32[4,256,512]{2,1,0:T(8,128)} %bitcast.8), calls=%async_computation.1 | async-start | bytes 4194304 | tf_op jit(solution)/shard_map/all_to_all | solution.py:24
  47.7 200.7 %all-gather.6.cloned.1.call-start = ((), (), s32[]{:S(2)}) async-start(), calls=%async_computation.10 | async-start | bytes 10321920 | tf_op jit(solution)/shard_map/all_gather | solution.py:459
  74.0 33.7 %copy-start.7 = (bf16[1,1024,336]{1,2,0:T(8,128)(2,1)S(1)}, bf16[1,1024,336]{1,2,0:T(8,128)(2,1)}, u32[]{:S(2)}) copy-start(bf16[1,1024,336]{1,2,0:T(8,128)(2,1)} %param.16) | copy-start | bytes 2064388
  74.0 33.7 %copy-start.9 = (bf16[1,1024,336]{1,2,0:T(8,128)(2,1)S(1)}, bf16[1,1024,336]{1,2,0:T(8,128)(2,1)}, u32[]{:S(2)}) copy-start(bf16[1,1024,336]{1,2,0:T(8,128)(2,1)} %param.17) | copy-start | bytes 2064388
  109.3 2.1 collective-permute-start.3
  114.7 34.4 %copy-start.13 = (bf16[4096]{0:T(1024)(128)(2,1)S(1)}, bf16[4096]{0:T(1024)(128)(2,1)}, u32[]{:S(2)}) copy-start(bf16[4096]{0:T(1024)(128)(2,1)} %param.20) | copy-start | bytes 24580
  114.7 35.9 %copy-start.14 = (s32[256]{0:T(256)S(1)}, s32[256]{0:T(256)}, u32[]{:S(2)}) copy-start(s32[256]{0:T(256)} %param.22) | copy-start | bytes 3076
  146.5 4.9 %collective-permute-start.4 = (bf16[256,2048]{1,0:T(8,128)(2,1)S(1)}, bf16[256,2048]{1,0:T(8,128)(2,1)S(1)}, u32[]{:S(2)}, u32[]{:S(2)}) collective-permute-start(bf16[256,2048]{1,0:T(8,128)(2,1)S(1)} %bitcast.49), channel_id=1, source_target_pairs={{0,1},{1,0},{2,3},{3,2},{4,5},{5,4},{6,7},{7,6},{8,9},{9,8},{10,11... | collective-permute-start | bytes 3145736 | tf_op jit(solution)/shard_map/ppermute | solution.py:20
  151.4 3.5 %copy-start = (bf16[4096,1024]{1,0:T(8,128)(2,1)S(1)}, bf16[4096,1024]{1,0:T(8,128)(2,1)}, u32[]{:S(2)}) copy-start(bf16[4096,1024]{1,0:T(8,128)(2,1)} %param.21) | copy-start | bytes 25165828
  154.9 24.6 %copy-start.3 = (f32[256]{0:T(256)S(1)}, f32[256]{0:T(256)}, u32[]{:S(2)}) copy-start(f32[256]{0:T(256)} %param.23) | copy-start | bytes 3076
  179.4 3.4 %copy-start.1 = (bf16[4096,1024]{1,0:T(8,128)(2,1)S(1)}, bf16[4096,1024]{1,0:T(8,128)(2,1)}, u32[]{:S(2)}) copy-start(bf16[4096,1024]{1,0:T(8,128)(2,1)} %param.21) | copy-start | bytes 25165828
  185.8 2.7 collective-permute-start.5
  189.8 30.8 %all-to-all-start.5 = ((bf16[32,8,2048]{2,1,0:T(8,128)(2,1)}), bf16[32,8,2048]{2,1,0:T(8,128)(2,1)S(1)}, u32[]{:S(2)}, u32[]{:S(2)}) async-start(bf16[32,8,2048]{2,1,0:T(8,128)(2,1)} %fusion.1), calls=%async_computation.5 | async-start | bytes 2097152 | tf_op jit(solution)/shard_map/all_to_all | solution.py:24
  220.7 2.2 copy-start.2
  223.6 23.5 %copy-start.10 = (f32[256,22]{1,0:T(8,128)S(1)}, f32[256,22]{1,0:T(8,128)}, u32[]{:S(2)}) copy-start(f32[256,22]{1,0:T(8,128)} %get-tuple-element.49) | copy-start | bytes 67588
  223.7 3.1 %collective-permute-start.6 = (f32[8,512]{1,0:T(8,128)S(1)}, f32[8,512]{1,0:T(8,128)S(1)}, u32[]{:S(2)}, u32[]{:S(2)}) collective-permute-start(f32[8,512]{1,0:T(8,128)S(1)} %slice_select_fusion.1), channel_id=1, source_target_pairs={{0,1},{1,0},{2,3},{3,2},{4,5},{5,4},{6,7},{7,6},{8,9},{9,8},{10,11... | collective-permute-start | bytes 49160 | tf_op jit(solution)/shard_map/ppermute | solution.py:20
  244.7 3.6 %copy-start.5 = (bf16[256,512]{1,0:T(8,128)(2,1)}, bf16[256,512]{1,0:T(8,128)(2,1)S(1)}, u32[]{:S(2)}) copy-start(bf16[256,512]{1,0:T(8,128)(2,1)S(1)} %slice_bitcast_fusion.own) | copy-start | bytes 786436
  244.7 3.6 %collective-permute-start.7 = (bf16[256,512]{1,0:T(8,128)(2,1)S(1)}, bf16[256,512]{1,0:T(8,128)(2,1)S(1)}, u32[]{:S(2)}, u32[]{:S(2)}) collective-permute-start(bf16[256,512]{1,0:T(8,128)(2,1)S(1)} %slice_bitcast_fusion.own), channel_id=1, source_target_pairs={{0,1},{1,0},{2,3},{3,2},{4,5},{5,4},{6,7},{7,6},{8,9},{9,8},{10,11... | collective-permute-start | bytes 786440 | tf_op jit(solution)/shard_map/ppermute | solution.py:20
  248.3 0.7 copy-start.11
  259.2 1.8 collective-permute-start.8
  279.3 16.0 %all-to-all-start.8 = ((bf16[32,8,640]{2,1,0:T(8,128)(2,1)}), bf16[32,8,640]{2,1,0:T(8,128)(2,1)S(1)}, u32[]{:S(2)}, u32[]{:S(2)}) async-start(bf16[32,8,640]{2,1,0:T(8,128)(2,1)} %broadcast_in_dim.60), calls=%async_computation.8 | async-start | bytes 655360 | tf_op jit(solution)/shard_map/all_to_all | solution.py:24
  295.3 5.3 %collective-permute-start.9 = (bf16[256,512]{1,0:T(8,128)(2,1)S(1)}, bf16[256,512]{1,0:T(8,128)(2,1)S(1)}, u32[]{:S(2)}, u32[]{:S(2)}) collective-permute-start(bf16[256,512]{1,0:T(8,128)(2,1)S(1)} %slice.100), channel_id=1, source_target_pairs={{0,1},{1,0},{2,3},{3,2},{4,5},{5,4},{6,7},{7,6},{8,9},{9,8},{10,11... | collective-permute-start | bytes 786440 | tf_op jit(solution)/shard_map/ppermute | solution.py:20
Sparse Core Ops, SparseCore 0:
  10.6 90.9 all-gather.3
  109.4 81.7 all-gather.5

commit v5 on v4

--- a/solution.py
+++ b/solution.py
@@ -148,27 +148,27 @@
 
 
 def expert_kernel(
-    core, own, peer, latent, marks, gate_w, up_w, out_w, keep, send, routed, block, term
+    core, own, peer, latent_t, marks, gate_w, up_w, out_w, keep, send, routed_t, block, term
 ):
     step = pl.program_id(0)
     half = own.shape[1]
-    width = latent.shape[1]
+    width, rows = latent_t.shape
     gate = jnp.sum(marks[...], axis=1, keepdims=True)
 
     @pl.when(step == 0)
     def _():
-        a = (own[...].astype(f32) * gate).astype(bf16)
-        b = (peer[...].astype(f32) * gate).astype(bf16)
+        a = (own[...].astype(f32) * gate).T.astype(bf16)
+        b = (peer[...].astype(f32) * gate).T.astype(bf16)
 
         @pl.when(core[0] == 0)
         def _():
-            routed[:, :half] = a
-            routed[:, half:] = b
+            routed_t[:half, :] = a
+            routed_t[half:, :] = b
 
         @pl.when(core[0] != 0)
         def _():
-            routed[:, :half] = b
-            routed[:, half:] = a
+            routed_t[:half, :] = b
+            routed_t[half:, :] = a
 
         block[...] = jnp.zeros_like(block)
         term[...] = jnp.zeros_like(term)
@@ -176,21 +176,23 @@
     gate_mat = gate_w[...].reshape(-1, width)
     up_mat = up_w[...].reshape(-1, width)
     out_mat = out_w[...].reshape(-1, width)
-    gate_pre = over_last(latent[...], gate_mat)
-    up_pre = over_last(latent[...], up_mat)
-    act_grad = over_last(routed[...], out_mat)
+    gate_pre = jnp.dot(gate_mat, latent_t[...], preferred_element_type=f32)
+    up_pre = jnp.dot(up_mat, latent_t[...], preferred_element_type=f32)
+    act_grad = jnp.dot(out_mat, routed_t[...], preferred_element_type=f32)
     sig = 1.0 / (1.0 + jnp.exp(-gate_pre))
-    active = (gate_pre * sig * up_pre).astype(bf16).astype(f32)
-    term[...] += jnp.sum(act_grad * active, axis=1, keepdims=True)
-    gate_back = (act_grad * up_pre * sig * (1.0 + gate_pre * (1.0 - sig))).astype(bf16)
-    up_back = (act_grad * gate_pre * sig).astype(bf16)
+    silu = gate_pre * sig
+    active = (silu * up_pre).astype(bf16).astype(f32)
+    term[...] += jnp.sum(act_grad * active, axis=0, keepdims=True)
+    gate_back = (act_grad * up_pre * sig * (1.0 + gate_pre * (1.0 - sig))).T.astype(bf16)
+    up_back = (act_grad * silu).T.astype(bf16)
     block[...] += jnp.dot(gate_back, gate_mat, preferred_element_type=f32) + jnp.dot(
         up_back, up_mat, preferred_element_type=f32
     )
 
     @pl.when(step == pl.num_programs(0) - 1)
     def _():
-        share = term[...] / jnp.where(gate > 0, gate, 1.0)
+        column = jnp.broadcast_to(term[...], (128, rows)).T[:, 0:1]
+        share = column / jnp.where(gate > 0, gate, 1.0)
         gate_grad = jnp.where(marks[...] > 0, share, 0.0)
         keep[:, half:] = gate_grad
         send[:, half:] = gate_grad.astype(bf16)
@@ -255,7 +257,7 @@
         [whole((rows, count)), whole((8, 128)), whole((rows, 128))],
         [struct((rows, count), f32), struct((8, 128), f32), struct((rows, 128), f32)],
         steps,
-        24,
+        57,
     )
 
 
@@ -288,7 +290,7 @@
             struct((rows, 128), f32),
         ],
         places // per,
-        24,
+        57,
     )
 
 
@@ -307,7 +309,7 @@
         pl.BlockSpec((rows, per * cols), lambda i, core: (0, i)),
         struct((rows, places * cols), f32),
         places // per,
-        24,
+        57,
         cost=pl.CostEstimate(
             flops=places * cols * rows * count * 2,
             bytes_accessed=places * cols * count * 2,
@@ -335,12 +337,12 @@
         [whole((places, chunk, 2 * cols)), whole((chunk, width))],
         [struct((places, chunk, 2 * cols), bf16), struct((chunk, width), f32)],
         1,
-        24,
-    )
-
-
-def call_expert(core, own, peer, latent, marks, weights):
-    rows, width = latent.shape
+        60,
+    )
+
+
+def call_expert(core, own, peer, latent_t, marks, weights):
+    width, rows = latent_t.shape
     quarters, _, units, _ = weights.shape
     lanes = own.shape[1] + marks.shape[1]
     per = 2
@@ -352,11 +354,11 @@
         expert_kernel,
         "expert",
         core,
-        (own, peer, latent, marks, weights, weights, weights),
+        (own, peer, latent_t, marks, weights, weights, weights),
         [
             whole(own.shape),
             whole(peer.shape),
-            whole(latent.shape),
+            whole(latent_t.shape),
             whole(marks.shape),
             part(0),
             part(1),
@@ -365,11 +367,11 @@
         [whole((rows, lanes)), whole((rows, lanes))],
         [struct((rows, lanes), f32), struct((rows, lanes), bf16)],
         quarters // per,
-        56,
+        58,
         scratch=[
-            pltpu.VMEM((rows, width), bf16),
+            pltpu.VMEM((width, rows), bf16),
             pltpu.VMEM((rows, width), f32),
-            pltpu.VMEM((rows, 1), f32),
+            pltpu.VMEM((1, rows), f32),
         ],
     )
 
@@ -417,7 +419,8 @@
         )
 
     gate_mat, up_mat, out_mat = w_gate[0], w_up[0], w_out[0]
-    lift_wide = lax.all_gather(w_lift.T, plane, axis=0, tiled=True)
+    lift_wide = lax.all_gather(w_lift.T[None], "z", axis=0, tiled=True)
+    lift_wide = lax.all_gather(lift_wide, "y", axis=1, tiled=True).reshape(wide, width)
 
     chosen = route_ids == own_index
     gate_own = jnp.sum(jnp.where(chosen, gates, 0.0), axis=1)
@@ -445,6 +448,7 @@
     active_peer = swap(active)
     part = dot(active, out_keep, 1, 0) * gate_all[:, None]
     part = part + dot(active_peer, out_peer, 1, 0) * gate_peer[:, None]
+    part, gate_mat, up_mat, out_mat = lax.optimization_barrier((part, gate_mat, up_mat, out_mat))
     summed = jnp.sum(deal(part, "dp").reshape(groups, rows, half), axis=0)
 
     summed = summed.reshape(places, chunk, half)
@@ -453,9 +457,6 @@
     dealt = deal(jnp.concatenate([summed, carried], axis=2), plane)
     comb_own = jnp.sum(dealt[:, :, :half], axis=0).astype(bf16)
     res_rows = dealt[:, :, half : half + cols].transpose(1, 0, 2).reshape(chunk, wide)
-    comb_own, gate_mat, up_mat, out_mat = lax.optimization_barrier(
-        (comb_own, gate_mat, up_mat, out_mat)
-    )
     weights = lax.all_gather(jnp.stack([gate_mat.T, up_mat.T, out_mat]), "dp")
 
     combined = joined(comb_own, swap(comb_own), 1)
@@ -493,7 +494,7 @@
 
     gate_marks = jnp.where(chosen, gates, 0.0)
     gate_marks = jnp.pad(gate_marks, ((0, 0), (0, 128 - gate_marks.shape[1])))
-    keep, send = call_expert(core_id, cg_own, swap(cg_own), latent, gate_marks, weights)
+    keep, send = call_expert(core_id, cg_own, swap(cg_own), latent.T, gate_marks, weights)
     keep = (keep + swap(send).astype(f32)).astype(bf16)
     tail = jnp.sum(deal(keep, plane).astype(f32).reshape(places, chunk, -1), axis=0).astype(bf16)
     tail = spread(tail, plane).reshape(rows, -1)

time: 310 us -> 351 us (1.13)
  waiting for transfers between devices: 70.7 us -> 105 us
  blocking collectives: 138 us -> 123 us
  Pallas kernels: 21.5 us -> 35.8 us
  starting transfers between devices: 28.3 us -> 34.1 us
  other arithmetic: 9.01 us -> 13.9 us
    all_gather x1 -> x2, waiting for transfers between devices: 0.01 us -> 39.3 us  [the longest x1 39.3 us: on_device(): lift_wide = lax.all_gather(w_lift.T[None], 'z', axis=0, tiled=True)]
    all_to_all x6, blocking collectives: 138 us -> 123 us  [deal(): return lax.all_to_all(x, axes, 0, 0, tiled=True)]
    pallas_call x5, Pallas kernels: 21.5 us -> 35.8 us  [call(): pl.pallas_call(kernel, grid_spec=pltpu.PrefetchScalarGridSpec(num_scalar_...]
    unnamed x35 -> x32, local copies, waits for them, and re-layouts: 13 us -> 6.94 us
    ppermute x10, starting transfers between devices: 15.8 us -> 21.8 us  [swap(): return lax.ppermute(x, 'c', [(0, 1), (1, 0)])]
    all_to_all x3, waiting for transfers between devices: 63.3 us -> 59.6 us  [deal(): return lax.all_to_all(x, axes, 0, 0, tiled=True)]
  transfers between devices with their start and end apart: 15 -> 16, of which waited for: 10 -> 9; matrix products, arithmetic and copies ran while one was open for 7% -> 9% of each run, Pallas kernels for 4% -> 7%
where the time goes in v5:
time: 351 us; the launch traced here: 350 us
  blocking collectives  123 us (35%)
  waiting for transfers between devices  105 us (30%)
  Pallas kernels  35.8 us (10%)
  starting transfers between devices  34.1 us (10%)
  local copies, waits for them, and re-layouts  14.4 us (4%)
  between operations  14.1 us (4%)
  other arithmetic  13.9 us (4%)
  matrix products  9.81 us (3%)
    all_to_all x6, blocking collectives, deal(): return lax.all_to_all(x, axes, 0, 0, tiled=True)  123 us
    all_to_all x3, waiting for transfers between devices, deal(): return lax.all_to_all(x, axes, 0, 0, tiled=True)  59.6 us
    all_gather x1, waiting for transfers between devices, on_device(): lift_wide = lax.all_gather(w_lift.T[None], 'z', axis=0, tiled=True)  39.3 us
    pallas_call x5, Pallas kernels, call(): pl.pallas_call(kernel, grid_spec=pltpu.PrefetchScalarGridSpec(num_scalar_...  35.8 us
    ppermute x10, starting transfers between devices, swap(): return lax.ppermute(x, 'c', [(0, 1), (1, 0)])  21.8 us
    all_to_all x3, starting transfers between devices, deal(): return lax.all_to_all(x, axes, 0, 0, tiled=True)  12.2 us
    dot_general x5, matrix products, dot(): lax.dot_general(a, b, (((ca,), (cb,)), ((), ())), preferred_element_type=...  9.81 us
  transfers between devices with their start and end apart: 16, of which 9 were waited for; matrix products, arithmetic and copies ran while one was open for 9% of the time, Pallas kernels for 7%

profile of v5, /device:TPU:1, one launch (start us, length us, event | category | flops | bytes accessed | tf_op | source)
XLA Modules:
  0.0 349.8 jit_solution(17274086798375258682)
XLA Ops:
  7.2 0.7 all-gather.8.cloned.1.call-update
  8.0 39.3 %all-gather.8.cloned.1.call-done = bf16[512,1024]{1,0:T(8,128)(2,1)} async-done(((bf16[64,1024]{1,0:T(8,128)(2,1)}), bf16[512,1024]{1,0:T(8,128)(2,1)}) %all-gather.8.cloned.1.call-update) | async-done | bytes 1048592 | tf_op jit(solution)/shard_map/all_gather | solution.py:422
  47.3 0.8 copy.32
  48.1 0.8 copy.31
  49.3 14.0 %all_to_all.53 = bf16[4,272,512]{2,1,0:T(8,128)(2,1)S(1)} all-to-all(bf16[4,272,512]{2,1,0:T(8,128)(2,1)S(1)} %broadcast_in_dim.56), channel_id=1, replica_groups=mesh['dp'=4,'z'=8,'y'=4,'c'=2] {'dp'}, dimensions={0} | all-to-all | bytes 2228224 | tf_op jit(solution)/shard_map/all_to_all | solution.py:24
  63.3 7.2 %collective-permute-start = (bf16[4,272,512]{2,1,0:T(8,128)(2,1)S(1)}, bf16[4,272,512]{2,1,0:T(8,128)(2,1)}, u32[]{:S(2)}, u32[]{:S(2)}) collective-permute-start(bf16[4,272,512]{2,1,0:T(8,128)(2,1)S(1)} %all_to_all.53), channel_id=1, source_target_pairs={{0,1},{1,0},{2,3},{3,2},{4,5},{5,4},{6,7},{7,6},{8,9},{9,8},{10,11... | collective-permute-start | bytes 3342344 | tf_op jit(solution)/shard_map/ppermute | solution.py:20
  70.5 0.8 broadcast_select_fusion
  71.5 1.6 collective-permute-done
  73.1 1.3 slice.84
  74.4 1.2 fusion.5
  75.6 1.3 multiply_convert_fusion
  76.9 0.5 collective-permute-start.1
  77.4 0.8 slice_convert_fusion.1
  78.2 0.7 fusion.6
  79.2 3.1 multiply_add_fusion
  82.3 3.6 %all-to-all-start.1 = ((f32[4,256,512]{2,1,0:T(8,128)}), f32[4,256,512]{2,1,0:T(8,128)S(1)}, u32[]{:S(2)}, u32[]{:S(2)}) async-start(f32[4,256,512]{2,1,0:T(8,128)} %bitcast.8), calls=%async_computation.1 | async-start | bytes 4194304 | tf_op jit(solution)/shard_map/all_to_all | solution.py:24
  85.9 2.8 pad_maximum_fusion
  89.0 23.0 %all-to-all-done.1 = f32[4,256,512]{2,1,0:T(8,128)S(1)} async-done(((f32[4,256,512]{2,1,0:T(8,128)}), f32[4,256,512]{2,1,0:T(8,128)S(1)}, u32[]{:S(2)}, u32[]{:S(2)}) %all-to-all-start.1) | async-done | bytes 2097184 | tf_op jit(solution)/shard_map/all_to_all | solution.py:24
  111.9 0.2 reduce_sum.40
  112.2 24.6 %all_to_all.54 = f32[32,8,640]{2,1,0:T(8,128)S(1)} all-to-all(f32[32,8,640]{2,1,0:T(8,128)S(1)} %pad_maximum_fusion.1), channel_id=1, replica_groups=mesh['dp'=4,'z'=8,'y'=4,'c'=2] {'z','y'}, dimensions={0} | all-to-all | bytes 1310720 | tf_op jit(solution)/shard_map/all_to_all | solution.py:24
  136.9 3.4 collective-permute-start.3
  140.4 0.7 collective-permute-done.3
  141.1 3.5 fusion.hidden
  144.6 30.9 %all_to_all.55 = bf16[32,8,2048]{2,1,0:T(8,128)(2,1)S(1)} all-to-all(bf16[32,8,2048]{2,1,0:T(8,128)(2,1)S(1)} %broadcast_in_dim.58), channel_id=1, replica_groups=mesh['dp'=4,'z'=8,'y'=4,'c'=2] {'z','y'}, dimensions={0} | all-to-all | bytes 2097152 | tf_op jit(solution)/shard_map/all_to_all | solution.py:24
  175.5 2.6 collective-permute-start.4
  178.3 0.5 broadcast.53
  178.8 0.7 fusion.26
  179.7 0.8 copy.35.target
  180.5 0.6 pad_maximum_fusion.3.gain
  181.1 1.0 copy-done.5
  182.1 8.9 %head.1 = (f32[256,1024]{1,0:T(8,128)}, f32[8,128]{1,0:T(8,128)}, f32[256,128]{1,0:T(8,128)}) custom-call(s32[1]{0:T(128)} %bitcast.core, bf16[256,2048]{1,0:T(8,128)(2,1)} %bitcast.60, bf16[256,2048]{1,0:T(8,128)(2,1)} %copy-done.5, f32[4,1,1024]{2,1,0:T(1,128)} %pad_maximum_fusion.3.gain, bf16[32,2,64,1024]{3,2,1,0:T(8,128)(2,1)} %bitcast.49, ...), custom_call_target="tpu_custom_call" | custom-call | tf_op jit(solution)/shard_map/head/pallas_call | solution.py:216
  190.9 0.7 broadcast_in_dim.60
  191.6 19.1 %all_to_all.56.stats = f32[64,8,128]{2,1,0:T(8,128)} all-to-all(f32[64,8,128]{2,1,0:T(8,128)S(1)} %broadcast_in_dim.60), channel_id=1, replica_groups=mesh['dp'=4,'z'=8,'y'=4,'c'=2] {'z','y','c'}, dimensions={0} | all-to-all | bytes 524288 | tf_op jit(solution)/shard_map/all_to_all | solution.py:24
  210.8 6.0 %loss.1 = (bf16[256,1024]{1,0:T(8,128)(2,1)}, bf16[256,2048]{1,0:T(8,128)(2,1)}, f32[8,256]{1,0:T(8,128)}, f32[256,128]{1,0:T(8,128)}) custom-call(s32[1]{0:T(128)} %bitcast.core, f32[64,8,128]{2,1,0:T(8,128)} %all_to_all.56.stats, f32[256,1024]{1,0:T(8,128)} %get-tuple-element.21.logits, s32[256,1]{1,0:T(8,128)} %copy.35.target, f32[1,256]{1,0:T(1,128)} %bitcast.79, ...), custom_call_target="tpu_custom_call" | custom-call | tf_op jit(solution)/shard_map/loss/pallas_call | solution.py:216
  216.8 0.3 collective-permute-start.5
  217.1 5.2 %keep.1 = f32[256,2048]{1,0:T(8,128)} custom-call(s32[1]{0:T(128)} %bitcast.core, bf16[256,1024]{1,0:T(8,128)(2,1)} %get-tuple-element.24.grad, bf16[32,2,64,1024]{3,2,1,0:T(8,128)(2,1)} %bitcast.51), custom_call_target="tpu_custom_call" | custom-call | flops 1073741824 | bytes 4194304 | tf_op jit(solution)/shard_map/keep/pallas_call | solution.py:216
  222.3 2.8 fusion.1
  225.2 4.0 %all-to-all-start.5 = ((bf16[32,8,2048]{2,1,0:T(8,128)(2,1)}), bf16[32,8,2048]{2,1,0:T(8,128)(2,1)S(1)}, u32[]{:S(2)}, u32[]{:S(2)}) async-start(bf16[32,8,2048]{2,1,0:T(8,128)(2,1)} %fusion.1), calls=%async_computation.5 | async-start | bytes 2097152 | tf_op jit(solution)/shard_map/all_to_all | solution.py:24
  229.2 0.7 select_n.120.gain
  229.9 26.6 %all-to-all-done.5.parts = bf16[32,8,2048]{2,1,0:T(8,128)(2,1)S(1)} async-done(((bf16[32,8,2048]{2,1,0:T(8,128)(2,1)}), bf16[32,8,2048]{2,1,0:T(8,128)(2,1)S(1)}, u32[]{:S(2)}, u32[]{:S(2)}) %all-to-all-start.5) | async-done | bytes 1048608 | tf_op jit(solution)/shard_map/all_to_all | solution.py:24
  256.5 1.0 copy-done.1
  257.5 3.9 %lower.1 = (bf16[32,8,128]{2,1,0:T(8,128)(2,1)}, f32[8,1024]{1,0:T(8,128)}) custom-call(s32[1]{0:T(128)} %bitcast.20.place, bf16[32,8,2048]{2,1,0:T(8,128)(2,1)} %copy-done.1, bf16[8,2048]{1,0:T(8,128)(2,1)} %copy-done.8, f32[1,2048]{1,0:T(1,128)} %select_n.120.gain, f32[256,128]{1,0:T(8,128)} %get-tuple-element.26.marks, bf16[2048,1024]{1,0:T(8,128)(2,1)} %bitcast.56), custom_call_target="tpu_custom_call" | custom-call | tf_op jit(solution)/shard_map/lower/pallas_call | solution.py:216
  261.4 0.7 slice_select_fusion.1
  262.1 1.7 collective-permute-start.6
  263.9 0.8 collective-permute-done.6
  264.7 0.7 add_convert_fusion.2
  265.5 0.9 pad_maximum_fusion.2
  266.3 17.9 %all_to_all.57 = bf16[32,8,640]{2,1,0:T(8,128)(2,1)S(1)} all-to-all(bf16[32,8,640]{2,1,0:T(8,128)(2,1)S(1)} %pad_maximum_fusion.2), channel_id=1, replica_groups=mesh['dp'=4,'z'=8,'y'=4,'c'=2] {'z','y'}, dimensions={0} | all-to-all | bytes 655360 | tf_op jit(solution)/shard_map/all_to_all | solution.py:24
  284.2 2.5 collective-permute-start.7
  286.7 1.0 copy.37
  287.7 0.7 pad.18.marks
  288.4 0.7 copy-done.9
  289.1 11.7 %expert.1 = (f32[256,640]{1,0:T(8,128)}, bf16[256,640]{1,0:T(8,128)(2,1)}) custom-call(s32[1]{0:T(128)} %bitcast.core, bf16[256,512]{1,0:T(8,128)(2,1)} %copy-done.4, bf16[256,512]{1,0:T(8,128)(2,1)} %copy-done.9, bf16[1024,256]{1,0:T(8,128)(2,1)} %bitcast.61, f32[256,128]{1,0:T(8,128)} %pad.18.marks, bf16[4,3,336,1024]{3,2,1,0:T(8,128)(2,1)} %bitcast.52, ...), custom_call_target="tpu_custom_call" | custom-call | tf_op jit(solution)/shard_map/expert/pallas_call | solution.py:216
  300.8 1.8 collective-permute-done.8
  302.6 1.1 fusion.9
  303.8 16.5 %all_to_all.58 = bf16[32,8,640]{2,1,0:T(8,128)(2,1)S(1)} all-to-all(bf16[32,8,640]{2,1,0:T(8,128)(2,1)S(1)} %fusion.9), channel_id=1, replica_groups=mesh['dp'=4,'z'=8,'y'=4,'c'=2] {'z','y'}, dimensions={0} | all-to-all | bytes 655360 | tf_op jit(solution)/shard_map/all_to_all | solution.py:24
  320.3 0.8 broadcast_in_dim.64
  321.1 4.5 %all-to-all-start.8 = ((bf16[32,8,640]{2,1,0:T(8,128)(2,1)}), bf16[32,8,640]{2,1,0:T(8,128)(2,1)S(1)}, u32[]{:S(2)}, u32[]{:S(2)}) async-start(bf16[32,8,640]{2,1,0:T(8,128)(2,1)} %broadcast_in_dim.64), calls=%async_computation.8 | async-start | bytes 655360 | tf_op jit(solution)/shard_map/all_to_all | solution.py:24
  325.7 1.3 slice.77
  326.9 10.0 %all-to-all-done.8 = bf16[32,8,640]{2,1,0:T(8,128)(2,1)S(1)} async-done(((bf16[32,8,640]{2,1,0:T(8,128)(2,1)}), bf16[32,8,640]{2,1,0:T(8,128)(2,1)S(1)}, u32[]{:S(2)}, u32[]{:S(2)}) %all-to-all-start.8) | async-done | bytes 327712 | tf_op jit(solution)/shard_map/all_to_all | solution.py:24
  336.9 3.8 %collective-permute-start.9 = (bf16[256,512]{1,0:T(8,128)(2,1)S(1)}, bf16[256,512]{1,0:T(8,128)(2,1)S(1)}, u32[]{:S(2)}, u32[]{:S(2)}) collective-permute-start(bf16[256,512]{1,0:T(8,128)(2,1)S(1)} %slice.100), channel_id=1, source_target_pairs={{0,1},{1,0},{2,3},{3,2},{4,5},{5,4},{6,7},{7,6},{8,9},{9,8},{10,11... | collective-permute-start | bytes 786440 | tf_op jit(solution)/shard_map/ppermute | solution.py:20
  340.8 0.7 copy.38
  341.5 0.7 copy.39
  342.2 1.1 fusion.3
  (70 shorter events, 1.8 us)
Async XLA Ops:
  7.2 42.0 %copy-start.3 = (bf16[256,1024]{1,0:T(8,128)(2,1)S(1)}, bf16[256,1024]{1,0:T(8,128)(2,1)}, u32[]{:S(2)}) copy-start(bf16[256,1024]{1,0:T(8,128)(2,1)} %param.12) | copy-start | bytes 1572868
  7.2 40.1 %all-gather.8.cloned.1.call-start = ((), (), s32[]{:S(2)}) async-start(), calls=%async_computation.10 | async-start | bytes 1179648 | tf_op jit(solution)/shard_map/all_gather | solution.py:422
  7.9 133.1 %all-gather.6.cloned.1.call-start = ((), (), s32[]{:S(2)}) async-start(), calls=%async_computation.9 | async-start | bytes 5242880 | tf_op jit(solution)/shard_map/all_gather | solution.py:423
  49.2 21.3 %copy-start = (bf16[1,336,1024]{2,1,0:T(8,128)(2,1)S(1)}, bf16[1,336,1024]{2,1,0:T(8,128)(2,1)}, u32[]{:S(2)}) copy-start(bf16[1,336,1024]{2,1,0:T(8,128)(2,1)} %param.18) | copy-start | bytes 2064388
  63.3 9.7 %collective-permute-start = (bf16[4,272,512]{2,1,0:T(8,128)(2,1)S(1)}, bf16[4,272,512]{2,1,0:T(8,128)(2,1)}, u32[]{:S(2)}, u32[]{:S(2)}) collective-permute-start(bf16[4,272,512]{2,1,0:T(8,128)(2,1)S(1)} %all_to_all.53), channel_id=1, source_target_pairs={{0,1},{1,0},{2,3},{3,2},{4,5},{5,4},{6,7},{7,6},{8,9},{9,8},{10,11... | collective-permute-start | bytes 3342344 | tf_op jit(solution)/shard_map/ppermute | solution.py:20
  71.3 7.6 %collective-permute-start.2 = (bf16[336,512]{1,0:T(8,128)(2,1)}, bf16[336,512]{1,0:T(8,128)(2,1)}, u32[]{:S(2)}, u32[]{:S(2)}) collective-permute-start(bf16[336,512]{1,0:T(8,128)(2,1)} %broadcast_select_fusion), channel_id=1, source_target_pairs={{0,1},{1,0},{2,3},{3,2},{4,5},{5,4},{6,7},{7,6},{8,9},{9,8},{10,11... | collective-permute-start | bytes 1032200 | tf_op jit(solution)/shard_map/ppermute | solution.py:20
  71.3 3.0 copy-start.6
  74.4 1.2 copy-start.7
  76.9 2.2 collective-permute-start.1
  82.3 29.7 %all-to-all-start.1 = ((f32[4,256,512]{2,1,0:T(8,128)}), f32[4,256,512]{2,1,0:T(8,128)S(1)}, u32[]{:S(2)}, u32[]{:S(2)}) async-start(f32[4,256,512]{2,1,0:T(8,128)} %bitcast.8), calls=%async_computation.1 | async-start | bytes 4194304 | tf_op jit(solution)/shard_map/all_to_all | solution.py:24
  85.9 202.5 %all-gather.10.cloned.1.call-start = ((), (), s32[]{:S(2)}) async-start(), calls=%async_computation.11 | async-start | bytes 10321920 | tf_op jit(solution)/shard_map/all_gather | solution.py:460
  85.9 2.9 copy-start.10
  136.9 4.2 %collective-permute-start.3 = (bf16[8,512]{1,0:T(8,128)(2,1)S(1)}, bf16[8,512]{1,0:T(8,128)(2,1)S(1)}, u32[]{:S(2)}, u32[]{:S(2)}) collective-permute-start(bf16[8,512]{1,0:T(8,128)(2,1)S(1)} %slice_reduce_fusion), channel_id=1, source_target_pairs={{0,1},{1,0},{2,3},{3,2},{4,5},{5,4},{6,7},{7,6},{8,9},{9,8},{10,11... | collective-permute-start | bytes 24584 | tf_op jit(solution)/shard_map/ppermute | solution.py:20
  144.5 46.4 %copy-start.8 = (bf16[8,2048]{1,0:T(8,128)(2,1)}, bf16[8,2048]{1,0:T(8,128)(2,1)S(1)}, u32[]{:S(2)}) copy-start(bf16[8,2048]{1,0:T(8,128)(2,1)S(1)} %fusion.hidden) | copy-start | bytes 98308
  144.5 33.7 %copy-start.11 = (bf16[4096]{0:T(1024)(128)(2,1)S(1)}, bf16[4096]{0:T(1024)(128)(2,1)}, u32[]{:S(2)}) copy-start(bf16[4096]{0:T(1024)(128)(2,1)} %param.20) | copy-start | bytes 24580
  144.5 35.2 %copy-start.12 = (s32[256]{0:T(256)S(1)}, s32[256]{0:T(256)}, u32[]{:S(2)}) copy-start(s32[256]{0:T(256)} %param.22) | copy-start | bytes 3076
  175.5 5.6 %copy-start.2 = (bf16[32,8,2048]{2,1,0:T(8,128)(2,1)}, bf16[32,8,2048]{2,1,0:T(8,128)(2,1)S(1)}, u32[]{:S(2)}) copy-start(bf16[32,8,2048]{2,1,0:T(8,128)(2,1)S(1)} %all_to_all.55) | copy-start | bytes 3145732
  175.5 5.6 %collective-permute-start.4 = (bf16[256,2048]{1,0:T(8,128)(2,1)S(1)}, bf16[256,2048]{1,0:T(8,128)(2,1)S(1)}, u32[]{:S(2)}, u32[]{:S(2)}) collective-permute-start(bf16[256,2048]{1,0:T(8,128)(2,1)S(1)} %bitcast.59), channel_id=1, source_target_pairs={{0,1},{1,0},{2,3},{3,2},{4,5},{5,4},{6,7},{7,6},{8,9},{9,8},{10,11... | collective-permute-start | bytes 3145736 | tf_op jit(solution)/shard_map/ppermute | solution.py:20
  181.1 1.0 copy-start.5
  216.8 5.5 %collective-permute-start.5 = (bf16[256,2048]{1,0:T(8,128)(2,1)}, bf16[256,2048]{1,0:T(8,128)(2,1)S(1)}, u32[]{:S(2)}, u32[]{:S(2)}) collective-permute-start(bf16[256,2048]{1,0:T(8,128)(2,1)} %get-tuple-element.25), channel_id=1, source_target_pairs={{0,1},{1,0},{2,3},{3,2},{4,5},{5,4},{6,7},{7,6},{8,9},{9,8},{10,11... | collective-permute-start | bytes 3145736 | tf_op jit(solution)/shard_map/ppermute | solution.py:20
  225.2 31.3 %all-to-all-start.5 = ((bf16[32,8,2048]{2,1,0:T(8,128)(2,1)}), bf16[32,8,2048]{2,1,0:T(8,128)(2,1)S(1)}, u32[]{:S(2)}, u32[]{:S(2)}) async-start(bf16[32,8,2048]{2,1,0:T(8,128)(2,1)} %fusion.1), calls=%async_computation.5 | async-start | bytes 2097152 | tf_op jit(solution)/shard_map/all_to_all | solution.py:24
  256.5 1.0 copy-start.1
  262.1 2.6 collective-permute-start.6
  284.2 4.2 %copy-start.4 = (bf16[256,512]{1,0:T(8,128)(2,1)}, bf16[256,512]{1,0:T(8,128)(2,1)S(1)}, u32[]{:S(2)}) copy-start(bf16[256,512]{1,0:T(8,128)(2,1)S(1)} %slice_bitcast_fusion.own) | copy-start | bytes 786436
  284.2 4.2 %collective-permute-start.7 = (bf16[256,512]{1,0:T(8,128)(2,1)S(1)}, bf16[256,512]{1,0:T(8,128)(2,1)S(1)}, u32[]{:S(2)}, u32[]{:S(2)}) collective-permute-start(bf16[256,512]{1,0:T(8,128)(2,1)S(1)} %slice_bitcast_fusion.own), channel_id=1, source_target_pairs={{0,1},{1,0},{2,3},{3,2},{4,5},{5,4},{6,7},{7,6},{8,9},{9,8},{10,11... | collective-permute-start | bytes 786440 | tf_op jit(solution)/shard_map/ppermute | solution.py:20
  288.4 0.7 copy-start.9
  300.8 1.8 collective-permute-start.8
  321.1 15.8 %all-to-all-start.8 = ((bf16[32,8,640]{2,1,0:T(8,128)(2,1)}), bf16[32,8,640]{2,1,0:T(8,128)(2,1)S(1)}, u32[]{:S(2)}, u32[]{:S(2)}) async-start(bf16[32,8,640]{2,1,0:T(8,128)(2,1)} %broadcast_in_dim.64), calls=%async_computation.8 | async-start | bytes 655360 | tf_op jit(solution)/shard_map/all_to_all | solution.py:24
  336.9 5.3 %collective-permute-start.9 = (bf16[256,512]{1,0:T(8,128)(2,1)S(1)}, bf16[256,512]{1,0:T(8,128)(2,1)S(1)}, u32[]{:S(2)}, u32[]{:S(2)}) collective-permute-start(bf16[256,512]{1,0:T(8,128)(2,1)S(1)} %slice.100), channel_id=1, source_target_pairs={{0,1},{1,0},{2,3},{3,2},{4,5},{5,4},{6,7},{7,6},{8,9},{9,8},{10,11... | collective-permute-start | bytes 786440 | tf_op jit(solution)/shard_map/ppermute | solution.py:20
Sparse Core Ops, SparseCore 0:
  9.8 37.4 all-gather.7
  49.1 54.3 all-gather.5
  105.3 84.9 all-gather.9

commit v6 on v2

v6 whole, which is shorter than its diff:
```python
import jax
import jax.numpy as jnp
from jax import lax
from jax.experimental import pallas as pl
from jax.experimental.pallas import tpu as pltpu
from jax.sharding import Mesh, PartitionSpec as P

norm_epsilon = 1e-05
plane = ("z", "y")
slab = ("z", "y", "c")
bf16 = jnp.bfloat16
f32 = jnp.float32


def dot(a, b, ca, cb):
    return lax.dot_general(a, b, (((ca,), (cb,)), ((), ())), preferred_element_type=f32)


def swap(x):
    return lax.ppermute(x, "c", [(0, 1), (1, 0)])


def deal(x, axes):
    return lax.all_to_all(x, axes, 0, 0, tiled=True)


def spread(x, axes):
    count = lax.axis_size(axes)
    return deal(jnp.broadcast_to(x[None], (count,) + x.shape), axes)


def over_last(x, w):
    return lax.dot_general(x, w, (((1,), (1,)), ((), ())), preferred_element_type=f32)


def bring(source, buffers, sems, count):
    copies = [pltpu.make_async_copy(source(k), buffers(k), sems.at[k]) for k in range(count)]
    for copy in copies:
        copy.start()
    return lambda k: copies[k].wait()


def head_kernel(core, own, peer, gain, words, target, logits, stats, scale, held, sems):
    rows, wide = own.shape
    blocks, per, cols, count = held.shape
    span = per * cols
    half = wide // span

    def source(k):
        side = core[0] if k < half else 1 - core[0]
        return words.at[pl.ds(k % half * per, per), side]

    wait = bring(source, lambda k: held.at[k], sems, blocks)
    total = jnp.zeros((rows, 128), f32)
    for k in range(wide // 128):
        a = own[:, k * 128 : (k + 1) * 128].astype(f32)
        b = peer[:, k * 128 : (k + 1) * 128].astype(f32)
        total = total + a * a + b * b
    mean = jnp.sum(total, axis=1, keepdims=True) / (2 * wide) + norm_epsilon
    guess = lax.rsqrt(mean)
    guess = guess * (1.5 - 0.5 * mean * guess * guess)
    scale[...] = jnp.broadcast_to(guess, scale.shape)
    for k in range(blocks):
        side = own if k < half else peer
        at = k % half * span
        h = side[:, at : at + span].astype(f32)
        h = (h * guess * gain[k : k + 1]).astype(bf16)
        wait(k)
        part = jnp.dot(h, held[k].reshape(span, count), preferred_element_type=f32)
        logits[...] = part if k == 0 else logits[...] + part

    values = logits[...]
    peak = jnp.max(values, axis=1, keepdims=True)
    below = values - peak
    weight = jnp.exp(below)
    total = jnp.sum(weight, axis=1, keepdims=True)
    lean = jnp.sum(weight * below, axis=1, keepdims=True)
    at = lax.broadcasted_iota(jnp.int32, values.shape, 1) == target[...]
    hit = jnp.sum(jnp.where(at, values, 0.0), axis=1, keepdims=True)
    lane = lax.broadcasted_iota(jnp.int32, (rows, 128), 1)
    packed = jnp.where(lane == 0, peak, jnp.where(lane == 1, total, 0.0))
    packed = jnp.where(lane == 2, lean, jnp.where(lane == 3, hit, packed))
    packed = packed.T
    stats[0:4, :] = packed[0:4, 0:128]
    stats[4:8, :] = packed[0:4, 128:256]


def grad_blocks(core, side, grad, words, held, sems):
    blocks, per, cols, count = held.shape
    wait = bring(
        lambda k: words.at[pl.ds(k * per, per), side], lambda k: held.at[k], sems, blocks
    )

    def block(k):
        wait(k)
        return over_last(grad[...], held[k].reshape(per * cols, count))

    return block


def loss_kernel(
    core, stats, logits, target, cot, scale, words, grad, send, loss, marks, held, sems
):
    block = grad_blocks(core, 1 - core[0], grad, words, held, sems)

    def stat(k):
        return jnp.concatenate([stats[:, k, :], stats[:, k + 4, :]], axis=1)

    peaks = stat(0)
    peak = jnp.max(peaks, axis=0, keepdims=True)
    gap = peaks - peak
    share = jnp.exp(gap)
    totals = stat(1)
    total = jnp.sum(share * totals, axis=0, keepdims=True)
    lean = jnp.sum(share * (stat(2) + gap * totals), axis=0, keepdims=True)
    hit = jnp.sum(stat(3), axis=0, keepdims=True)
    inverse = 1.0 / total
    inner = cot[...] * (lean * inverse - (hit - peak))
    row = lax.broadcasted_iota(jnp.int32, (128, peak.shape[1]), 0)
    packed = jnp.where(row == 0, peak, jnp.where(row == 1, inverse, 0.0))
    packed = jnp.where(row == 2, cot[...], jnp.where(row == 3, inner, packed))
    col = packed.T
    loss[...] = jnp.broadcast_to(peak + jnp.log(total) - hit, loss.shape)
    lane = lax.broadcasted_iota(jnp.int32, marks.shape, 1)
    marks[...] = jnp.where(lane == 0, scale[...], col[:, 3:4])
    probs = jnp.exp(logits[...] - col[:, 0:1]) * col[:, 1:2]
    at = lax.broadcasted_iota(jnp.int32, probs.shape, 1) == target[...]
    grad[...] = (col[:, 2:3] * (probs - jnp.where(at, 1.0, 0.0))).astype(bf16)
    blocks, per, cols, _ = held.shape
    span = per * cols
    for k in range(blocks):
        send[:, k * span : (k + 1) * span] = block(k).astype(send.dtype)


def keep_kernel(core, grad, words, keep, held, sems):
    block = grad_blocks(core, core[0], grad, words, held, sems)
    blocks, per, cols, _ = held.shape
    span = per * cols
    for k in range(blocks):
        keep[:, k * span : (k + 1) * span] = block(k)


def lift_kernel(core, own, peer, residual, lift, hidden, joined, held, sems):
    blocks, span, _ = held.shape
    half = own.shape[1]
    wait = bring(
        lambda k: lift.at[pl.ds(k * span, span)], lambda k: held.at[k], sems, blocks
    )
    flip = core[0] != 0
    joined[:, :half] = jnp.where(flip, peer[...], own[...])
    joined[:, half:] = jnp.where(flip, own[...], peer[...])
    rows = joined[...].astype(bf16)
    for k in range(blocks):
        wait(k)
        at = slice(k * span, (k + 1) * span)
        hidden[:, at] = (residual[:, at] + over_last(rows, held[k])).astype(bf16)


def lower_kernel(place, parts, hidden, gain, marks, lift, chunks, partial, held, sems):
    blocks, span, _ = held.shape
    wait = bring(
        lambda k: lift.at[pl.ds(k * span, span)], lambda k: held.at[k], sems, blocks
    )
    total = jnp.sum(parts[...].astype(f32), axis=0)
    scale = marks[:, 0:1]
    inner = marks[:, 1:2]
    model = 2 * hidden.shape[1]
    d_res = scale * (total * gain[...])
    d_res = d_res - hidden[...].astype(f32) * (scale * scale * (inner / model))
    high = d_res.astype(bf16)
    low = (d_res - high.astype(f32)).astype(bf16)
    cols = chunks.shape[2] // 2
    for k in range(chunks.shape[0]):
        chunks[k, :, :cols] = high[:, k * cols : (k + 1) * cols]
        chunks[k, :, cols:] = low[:, k * cols : (k + 1) * cols]
    out = jnp.zeros(partial.shape, f32)
    for k in range(blocks):
        wait(k)
        out = out + jnp.dot(
            high[:, k * span : (k + 1) * span], held[k], preferred_element_type=f32
        )
    partial[...] = out


def expert_kernel(core, own, peer, latent_t, marks_t, weights, keep, send, routed_t, held, sems):
    half = own.shape[1]
    width, rows = latent_t.shape
    quarters, mats, units, _ = weights.shape
    per = 2
    span = per * units
    copies = quarters * mats
    wait = bring(
        lambda k: weights.at[k // mats, k % mats],
        lambda k: held.at[k % mats, pl.ds(k // mats * units, units)],
        sems,
        copies,
    )
    gate = jnp.sum(marks_t[...], axis=0, keepdims=True)
    a = (own[...].astype(f32).T * gate).astype(bf16)
    b = (peer[...].astype(f32).T * gate).astype(bf16)

    @pl.when(core[0] == 0)
    def _():
        routed_t[:half, :] = a
        routed_t[half:, :] = b

    @pl.when(core[0] != 0)
    def _():
        routed_t[:half, :] = b
        routed_t[half:, :] = a

    def over_first(x, w):
        return lax.dot_general(x, w, (((0,), (0,)), ((), ())), preferred_element_type=f32)

    term = jnp.zeros((1, rows), f32)
    block = jnp.zeros((rows, width), f32)
    for k in range(quarters // per):
        for j in range(k * per * mats, (k + 1) * per * mats):
            wait(j)
        at = pl.ds(k * span, span)
        gate_mat, up_mat, out_mat = held[0, at], held[1, at], held[2, at]
        gate_pre = jnp.dot(gate_mat, latent_t[...], preferred_element_type=f32)
        up_pre = jnp.dot(up_mat, latent_t[...], preferred_element_type=f32)
        act_grad = jnp.dot(out_mat, routed_t[...], preferred_element_type=f32)
        sig = 1.0 / (1.0 + jnp.exp(-gate_pre))
        silu = gate_pre * sig
        active = (silu * up_pre).astype(bf16).astype(f32)
        term = term + jnp.sum(act_grad * active, axis=0, keepdims=True)
        gate_back = (act_grad * up_pre * sig * (1.0 + gate_pre * (1.0 - sig))).astype(bf16)
        up_back = (act_grad * silu).astype(bf16)
        block = block + over_first(gate_back, gate_mat) + over_first(up_back, up_mat)

    share = term / jnp.where(gate > 0, gate, 1.0)
    gate_grad = jnp.where(marks_t[...] > 0, share, 0.0).T
    keep[:, half:] = gate_grad
    send[:, half:] = gate_grad.astype(bf16)
    flip = core[0] != 0
    keep[:, :half] = jnp.where(flip, block[:, half:], block[:, :half])
    send[:, :half] = jnp.where(flip, block[:, :half], block[:, half:]).astype(bf16)


def struct(shape, dtype):
    return jax.ShapeDtypeStruct(shape, dtype)


def call(kernel, name, scalar, args, hbm, out_shape, scratch, mib=28, flops=0, choose=None):
    def spec(k, x):
        if k in hbm:
            return pl.BlockSpec(memory_space=pltpu.HBM)
        if choose is not None and k == choose[0]:
            return pl.BlockSpec(*choose[1:])
        return pl.BlockSpec(x.shape, lambda i, core: (0,) * x.ndim)

    def out_spec(x):
        return pl.BlockSpec(x.shape, lambda i, core: (0,) * len(x.shape))

    cost = None
    if flops:
        cost = pl.CostEstimate(flops=flops, bytes_accessed=flops // 512, transcendentals=0)
    args = [
        pltpu.with_memory_space_constraint(x, pltpu.HBM) if k in hbm else x
        for k, x in enumerate(args)
    ]
    return pl.pallas_call(
        kernel,
        grid_spec=pltpu.PrefetchScalarGridSpec(
            num_scalar_prefetch=1,
            grid=(1,),
            in_specs=[spec(k, x) for k, x in enumerate(args)],
            out_specs=[out_spec(x) for x in out_shape],
            scratch_shapes=scratch,
        ),
        out_shape=out_shape,
        compiler_params=pltpu.CompilerParams(vmem_limit_bytes=mib << 20),
        cost_estimate=cost,
        name=name,
    )(scalar, *args)


def block_scratch(blocks, shape):
    return [pltpu.VMEM((blocks,) + shape, bf16), pltpu.SemaphoreType.DMA((blocks,))]


def call_head(core, own, peer, gain, words, target):
    rows = own.shape[0]
    places, _, cols, count = words.shape
    blocks = gain.shape[0]
    return call(
        head_kernel,
        "head",
        core,
        (own, peer, gain, words, target),
        (3,),
        [struct((rows, count), f32), struct((8, 128), f32), struct((rows, 128), f32)],
        block_scratch(blocks, (2 * places // blocks, cols, count)),
    )


def call_loss(core, stats, logits, target, cot, scale, words):
    places, _, cols, count = words.shape
    rows = logits.shape[0]
    return call(
        loss_kernel,
        "loss",
        core,
        (stats, logits, target, cot, scale, words),
        (5,),
        [
            struct((rows, count), bf16),
            struct((rows, places * cols), bf16),
            struct((8, rows), f32),
            struct((rows, 128), f32),
        ],
        block_scratch(4, (places // 4, cols, count)),
    )


def call_keep(core, grad, words):
    places, _, cols, count = words.shape
    rows = grad.shape[0]
    return call(
        keep_kernel,
        "keep",
        core,
        (grad, words),
        (1,),
        [struct((rows, places * cols), f32)],
        block_scratch(4, (places // 4, cols, count)),
        flops=places * cols * rows * count * 2,
    )[0]


def call_lift(core, own, peer, residual, lift):
    wide, width = lift.shape
    return call(
        lift_kernel,
        "lift",
        core,
        (own.astype(f32), peer.astype(f32), residual, lift),
        (3,),
        [struct(residual.shape, bf16)],
        [pltpu.VMEM((own.shape[0], width), f32)] + block_scratch(4, (wide // 4, width)),
    )[0]


def call_lower(place, parts, hidden, gain, marks, lift):
    places, chunk, wide = parts.shape
    width = lift.shape[1]
    return call(
        lower_kernel,
        "lower",
        place,
        (parts, hidden, gain, marks, lift),
        (4,),
        [struct((places, chunk, 2 * (wide // places)), bf16), struct((chunk, width), f32)],
        block_scratch(4, (wide // 4, width)),
        choose=(3, (chunk, 128), lambda i, place: (place[0], 0)),
    )


def call_expert(core, own, peer, latent_t, marks_t, weights):
    width, rows = latent_t.shape
    quarters, mats, units, _ = weights.shape
    lanes = own.shape[1] + marks_t.shape[0]
    return call(
        expert_kernel,
        "expert",
        core,
        (own, peer, latent_t, marks_t, weights),
        (4,),
        [struct((rows, lanes), f32), struct((rows, lanes), bf16)],
        [
            pltpu.VMEM((width, rows), bf16),
            pltpu.VMEM((mats, quarters * units, width), bf16),
            pltpu.SemaphoreType.DMA((quarters * mats,)),
        ],
    )


def on_device(
    latent,
    residual,
    gates,
    route_ids,
    w_gate,
    w_up,
    w_out,
    w_lift,
    norm_gain,
    w_vocab,
    targets,
    loss_cot,
):
    core = lax.axis_index("c")
    own_index = lax.axis_index(slab)
    place = lax.axis_index(plane)
    places = lax.axis_size(plane)
    groups = lax.axis_size("dp")
    rows, width = latent.shape
    half = width // 2
    cols = residual.shape[1]
    words = w_vocab.shape[1]
    chunk = rows // places
    wide = places * cols
    first = core == 0

    def mine(x, axis):
        a, b = jnp.split(x, 2, axis)
        return jnp.where(first, a, b)

    def other(x, axis):
        a, b = jnp.split(x, 2, axis)
        return jnp.where(first, b, a)

    def joined(own, peer, axis):
        return jnp.where(
            first,
            jnp.concatenate([own, peer], axis),
            jnp.concatenate([peer, own], axis),
        )

    gate_mat, up_mat, out_mat = w_gate[0], w_up[0], w_out[0]
    lift_wide = lax.all_gather(w_lift.T, plane, axis=0, tiled=True)

    gate_marks = jnp.where(route_ids.T == own_index, gates.T, 0.0)
    gate_own = jnp.sum(gate_marks, axis=0)
    high = lax.reduce_precision(gate_own, 8, 7)
    middle = lax.reduce_precision(gate_own - high, 8, 7)
    low = gate_own - high - middle
    gate_rows = jnp.concatenate([high, middle, low, jnp.zeros_like(low)]).reshape(-1, half)
    extra = jnp.pad(gate_rows.astype(bf16), ((0, 16 - gate_rows.shape[0]), (0, 0)))
    out_keep = mine(out_mat, 1)
    out_peer = swap(other(out_mat, 1))

    lat_own = spread(jnp.concatenate([mine(latent, 1), extra]), "dp")
    lat_peer = swap(lat_own)

    def gate_of(x):
        parts = x[:, rows : rows + gate_rows.shape[0]].reshape(groups, -1).astype(f32)
        parts = parts.reshape(groups, -1, rows)
        return (parts[:, 0] + parts[:, 1] + parts[:, 2]).reshape(-1)

    gate_all, gate_peer = gate_of(lat_own), gate_of(lat_peer)
    lat_all = joined(lat_own[:, :rows], lat_peer[:, :rows], 2).reshape(-1, width)
    gate_part = dot(lat_all, gate_mat, 1, 0)
    up_part = dot(lat_all, up_mat, 1, 0)
    active = (jax.nn.silu(gate_part) * up_part).astype(bf16)
    active_peer = swap(active)
    part = dot(active, out_keep, 1, 0) * gate_all[:, None]
    part = part + dot(active_peer, out_peer, 1, 0) * gate_peer[:, None]
    part, gate_mat, up_mat, out_mat = lax.optimization_barrier((part, gate_mat, up_mat, out_mat))
    summed = jnp.sum(deal(part, "dp").reshape(groups, rows, half), axis=0)

    summed = summed.reshape(places, chunk, half)
    carried = residual.reshape(places, chunk, cols).astype(f32)
    carried = jnp.pad(carried, ((0, 0), (0, 0), (0, 128 - cols)))
    dealt = deal(jnp.concatenate([summed, carried], axis=2), plane)
    comb_own = jnp.sum(dealt[:, :, :half], axis=0).astype(bf16)
    res_rows = dealt[:, :, half : half + cols].transpose(1, 0, 2).reshape(chunk, wide)
    weights = lax.all_gather(jnp.stack([gate_mat.T, up_mat.T, out_mat]), "dp")

    core_id = core.astype(jnp.int32)[None]
    hidden = call_lift(core_id, comb_own, swap(comb_own), res_rows, lift_wide)
    hid_own = spread(hidden, plane).reshape(rows, wide)

    steps = 2
    gain_sides = norm_gain.astype(f32).reshape(places, 2, cols)
    gain_own = jnp.where(first, gain_sides[:, 0], gain_sides[:, 1]).reshape(steps, -1)
    gain_peer = jnp.where(first, gain_sides[:, 1], gain_sides[:, 0]).reshape(steps, -1)
    target = (targets - own_index * words)[:, None]
    vocab = w_vocab.reshape(places, 2, cols, words)
    logits, stats, scale = call_head(
        core_id, hid_own, swap(hid_own), jnp.concatenate([gain_own, gain_peer]), vocab, target
    )
    stats_all = spread(stats, slab)
    grad, send, loss, marks = call_loss(
        core_id, stats_all, logits, target, loss_cot[None], scale, vocab
    )
    row_loss = loss[0]
    keep = call_keep(core_id, grad, vocab)
    keep = (keep + swap(send).astype(f32)).astype(bf16)
    parts = deal(keep.reshape(places, chunk, wide), plane)
    chunks, partial = call_lower(
        place.astype(jnp.int32)[None], parts, hidden, gain_own.reshape(1, wide), marks, lift_wide
    )
    cg_rows = (mine(partial, 1) + swap(other(partial, 1))).astype(bf16)
    cg_rows = jnp.broadcast_to(cg_rows[None], (places, chunk, half))
    dealt = deal(jnp.concatenate([cg_rows, chunks], axis=2), plane)
    cg_own = dealt[:, :, :half].reshape(rows, half)
    d_residual = dealt[:, :, half : half + cols].astype(f32) + dealt[:, :, half + cols :].astype(f32)
    d_residual = d_residual.reshape(rows, cols)

    gate_marks = jnp.pad(gate_marks, ((0, 128 - gate_marks.shape[0]), (0, 0)))
    keep, send = call_expert(core_id, cg_own, swap(cg_own), latent.T, gate_marks, weights)
    keep = (keep + swap(send).astype(f32)).astype(bf16)
    tail = jnp.sum(deal(keep, plane).astype(f32).reshape(places, chunk, -1), axis=0).astype(bf16)
    tail = spread(tail, plane).reshape(rows, -1)
    d_latent = joined(tail[:, :half], swap(tail[:, :half]), 1).astype(f32)
    d_gates = tail[:, half : half + gates.shape[1]].astype(f32)
    return (row_loss, d_residual, d_latent, d_gates)


def solution(mesh):
    fine = Mesh(mesh.devices.reshape(mesh.devices.shape[0], 8, 4, 2), ("dp", "z", "y", "c"))
    in_specs = (
        P("dp", None),
        P("dp", slab),
        P("dp", None),
        P("dp", None),
        P(slab, None, "dp"),
        P(slab, None, "dp"),
        P(slab, "dp", None),
        P(None, slab),
        P(),
        P(None, slab),
        P("dp"),
        P("dp"),
    )
    out_specs = (P("dp"), P("dp", slab), P("dp", None), P("dp", None))
    return jax.shard_map(
        on_device, mesh=fine, in_specs=in_specs, out_specs=out_specs, check_vma=False
    )
```

time: 332 us -> 300 us (0.904)
  matrix products: 37 us -> 8.27 us
  Pallas kernels: 0 us -> 27.4 us
  blocking collectives: 153 us -> 138 us
  other arithmetic: 14.1 us -> 7.26 us
  starting transfers between devices: 33.4 us -> 28.5 us
    pallas_call x0 -> x6, Pallas kernels: none -> 27.4 us  [call(): pl.pallas_call(kernel, grid_spec=pltpu.PrefetchScalarGridSpec(num_scalar_...]
    dot_general x7 -> x0, matrix products: 22 us -> none  [the longest x1 6.82 us: on_device(): jnp.einsum('qtf,qlf->tl', gate_back, gate_full, preferred_element_type=f32)]
    all_to_all x8 -> x6, blocking collectives: 153 us -> 138 us  [deal(): return lax.all_to_all(x, axes, 0, 0, tiled=True)]
    all_to_all x3, waiting for transfers between devices: 56 us -> 63.7 us  [deal(): return lax.all_to_all(x, axes, 0, 0, tiled=True)]
    convert_element_type x6 -> x5, other arithmetic: 7.71 us -> 0.03 us  [the longest x2 0.01 us: gate_of(): parts = x[:, rows:rows + gate_rows.shape[0]].reshape(groups, -1).astype(f32)]
    dot_general x5 -> x4, matrix products: 15 us -> 8.27 us  [dot(): lax.dot_general(a, b, (((ca,), (cb,)), ((), ())), preferred_element_type=...]
    dot_general x1 -> x0, local copies, waits for them, and re-layouts: 5.63 us -> none  [dot(): lax.dot_general(a, b, (((ca,), (cb,)), ((), ())), preferred_element_type=...]
    ppermute x10, waiting for transfers between devices: 11.7 us -> 6.64 us  [swap(): return lax.ppermute(x, 'c', [(0, 1), (1, 0)])]
  transfers between devices with their start and end apart: 16 -> 15, of which waited for: 11 -> 10; matrix products, arithmetic and copies ran while one was open for 10% -> 6% of each run, Pallas kernels for 0% -> 6%
where the time goes in v6:
time: 300 us; the launch traced here: 299 us
  blocking collectives  138 us (46%)
  waiting for transfers between devices  71.1 us (24%)
  starting transfers between devices  28.5 us (10%)
  Pallas kernels  27.4 us (9%)
  between operations  14.5 us (5%)
  matrix products  8.27 us (3%)
  other arithmetic  7.26 us (2%)
  local copies, waits for them, and re-layouts  4.68 us (2%)
    all_to_all x6, blocking collectives, deal(): return lax.all_to_all(x, axes, 0, 0, tiled=True)  138 us
    all_to_all x3, waiting for transfers between devices, deal(): return lax.all_to_all(x, axes, 0, 0, tiled=True)  63.7 us
    pallas_call x6, Pallas kernels, call(): pl.pallas_call(kernel, grid_spec=pltpu.PrefetchScalarGridSpec(num_scalar_...  27.4 us
    ppermute x10, starting transfers between devices, swap(): return lax.ppermute(x, 'c', [(0, 1), (1, 0)])  16 us
    all_to_all x3, starting transfers between devices, deal(): return lax.all_to_all(x, axes, 0, 0, tiled=True)  12.4 us
    dot_general x4, matrix products, dot(): lax.dot_general(a, b, (((ca,), (cb,)), ((), ())), preferred_element_type=...  8.27 us
    ppermute x10, waiting for transfers between devices, swap(): return lax.ppermute(x, 'c', [(0, 1), (1, 0)])  6.64 us
  transfers between devices with their start and end apart: 15, of which 10 were waited for; matrix products, arithmetic and copies ran while one was open for 6% of the time, Pallas kernels for 6%

profile of v6, /device:TPU:1, one launch (start us, length us, event | category | flops | bytes accessed | tf_op | source)
XLA Modules:
  0.0 299.4 jit_solution(13931362652359018475)
XLA Ops:
  7.2 0.7 all-gather.4.cloned.1.call-update
  8.0 0.8 fusion.13
  8.8 1.1 slice_select_fusion
  9.9 0.1 broadcast_in_dim.52
  10.0 19.3 %all_to_all.53 = bf16[4,272,512]{2,1,0:T(8,128)(2,1)S(1)} all-to-all(bf16[4,272,512]{2,1,0:T(8,128)(2,1)S(1)} %broadcast_in_dim.52), channel_id=1, replica_groups=mesh['dp'=4,'z'=8,'y'=4,'c'=2] {'dp'}, dimensions={0} | all-to-all | bytes 2228224 | tf_op jit(solution)/shard_map/all_to_all | solution.py:24
  29.3 2.2 collective-permute-start
  31.6 0.1 collective-permute-start.2
  31.7 0.1 slice.83
  31.8 2.3 collective-permute-done
  34.1 0.1 slice.84
  34.2 1.2 fusion.4
  35.5 2.0 multiply_convert_fusion
  37.5 0.4 collective-permute-start.1
  37.9 1.9 fusion.5
  39.8 3.2 %multiply_add_fusion = f32[1024,512]{1,0:T(8,128)} fusion(f32[1024,512]{1,0:T(8,128)S(1)} %fusion.5, bf16[1024,336]{0,1:T(8,128)(2,1)S(1)} %collective-permute-done.1, bf16[336,512]{1,0:T(8,128)(2,1)} %collective-permute-done.2, f32[1024]{0:T(1024)S(1)} %bitcast.71, f32[1024]{0:T(1024)S(1)} %bitcast.70), kind=kOutput, calls=%fused_computation.2 | convolution fusion | flops 353894400 | bytes 5234688 | tf_op jit(solution)/shard_map/dot_general | solution.py:16
  43.0 1.5 pad_maximum_fusion
  44.6 3.6 %all-to-all-start.1 = ((f32[4,256,512]{2,1,0:T(8,128)}), f32[4,256,512]{2,1,0:T(8,128)S(1)}, u32[]{:S(2)}, u32[]{:S(2)}) async-start(f32[4,256,512]{2,1,0:T(8,128)} %bitcast.8), calls=%async_computation.1 | async-start | bytes 4194304 | tf_op jit(solution)/shard_map/all_to_all | solution.py:24
  48.2 0.1 copy.27
  48.3 25.9 %all-to-all-done.1 = f32[4,256,512]{2,1,0:T(8,128)S(1)} async-done(((f32[4,256,512]{2,1,0:T(8,128)}), f32[4,256,512]{2,1,0:T(8,128)S(1)}, u32[]{:S(2)}, u32[]{:S(2)}) %all-to-all-start.1) | async-done | bytes 2097184 | tf_op jit(solution)/shard_map/all_to_all | solution.py:24
  74.2 0.2 reduce_sum.40
  74.5 32.9 %all_to_all.54 = f32[32,8,640]{2,1,0:T(8,128)S(1)} all-to-all(f32[32,8,640]{2,1,0:T(8,128)S(1)} %pad_maximum_fusion.1), channel_id=1, replica_groups=mesh['dp'=4,'z'=8,'y'=4,'c'=2] {'z','y'}, dimensions={0} | all-to-all | bytes 1310720 | tf_op jit(solution)/shard_map/all_to_all | solution.py:24
  107.5 1.6 collective-permute-start.3
  109.2 0.1 reshape.134.residual
  109.3 0.7 collective-permute-done.3
  109.9 2.8 lift.1.hidden
  112.8 0.1 broadcast_in_dim.53
  112.9 32.3 %all_to_all.55 = bf16[32,8,2048]{2,1,0:T(8,128)(2,1)S(1)} all-to-all(bf16[32,8,2048]{2,1,0:T(8,128)(2,1)S(1)} %broadcast_in_dim.53), channel_id=1, replica_groups=mesh['dp'=4,'z'=8,'y'=4,'c'=2] {'z','y'}, dimensions={0} | all-to-all | bytes 2097152 | tf_op jit(solution)/shard_map/all_to_all | solution.py:24
  145.2 2.6 collective-permute-start.4
  147.8 0.1 reshape.146
  147.9 0.5 broadcast.45
  148.4 0.7 fusion.20
  149.2 0.1 select_n.98
  149.2 0.1 select_n.96
  149.3 0.1 copy.29.target
  149.5 0.6 collective-permute-done.4.peer
  150.1 5.2 %head.1 = (f32[256,1024]{1,0:T(8,128)S(1)}, f32[8,128]{1,0:T(8,128)S(1)}, f32[256,128]{1,0:T(8,128)S(1)}) custom-call(s32[1]{0:T(128)} %bitcast.core, bf16[256,2048]{1,0:T(8,128)(2,1)S(1)} %bitcast.49, bf16[256,2048]{1,0:T(8,128)(2,1)S(1)} %collective-permute-done.4.peer, f32[4,1024]{1,0:T(4,128)S(1)} %pad_maximum_fusion.3.gain, ...), custom_call_target="tpu_custom_call" | custom-call | tf_op jit(solution)/shard_map/head/pallas_call | solution.py:264
  155.3 19.1 %all_to_all.56.stats = f32[64,8,128]{2,1,0:T(8,128)S(1)} all-to-all(f32[64,8,128]{2,1,0:T(8,128)S(1)} %broadcast_in_dim.55), channel_id=1, replica_groups=mesh['dp'=4,'z'=8,'y'=4,'c'=2] {'z','y','c'}, dimensions={0} | all-to-all | bytes 524288 | tf_op jit(solution)/shard_map/all_to_all | solution.py:24
  174.4 3.7 %loss.1 = (bf16[256,1024]{1,0:T(8,128)(2,1)S(1)}, bf16[256,2048]{1,0:T(8,128)(2,1)S(1)}, f32[8,256]{1,0:T(8,128)S(1)}, f32[256,128]{1,0:T(8,128)S(1)}) custom-call(s32[1]{0:T(128)} %bitcast.core, f32[64,8,128]{2,1,0:T(8,128)S(1)} %all_to_all.56.stats, f32[256,1024]{1,0:T(8,128)S(1)} %get-tuple-element.21.logits, s32[256,1]{1,0:T(8,128)S(1)} %copy.29.target, ...), custom_call_target="tpu_custom_call" | custom-call | tf_op jit(solution)/shard_map/loss/pallas_call | solution.py:264
  178.1 0.3 collective-permute-start.5
  178.4 3.1 %keep.1 = f32[256,2048]{1,0:T(8,128)S(1)} custom-call(s32[1]{0:T(128)} %bitcast.core, bf16[256,1024]{1,0:T(8,128)(2,1)S(1)} %get-tuple-element.24.grad, bf16[32,2,64,1024]{3,2,1,0:T(8,128)(2,1)} %bitcast.54), custom_call_target="tpu_custom_call" | custom-call | flops 1073741824 | bytes 2097152 | tf_op jit(solution)/shard_map/keep/pallas_call | solution.py:264
  181.6 1.3 fusion
  182.9 4.0 %all-to-all-start.5 = ((bf16[32,8,2048]{2,1,0:T(8,128)(2,1)}), bf16[32,8,2048]{2,1,0:T(8,128)(2,1)S(1)}, u32[]{:S(2)}, u32[]{:S(2)}) async-start(bf16[32,8,2048]{2,1,0:T(8,128)(2,1)} %fusion), calls=%async_computation.5 | async-start | bytes 2097152 | tf_op jit(solution)/shard_map/all_to_all | solution.py:24
  186.9 0.1 select_n.100.gain
  187.0 27.2 %all-to-all-done.5.parts = bf16[32,8,2048]{2,1,0:T(8,128)(2,1)S(1)} async-done(((bf16[32,8,2048]{2,1,0:T(8,128)(2,1)}), bf16[32,8,2048]{2,1,0:T(8,128)(2,1)S(1)}, u32[]{:S(2)}, u32[]{:S(2)}) %all-to-all-start.5) | async-done | bytes 1048608 | tf_op jit(solution)/shard_map/all_to_all | solution.py:24
  214.1 2.6 lower.1
  216.8 1.8 collective-permute-start.6
  218.7 0.8 collective-permute-done.6
  219.6 17.9 %all_to_all.57 = bf16[32,8,640]{2,1,0:T(8,128)(2,1)S(1)} all-to-all(bf16[32,8,640]{2,1,0:T(8,128)(2,1)S(1)} %pad_maximum_fusion.2), channel_id=1, replica_groups=mesh['dp'=4,'z'=8,'y'=4,'c'=2] {'z','y'}, dimensions={0} | all-to-all | bytes 655360 | tf_op jit(solution)/shard_map/all_to_all | solution.py:24
  237.5 2.7 collective-permute-start.7
  240.2 0.2 copy.31
  240.4 0.9 collective-permute-done.7.peer
  241.3 9.9 %expert.1 = (f32[256,640]{1,0:T(8,128)S(1)}, bf16[256,640]{1,0:T(8,128)(2,1)S(1)}) custom-call(s32[1]{0:T(128)} %bitcast.core, bf16[256,512]{1,0:T(8,128)(2,1)S(1)} %slice_bitcast_fusion.own, bf16[256,512]{1,0:T(8,128)(2,1)S(1)} %collective-permute-done.7.peer, bf16[1024,256]{1,0:T(8,128)(2,1)S(1)} %bitcast.50, f32[128,256]{1,0:T(8,128)S(1)} %pad.18.marks_t, ...), custom_call_target="tpu_custom_call" | custom-call | tf_op jit(solution)/shard_map/expert/pallas_call | solution.py:264
  251.2 0.5 collective-permute-start.8
  251.7 1.3 collective-permute-done.8
  253.0 16.3 %all_to_all.58 = bf16[32,8,640]{2,1,0:T(8,128)(2,1)S(1)} all-to-all(bf16[32,8,640]{2,1,0:T(8,128)(2,1)S(1)} %fusion.8), channel_id=1, replica_groups=mesh['dp'=4,'z'=8,'y'=4,'c'=2] {'z','y'}, dimensions={0} | all-to-all | bytes 655360 | tf_op jit(solution)/shard_map/all_to_all | solution.py:24
  269.3 0.8 broadcast_in_dim.59
  270.1 4.8 %all-to-all-start.8 = ((bf16[32,8,640]{2,1,0:T(8,128)(2,1)}), bf16[32,8,640]{2,1,0:T(8,128)(2,1)S(1)}, u32[]{:S(2)}, u32[]{:S(2)}) async-start(bf16[32,8,640]{2,1,0:T(8,128)(2,1)} %broadcast_in_dim.59), calls=%async_computation.8 | async-start | bytes 655360 | tf_op jit(solution)/shard_map/all_to_all | solution.py:24
  274.9 0.6 slice.77
  275.4 10.7 %all-to-all-done.8 = bf16[32,8,640]{2,1,0:T(8,128)(2,1)S(1)} async-done(((bf16[32,8,640]{2,1,0:T(8,128)(2,1)}), bf16[32,8,640]{2,1,0:T(8,128)(2,1)S(1)}, u32[]{:S(2)}, u32[]{:S(2)}) %all-to-all-start.8) | async-done | bytes 327712 | tf_op jit(solution)/shard_map/all_to_all | solution.py:24
  286.1 3.8 %collective-permute-start.9 = (bf16[256,512]{1,0:T(8,128)(2,1)S(1)}, bf16[256,512]{1,0:T(8,128)(2,1)S(1)}, u32[]{:S(2)}, u32[]{:S(2)}) collective-permute-start(bf16[256,512]{1,0:T(8,128)(2,1)S(1)} %slice.100), channel_id=1, source_target_pairs={{0,1},{1,0},{2,3},{3,2},{4,5},{5,4},{6,7},{7,6},{8,9},{9,8},{10,11... | collective-permute-start | bytes 786440 | tf_op jit(solution)/shard_map/ppermute | solution.py:20
  289.9 0.1 add_bitcast_fusion
  290.0 0.7 copy.32
  290.7 0.7 copy.33
  291.4 1.1 fusion.2
  (61 shorter events, 0.9 us)
Async XLA Ops:
  7.2 102.8 %all-gather.4.cloned.1.call-start = ((), (), s32[]{:S(2)}) async-start(), calls=%async_computation.9 | async-start | bytes 4325376 | tf_op jit(solution)/shard_map/all_gather | solution.py:423
  7.9 232.5 %all-gather.6.cloned.1.call-start = ((), (), s32[]{:S(2)}) async-start(), calls=%async_computation.10 | async-start | bytes 10321920 | tf_op jit(solution)/shard_map/all_gather | solution.py:460
  9.9 21.7 %copy-start.1 = (bf16[1,336,1024]{2,1,0:T(8,128)(2,1)S(1)}, bf16[1,336,1024]{2,1,0:T(8,128)(2,1)}, u32[]{:S(2)}) copy-start(bf16[1,336,1024]{2,1,0:T(8,128)(2,1)} %param.18) | copy-start | bytes 2064388
  29.3 4.8 %collective-permute-start = (bf16[4,272,512]{2,1,0:T(8,128)(2,1)S(1)}, bf16[4,272,512]{2,1,0:T(8,128)(2,1)S(1)}, u32[]{:S(2)}, u32[]{:S(2)}) collective-permute-start(bf16[4,272,512]{2,1,0:T(8,128)(2,1)S(1)} %all_to_all.53), channel_id=1, source_target_pairs={{0,1},{1,0},{2,3},{3,2},{4,5},{5,4},{6,7},{7,6},{8,9},{9,8},{10,11... | collective-permute-start | bytes 3342344 | tf_op jit(solution)/shard_map/ppermute | solution.py:20
  31.6 8.2 %collective-permute-start.2 = (bf16[336,512]{1,0:T(8,128)(2,1)S(1)}, bf16[336,512]{1,0:T(8,128)(2,1)}, u32[]{:S(2)}, u32[]{:S(2)}) collective-permute-start(bf16[336,512]{1,0:T(8,128)(2,1)S(1)} %broadcast_select_fusion), channel_id=1, source_target_pairs={{0,1},{1,0},{2,3},{3,2},{4,5},{5,4},{6,7},{7,6},{8,9},{9,8},{10,11... | collective-permute-start | bytes 1032200 | tf_op jit(solution)/shard_map/ppermute | solution.py:20
  31.7 2.5 copy-start.3
  34.2 1.2 copy-start.5
  37.5 2.4 collective-permute-start.1
  39.8 3.2 %copy-start.4 = (bf16[1,1024,336]{1,2,0:T(8,128)(2,1)S(1)}, bf16[1,1024,336]{1,2,0:T(8,128)(2,1)}, u32[]{:S(2)}) copy-start(bf16[1,1024,336]{1,2,0:T(8,128)(2,1)} %param.16) | copy-start | bytes 2064388
  39.8 3.2 %copy-start.6 = (bf16[1,1024,336]{1,2,0:T(8,128)(2,1)S(1)}, bf16[1,1024,336]{1,2,0:T(8,128)(2,1)}, u32[]{:S(2)}) copy-start(bf16[1,1024,336]{1,2,0:T(8,128)(2,1)} %param.17) | copy-start | bytes 2064388
  44.6 3.6 %copy-start.7 = (bf16[256,64]{0,1:T(8,128)(2,1)S(1)}, bf16[256,64]{0,1:T(8,128)(2,1)}, u32[]{:S(2)}) copy-start(bf16[256,64]{0,1:T(8,128)(2,1)} %param.13) | copy-start | bytes 98308
  44.6 29.7 %all-to-all-start.1 = ((f32[4,256,512]{2,1,0:T(8,128)}), f32[4,256,512]{2,1,0:T(8,128)S(1)}, u32[]{:S(2)}, u32[]{:S(2)}) async-start(f32[4,256,512]{2,1,0:T(8,128)} %bitcast.8), calls=%async_computation.1 | async-start | bytes 4194304 | tf_op jit(solution)/shard_map/all_to_all | solution.py:24
  107.5 2.4 collective-permute-start.3
  112.8 35.0 %copy-start.8 = (bf16[4096]{0:T(1024)(128)(2,1)S(1)}, bf16[4096]{0:T(1024)(128)(2,1)}, u32[]{:S(2)}) copy-start(bf16[4096]{0:T(1024)(128)(2,1)} %param.20) | copy-start | bytes 24580
  112.8 36.5 %copy-start.9 = (s32[256]{0:T(256)S(1)}, s32[256]{0:T(256)}, u32[]{:S(2)}) copy-start(s32[256]{0:T(256)} %param.22) | copy-start | bytes 3076
  145.2 4.9 %collective-permute-start.4 = (bf16[256,2048]{1,0:T(8,128)(2,1)S(1)}, bf16[256,2048]{1,0:T(8,128)(2,1)S(1)}, u32[]{:S(2)}, u32[]{:S(2)}) collective-permute-start(bf16[256,2048]{1,0:T(8,128)(2,1)S(1)} %bitcast.48), channel_id=1, source_target_pairs={{0,1},{1,0},{2,3},{3,2},{4,5},{5,4},{6,7},{7,6},{8,9},{9,8},{10,11... | collective-permute-start | bytes 3145736 | tf_op jit(solution)/shard_map/ppermute | solution.py:20
  150.1 24.3 %copy-start = (f32[256]{0:T(256)S(1)}, f32[256]{0:T(256)}, u32[]{:S(2)}) copy-start(f32[256]{0:T(256)} %param.23) | copy-start | bytes 3076
  178.1 3.5 %collective-permute-start.5 = (bf16[256,2048]{1,0:T(8,128)(2,1)S(1)}, bf16[256,2048]{1,0:T(8,128)(2,1)S(1)}, u32[]{:S(2)}, u32[]{:S(2)}) collective-permute-start(bf16[256,2048]{1,0:T(8,128)(2,1)S(1)} %get-tuple-element.25), channel_id=1, source_target_pairs={{0,1},{1,0},{2,3},{3,2},{4,5},{5,4},{6,7},{7,6},{8,9},{9,8},{10,11... | collective-permute-start | bytes 3145736 | tf_op jit(solution)/shard_map/ppermute | solution.py:20
  182.9 31.3 %all-to-all-start.5 = ((bf16[32,8,2048]{2,1,0:T(8,128)(2,1)}), bf16[32,8,2048]{2,1,0:T(8,128)(2,1)S(1)}, u32[]{:S(2)}, u32[]{:S(2)}) async-start(bf16[32,8,2048]{2,1,0:T(8,128)(2,1)} %fusion), calls=%async_computation.5 | async-start | bytes 2097152 | tf_op jit(solution)/shard_map/all_to_all | solution.py:24
  216.8 23.4 %copy-start.2 = (bf16[256,1024]{1,0:T(8,128)(2,1)S(1)}, bf16[256,1024]{1,0:T(8,128)(2,1)}, u32[]{:S(2)}) copy-start(bf16[256,1024]{1,0:T(8,128)(2,1)} %param.12) | copy-start | bytes 1572868
  216.8 2.7 collective-permute-start.6
  237.5 3.9 %collective-permute-start.7 = (bf16[256,512]{1,0:T(8,128)(2,1)S(1)}, bf16[256,512]{1,0:T(8,128)(2,1)S(1)}, u32[]{:S(2)}, u32[]{:S(2)}) collective-permute-start(bf16[256,512]{1,0:T(8,128)(2,1)S(1)} %slice_bitcast_fusion.own), channel_id=1, source_target_pairs={{0,1},{1,0},{2,3},{3,2},{4,5},{5,4},{6,7},{7,6},{8,9},{9,8},{10,11... | collective-permute-start | bytes 786440 | tf_op jit(solution)/shard_map/ppermute | solution.py:20
  251.2 1.7 collective-permute-start.8
  270.1 16.0 %all-to-all-start.8 = ((bf16[32,8,640]{2,1,0:T(8,128)(2,1)}), bf16[32,8,640]{2,1,0:T(8,128)(2,1)S(1)}, u32[]{:S(2)}, u32[]{:S(2)}) async-start(bf16[32,8,640]{2,1,0:T(8,128)(2,1)} %broadcast_in_dim.59), calls=%async_computation.8 | async-start | bytes 655360 | tf_op jit(solution)/shard_map/all_to_all | solution.py:24
  286.1 5.3 %collective-permute-start.9 = (bf16[256,512]{1,0:T(8,128)(2,1)S(1)}, bf16[256,512]{1,0:T(8,128)(2,1)S(1)}, u32[]{:S(2)}, u32[]{:S(2)}) collective-permute-start(bf16[256,512]{1,0:T(8,128)(2,1)S(1)} %slice.100), channel_id=1, source_target_pairs={{0,1},{1,0},{2,3},{3,2},{4,5},{5,4},{6,7},{7,6},{8,9},{9,8},{10,11... | collective-permute-start | bytes 786440 | tf_op jit(solution)/shard_map/ppermute | solution.py:20
Sparse Core Ops, SparseCore 0:
  10.6 90.3 all-gather.3
  102.8 87.0 all-gather.5

commit v7 on v6

--- a/solution.py
+++ b/solution.py
@@ -182,19 +182,39 @@
     partial[...] = out
 
 
-def expert_kernel(core, own, peer, latent_t, marks_t, weights, keep, send, routed_t, held, sems):
+def unit_blocks(weights, mats, held, sems):
+    quarters, _, units, _ = weights.shape
+    many = len(mats)
+    return bring(
+        lambda k: weights.at[k // many, mats[k % many]],
+        lambda k: held.at[k % many, pl.ds(k // many * units, units)],
+        sems,
+        quarters * many,
+    )
+
+
+def prepare_kernel(core, latent_t, weights, slope, silu, active, held, sems):
+    wait = unit_blocks(weights, (0, 1), held, sems)
+    span = weights.shape[2] * 2
+    for k in range(2):
+        for j in range(4 * k, 4 * k + 4):
+            wait(j)
+        at = pl.ds(k * span, span)
+        gate_pre = jnp.dot(held[0, at], latent_t[...], preferred_element_type=f32)
+        up_pre = jnp.dot(held[1, at], latent_t[...], preferred_element_type=f32)
+        sig = 1.0 / (1.0 + jnp.exp(-gate_pre))
+        silu[at, :] = gate_pre * sig
+        slope[at, :] = up_pre * sig * (1.0 + gate_pre * (1.0 - sig))
+        active[at, :] = (gate_pre * sig * up_pre).astype(bf16)
+
+
+def expert_kernel(
+    core, own, peer, slope, silu, active, marks_t, weights, keep, send, routed_t, held, sems
+):
     half = own.shape[1]
-    width, rows = latent_t.shape
-    quarters, mats, units, _ = weights.shape
-    per = 2
-    span = per * units
-    copies = quarters * mats
-    wait = bring(
-        lambda k: weights.at[k // mats, k % mats],
-        lambda k: held.at[k % mats, pl.ds(k // mats * units, units)],
-        sems,
-        copies,
-    )
+    width, rows = routed_t.shape
+    span = weights.shape[2] * 2
+    wait = unit_blocks(weights, (2, 0, 1), held, sems)
     gate = jnp.sum(marks_t[...], axis=0, keepdims=True)
     a = (own[...].astype(f32).T * gate).astype(bf16)
     b = (peer[...].astype(f32).T * gate).astype(bf16)
@@ -214,21 +234,15 @@
 
     term = jnp.zeros((1, rows), f32)
     block = jnp.zeros((rows, width), f32)
-    for k in range(quarters // per):
-        for j in range(k * per * mats, (k + 1) * per * mats):
+    for k in range(2):
+        for j in range(6 * k, 6 * k + 6):
             wait(j)
         at = pl.ds(k * span, span)
-        gate_mat, up_mat, out_mat = held[0, at], held[1, at], held[2, at]
-        gate_pre = jnp.dot(gate_mat, latent_t[...], preferred_element_type=f32)
-        up_pre = jnp.dot(up_mat, latent_t[...], preferred_element_type=f32)
-        act_grad = jnp.dot(out_mat, routed_t[...], preferred_element_type=f32)
-        sig = 1.0 / (1.0 + jnp.exp(-gate_pre))
-        silu = gate_pre * sig
-        active = (silu * up_pre).astype(bf16).astype(f32)
-        term = term + jnp.sum(act_grad * active, axis=0, keepdims=True)
-        gate_back = (act_grad * up_pre * sig * (1.0 + gate_pre * (1.0 - sig))).astype(bf16)
-        up_back = (act_grad * silu).astype(bf16)
-        block = block + over_first(gate_back, gate_mat) + over_first(up_back, up_mat)
+        act_grad = jnp.dot(held[0, at], routed_t[...], preferred_element_type=f32)
+        term = term + jnp.sum(act_grad * active[at, :].astype(f32), axis=0, keepdims=True)
+        gate_back = (act_grad * slope[at, :]).astype(bf16)
+        up_back = (act_grad * silu[at, :]).astype(bf16)
+        block = block + over_first(gate_back, held[1, at]) + over_first(up_back, held[2, at])
 
     share = term / jnp.where(gate > 0, gate, 1.0)
     gate_grad = jnp.where(marks_t[...] > 0, share, 0.0).T
@@ -237,6 +251,24 @@
     flip = core[0] != 0
     keep[:, :half] = jnp.where(flip, block[:, half:], block[:, :half])
     send[:, :half] = jnp.where(flip, block[:, :half], block[:, half:]).astype(bf16)
+
+
+def mix_kernel(spot, own, peer, keep, other, gates, out):
+    groups = gates.shape[0] // 2
+    rows = gates.shape[1]
+    row = lax.broadcasted_iota(jnp.int32, (128, rows), 0)
+
+    def over_first(x, w):
+        return lax.dot_general(x, w, (((0,), (0,)), ((), ())), preferred_element_type=f32)
+
+    for k in range(groups):
+        at = slice(k * rows, (k + 1) * rows)
+        back = lax.rem(spot[1] + groups - k, groups)
+        gate = gates[pl.ds(back, 1), :]
+        gate_peer = gates[pl.ds(groups + back, 1), :]
+        col = jnp.where(row == 0, gate, gate_peer).T
+        part = over_first(own[:, at], keep[...]) * col[:, 0:1]
+        out[at, :] = part + over_first(peer[:, at], other[...]) * col[:, 1:2]
 
 
 def struct(shape, dtype):
@@ -358,23 +390,49 @@
     )
 
 
-def call_expert(core, own, peer, latent_t, marks_t, weights):
+def unit_scratch(weights, mats):
+    quarters, _, units, width = weights.shape
+    return [
+        pltpu.VMEM((mats, quarters * units, width), bf16),
+        pltpu.SemaphoreType.DMA((quarters * mats,)),
+    ]
+
+
+def call_prepare(core, latent_t, weights):
     width, rows = latent_t.shape
-    quarters, mats, units, _ = weights.shape
-    lanes = own.shape[1] + marks_t.shape[0]
+    quarters, _, units, _ = weights.shape
+    shape = (quarters * units, rows)
+    return call(
+        prepare_kernel,
+        "prepare",
+        core,
+        (latent_t, weights),
+        (1,),
+        [struct(shape, f32), struct(shape, f32), struct(shape, bf16)],
+        unit_scratch(weights, 2),
+        flops=4 * rows * width * quarters * units,
+    )
+
+
+def call_expert(core, own, peer, prepared, marks_t, weights):
+    rows, half = own.shape
+    lanes = half + marks_t.shape[0]
     return call(
         expert_kernel,
         "expert",
         core,
-        (own, peer, latent_t, marks_t, weights),
-        (4,),
+        (own, peer) + tuple(prepared) + (marks_t, weights),
+        (6,),
         [struct((rows, lanes), f32), struct((rows, lanes), bf16)],
-        [
-            pltpu.VMEM((width, rows), bf16),
-            pltpu.VMEM((mats, quarters * units, width), bf16),
-            pltpu.SemaphoreType.DMA((quarters * mats,)),
-        ],
-    )
+        [pltpu.VMEM((2 * half, rows), bf16)] + unit_scratch(weights, 3),
+    )
+
+
+def call_mix(core, own, peer, keep, other, gates):
+    shape = (own.shape[1], keep.shape[1])
+    return call(
+        mix_kernel, "mix", core, (own, peer, keep, other, gates), (), [struct(shape, f32)], []
+    )[0]
 
 
 def on_device(
@@ -420,36 +478,46 @@
         )
 
     gate_mat, up_mat, out_mat = w_gate[0], w_up[0], w_out[0]
-    lift_wide = lax.all_gather(w_lift.T, plane, axis=0, tiled=True)
+    lift_t = w_lift.T
+    ring = lax.axis_size("y")
+    around = [lift_t] + [
+        lax.ppermute(lift_t, "y", [((i + k) % ring, i) for i in range(ring)])
+        for k in range(1, ring)
+    ]
 
     gate_marks = jnp.where(route_ids.T == own_index, gates.T, 0.0)
     gate_own = jnp.sum(gate_marks, axis=0)
-    high = lax.reduce_precision(gate_own, 8, 7)
-    middle = lax.reduce_precision(gate_own - high, 8, 7)
-    low = gate_own - high - middle
-    gate_rows = jnp.concatenate([high, middle, low, jnp.zeros_like(low)]).reshape(-1, half)
-    extra = jnp.pad(gate_rows.astype(bf16), ((0, 16 - gate_rows.shape[0]), (0, 0)))
+    ahead = [gate_own] + [
+        lax.ppermute(gate_own, "dp", [(i, (i + k) % groups) for i in range(groups)])
+        for k in range(1, groups)
+    ]
     out_keep = mine(out_mat, 1)
     out_peer = swap(other(out_mat, 1))
 
-    lat_own = spread(jnp.concatenate([mine(latent, 1), extra]), "dp")
+    lat_own = spread(mine(latent, 1), "dp")
+    *ahead, lat_own = lax.optimization_barrier((*ahead, lat_own))
     lat_peer = swap(lat_own)
-
-    def gate_of(x):
-        parts = x[:, rows : rows + gate_rows.shape[0]].reshape(groups, -1).astype(f32)
-        parts = parts.reshape(groups, -1, rows)
-        return (parts[:, 0] + parts[:, 1] + parts[:, 2]).reshape(-1)
-
-    gate_all, gate_peer = gate_of(lat_own), gate_of(lat_peer)
-    lat_all = joined(lat_own[:, :rows], lat_peer[:, :rows], 2).reshape(-1, width)
+    turn = (ring - lax.axis_index("y")) % ring
+    *around, lat_own = lax.optimization_barrier((*around, lat_own))
+    lift_deep = lax.dynamic_slice_in_dim(jnp.stack(around + around), turn, ring, 0)
+    lift_wide = lax.all_gather(lift_deep, "z", axis=0, tiled=True).reshape(wide, width)
+
+    lat_all = joined(lat_own, lat_peer, 2).reshape(-1, width)
     gate_part = dot(lat_all, gate_mat, 1, 0)
     up_part = dot(lat_all, up_mat, 1, 0)
     active = (jax.nn.silu(gate_part) * up_part).astype(bf16)
-    active_peer = swap(active)
-    part = dot(active, out_keep, 1, 0) * gate_all[:, None]
-    part = part + dot(active_peer, out_peer, 1, 0) * gate_peer[:, None]
+    core_id = core.astype(jnp.int32)[None]
+    ahead = jnp.stack(ahead)
+    gate_rows = jnp.concatenate([ahead, swap(ahead)])
+    spot = jnp.stack([core, lax.axis_index("dp")]).astype(jnp.int32)
+    active_t = active.T
+    part = call_mix(spot, active_t, swap(active_t), out_keep, out_peer, gate_rows)
     part, gate_mat, up_mat, out_mat = lax.optimization_barrier((part, gate_mat, up_mat, out_mat))
+    weights = jnp.stack([gate_mat.T, up_mat.T, out_mat])
     summed = jnp.sum(deal(part, "dp").reshape(groups, rows, half), axis=0)
+
+    summed, weights = lax.optimization_barrier((summed, weights))
+    weights = lax.all_gather(weights, "dp")
 
     summed = summed.reshape(places, chunk, half)
     carried = residual.reshape(places, chunk, cols).astype(f32)
@@ -457,9 +525,6 @@
     dealt = deal(jnp.concatenate([summed, carried], axis=2), plane)
     comb_own = jnp.sum(dealt[:, :, :half], axis=0).astype(bf16)
     res_rows = dealt[:, :, half : half + cols].transpose(1, 0, 2).reshape(chunk, wide)
-    weights = lax.all_gather(jnp.stack([gate_mat.T, up_mat.T, out_mat]), "dp")
-
-    core_id = core.astype(jnp.int32)[None]
     hidden = call_lift(core_id, comb_own, swap(comb_own), res_rows, lift_wide)
     hid_own = spread(hidden, plane).reshape(rows, wide)
 
@@ -480,6 +545,8 @@
     keep = call_keep(core_id, grad, vocab)
     keep = (keep + swap(send).astype(f32)).astype(bf16)
     parts = deal(keep.reshape(places, chunk, wide), plane)
+    prepared = call_prepare(core_id, latent.T, weights)
+    parts, *prepared = lax.optimization_barrier((parts, *prepared))
     chunks, partial = call_lower(
         place.astype(jnp.int32)[None], parts, hidden, gain_own.reshape(1, wide), marks, lift_wide
     )
@@ -491,7 +558,7 @@
     d_residual = d_residual.reshape(rows, cols)
 
     gate_marks = jnp.pad(gate_marks, ((0, 128 - gate_marks.shape[0]), (0, 0)))
-    keep, send = call_expert(core_id, cg_own, swap(cg_own), latent.T, gate_marks, weights)
+    keep, send = call_expert(core_id, cg_own, swap(cg_own), prepared, gate_marks, weights)
     keep = (keep + swap(send).astype(f32)).astype(bf16)
     tail = jnp.sum(deal(keep, plane).astype(f32).reshape(places, chunk, -1), axis=0).astype(bf16)
     tail = spread(tail, plane).reshape(rows, -1)

time: 300 us -> 294 us (0.980)
  blocking collectives: 138 us -> 113 us
  starting transfers between devices: 28.5 us -> 49.5 us
  matrix products: 8.27 us -> 2.47 us
  waiting for transfers between devices: 71.1 us -> 65.7 us
  Pallas kernels: 27.4 us -> 31.5 us
  local copies, waits for them, and re-layouts: 4.68 us -> 8.36 us
    all_to_all x6 -> x5, blocking collectives: 138 us -> 113 us  [deal(): return lax.all_to_all(x, axes, 0, 0, tiled=True)]
    ppermute x0 -> x6, starting transfers between devices: none -> 11.4 us  [the longest x3 7.52 us: on_device(): lax.ppermute(gate_own, 'dp', [(i, (i + k) % groups) for i in range(groups)])]
    all_to_all x3 -> x4, waiting for transfers between devices: 63.7 us -> 54.9 us  [deal(): return lax.all_to_all(x, axes, 0, 0, tiled=True)]
    all_to_all x3 -> x4, starting transfers between devices: 12.4 us -> 18.4 us  [deal(): return lax.all_to_all(x, axes, 0, 0, tiled=True)]
    dot_general x4 -> x2, matrix products: 8.27 us -> 2.47 us  [dot(): lax.dot_general(a, b, (((ca,), (cb,)), ((), ())), preferred_element_type=...]
    pallas_call x6 -> x8, Pallas kernels: 27.4 us -> 31.5 us  [call(): pl.pallas_call(kernel, grid_spec=pltpu.PrefetchScalarGridSpec(num_scalar_...]
    ppermute x10 -> x11, starting transfers between devices: 16 us -> 19.7 us  [swap(): return lax.ppermute(x, 'c', [(0, 1), (1, 0)])]
    ppermute x10 -> x11, waiting for transfers between devices: 6.64 us -> 7.95 us  [swap(): return lax.ppermute(x, 'c', [(0, 1), (1, 0)])]
  transfers between devices with their start and end apart: 15 -> 23, of which waited for: 10 -> 13; matrix products, arithmetic and copies ran while one was open for 6% -> 4% of each run, Pallas kernels for 6% -> 8%
where the time goes in v7:
time: 294 us; the launch traced here: 293 us
  blocking collectives  113 us (38%)
  waiting for transfers between devices  65.7 us (22%)
  starting transfers between devices  49.5 us (17%)
  Pallas kernels  31.5 us (11%)
  between operations  14.5 us (5%)
  other arithmetic  8.42 us (3%)
  local copies, waits for them, and re-layouts  8.36 us (3%)
    all_to_all x5, blocking collectives, deal(): return lax.all_to_all(x, axes, 0, 0, tiled=True)  113 us
    all_to_all x4, waiting for transfers between devices, deal(): return lax.all_to_all(x, axes, 0, 0, tiled=True)  54.9 us
    pallas_call x8, Pallas kernels, call(): pl.pallas_call(kernel, grid_spec=pltpu.PrefetchScalarGridSpec(num_scalar_...  31.5 us
    ppermute x11, starting transfers between devices, swap(): return lax.ppermute(x, 'c', [(0, 1), (1, 0)])  19.7 us
    all_to_all x4, starting transfers between devices, deal(): return lax.all_to_all(x, axes, 0, 0, tiled=True)  18.4 us
    ppermute x11, waiting for transfers between devices, swap(): return lax.ppermute(x, 'c', [(0, 1), (1, 0)])  7.95 us
    ppermute x3, starting transfers between devices, on_device(): lax.ppermute(gate_own, 'dp', [(i, (i + k) % groups) for i in range(groups)])  7.52 us
  transfers between devices with their start and end apart: 23, of which 13 were waited for; matrix products, arithmetic and copies ran while one was open for 4% of the time, Pallas kernels for 8%

profile of v7, /device:TPU:1, one launch (start us, length us, event | category | flops | bytes accessed | tf_op | source)
XLA Modules:
  0.0 293.5 jit_solution(8399458920089644222)
XLA Ops:
  7.2 1.1 slice_select_fusion
  8.3 1.1 broadcast_in_dim.24
  9.4 4.8 %all-to-all-start = ((bf16[4,256,512]{2,1,0:T(8,128)(2,1)}), bf16[4,256,512]{2,1,0:T(8,128)(2,1)S(1)}, u32[]{:S(2)}, u32[]{:S(2)}) async-start(bf16[4,256,512]{2,1,0:T(8,128)(2,1)} %broadcast_in_dim.24), calls=%async_computation | async-start | bytes 2097152 | tf_op jit(solution)/shard_map/all_to_all | solution.py:24
  14.2 2.8 collective-permute-start
  17.0 0.3 collective-permute-start.1
  17.4 0.7 collective-permute-start.2
  18.1 1.5 collective-permute-start.3
  19.6 2.4 collective-permute-start.4
  22.0 2.1 collective-permute-done.3
  24.2 3.6 %collective-permute-start.5 = (f32[256]{0:T(256)S(1)}, f32[256]{0:T(256)S(1)}, u32[]{:S(2)}, u32[]{:S(2)}) collective-permute-start(f32[256]{0:T(256)S(1)} %get-tuple-element.40), channel_id=1, source_target_pairs={{0,192},{64,0},{128,64},{192,128},{1,193},{65,1},{129,65},{193,129... | collective-permute-start | bytes 3080 | tf_op jit(solution)/shard_map/ppermute | solution.py:491
  27.8 0.7 collective-permute-done.5
  28.7 0.8 constant_dynamic-slice_fusion
  29.5 3.8 %collective-permute-start.6 = (bf16[4,256,512]{2,1,0:T(8,128)(2,1)S(1)}, bf16[4,256,512]{2,1,0:T(8,128)(2,1)S(1)}, u32[]{:S(2)}, u32[]{:S(2)}) collective-permute-start(bf16[4,256,512]{2,1,0:T(8,128)(2,1)S(1)} %all-to-all-done), channel_id=1, source_target_pairs={{0,1},{1,0},{2,3},{3,2},{4,5},{5,4},{6,7},{7,6},{8,9},{9,8},{10,11... | collective-permute-start | bytes 3145736 | tf_op jit(solution)/shard_map/ppermute | solution.py:20
  33.3 2.3 collective-permute-done.6
  35.6 1.2 convolution_bitcast_fusion.1
  36.8 1.3 multiply_convert_fusion.own
  38.1 0.5 collective-permute-start.7
  38.5 0.8 broadcast_select_fusion
  39.5 0.5 collective-permute-start.9
  40.0 1.0 collective-permute-done.9
  41.2 3.2 %mix.1 = f32[1024,512]{1,0:T(8,128)} custom-call(s32[2]{0:T(128)S(1)} %pad_add_fusion.spot, bf16[336,1024]{1,0:T(8,128)(2,1)S(1)} %multiply_convert_fusion.own, bf16[336,1024]{1,0:T(8,128)(2,1)S(1)} %collective-permute-done.7.peer, bf16[336,512]{1,0:T(8,128)(2,1)S(1)} %get-tuple-element.87.keep, bf16[336,512]{1,0:T(8,128)(2,1)S(1)} %collective-permute-done.8.other, ...), custom_call_target="tpu_custom_call" | custom-call | tf_op jit(solution)/shard_map/mix/pallas_call | solution.py:296
  44.4 4.5 %all-to-all-start.1 = ((f32[4,256,512]{2,1,0:T(8,128)}), f32[4,256,512]{2,1,0:T(8,128)S(1)}, u32[]{:S(2)}, u32[]{:S(2)}) async-start(f32[4,256,512]{2,1,0:T(8,128)} %bitcast.14), calls=%async_computation.1 | async-start | bytes 4194304 | tf_op jit(solution)/shard_map/all_to_all | solution.py:24
  48.9 2.6 pad_maximum_fusion
  51.5 23.3 %all-to-all-done.1 = f32[4,256,512]{2,1,0:T(8,128)S(1)} async-done(((f32[4,256,512]{2,1,0:T(8,128)}), f32[4,256,512]{2,1,0:T(8,128)S(1)}, u32[]{:S(2)}, u32[]{:S(2)}) %all-to-all-start.1) | async-done | bytes 2097184 | tf_op jit(solution)/shard_map/all_to_all | solution.py:24
  74.8 0.2 reduce_sum.40
  75.3 29.3 %all_to_all.53 = f32[32,8,640]{2,1,0:T(8,128)S(1)} all-to-all(f32[32,8,640]{2,1,0:T(8,128)S(1)} %pad_maximum_fusion.1), channel_id=1, replica_groups=mesh['dp'=4,'z'=8,'y'=4,'c'=2] {'z','y'}, dimensions={0} | all-to-all | bytes 1310720 | tf_op jit(solution)/shard_map/all_to_all | solution.py:24
  104.7 3.4 %collective-permute-start.10 = (bf16[8,512]{1,0:T(8,128)(2,1)S(1)}, bf16[8,512]{1,0:T(8,128)(2,1)S(1)}, u32[]{:S(2)}, u32[]{:S(2)}) collective-permute-start(bf16[8,512]{1,0:T(8,128)(2,1)S(1)} %slice_reduce_fusion), channel_id=1, source_target_pairs={{0,1},{1,0},{2,3},{3,2},{4,5},{5,4},{6,7},{7,6},{8,9},{9,8},{10,11... | collective-permute-start | bytes 24584 | tf_op jit(solution)/shard_map/ppermute | solution.py:20
  108.3 0.7 collective-permute-done.10
  108.9 3.2 %lift.1.hidden = bf16[8,2048]{1,0:T(8,128)(2,1)S(1)} custom-call(s32[1]{0:T(128)} %bitcast.core, f32[8,512]{1,0:T(8,128)S(1)} %convert_element_type.59.own, f32[8,512]{1,0:T(8,128)S(1)} %convert_element_type.60.peer, f32[8,2048]{1,0:T(8,128)S(1)} %reshape.93.residual, bf16[2048,1024]{1,0:T(8,128)(2,1)} %bitcast.76), custom_call_target="tpu_custom_call" | custom-call | tf_op jit(solution)/shard_map/lift/pallas_call | solution.py:296
  112.3 30.4 %all_to_all.54 = bf16[32,8,2048]{2,1,0:T(8,128)(2,1)S(1)} all-to-all(bf16[32,8,2048]{2,1,0:T(8,128)(2,1)S(1)} %broadcast_in_dim.25), channel_id=1, replica_groups=mesh['dp'=4,'z'=8,'y'=4,'c'=2] {'z','y'}, dimensions={0} | all-to-all | bytes 2097152 | tf_op jit(solution)/shard_map/all_to_all | solution.py:24
  142.7 2.6 collective-permute-start.11
  145.4 0.5 broadcast.39
  145.9 0.7 fusion.10
  147.0 0.6 collective-permute-done.11.peer
  147.6 5.2 %head.1 = (f32[256,1024]{1,0:T(8,128)S(1)}, f32[8,128]{1,0:T(8,128)S(1)}, f32[256,128]{1,0:T(8,128)S(1)}) custom-call(s32[1]{0:T(128)} %bitcast.core, bf16[256,2048]{1,0:T(8,128)(2,1)S(1)} %bitcast.68, bf16[256,2048]{1,0:T(8,128)(2,1)S(1)} %collective-permute-done.11.peer, f32[4,1024]{1,0:T(4,128)S(1)} %pad_maximum_fusion.3.gain, ...), custom_call_target="tpu_custom_call" | custom-call | tf_op jit(solution)/shard_map/head/pallas_call | solution.py:296
  152.8 19.1 %all_to_all.55.stats = f32[64,8,128]{2,1,0:T(8,128)S(1)} all-to-all(f32[64,8,128]{2,1,0:T(8,128)S(1)} %broadcast_in_dim.51), channel_id=1, replica_groups=mesh['dp'=4,'z'=8,'y'=4,'c'=2] {'z','y','c'}, dimensions={0} | all-to-all | bytes 524288 | tf_op jit(solution)/shard_map/all_to_all | solution.py:24
  171.9 3.7 %loss.1 = (bf16[256,1024]{1,0:T(8,128)(2,1)S(1)}, bf16[256,2048]{1,0:T(8,128)(2,1)S(1)}, f32[8,256]{1,0:T(8,128)S(1)}, f32[256,128]{1,0:T(8,128)S(1)}) custom-call(s32[1]{0:T(128)} %bitcast.core, f32[64,8,128]{2,1,0:T(8,128)S(1)} %all_to_all.55.stats, f32[256,1024]{1,0:T(8,128)S(1)} %get-tuple-element.54.logits, s32[256,1]{1,0:T(8,128)S(1)} %copy.29.target, ...), custom_call_target="tpu_custom_call" | custom-call | tf_op jit(solution)/shard_map/loss/pallas_call | solution.py:296
  175.6 0.3 collective-permute-start.12
  175.9 3.1 %keep.1 = f32[256,2048]{1,0:T(8,128)S(1)} custom-call(s32[1]{0:T(128)} %bitcast.core, bf16[256,1024]{1,0:T(8,128)(2,1)S(1)} %get-tuple-element.57.grad, bf16[32,2,64,1024]{3,2,1,0:T(8,128)(2,1)} %bitcast.73), custom_call_target="tpu_custom_call" | custom-call | flops 1073741824 | bytes 2097152 | tf_op jit(solution)/shard_map/keep/pallas_call | solution.py:296
  179.1 1.3 fusion
  180.4 4.4 %all-to-all-start.5 = ((bf16[32,8,2048]{2,1,0:T(8,128)(2,1)}), bf16[32,8,2048]{2,1,0:T(8,128)(2,1)S(1)}, u32[]{:S(2)}, u32[]{:S(2)}) async-start(bf16[32,8,2048]{2,1,0:T(8,128)(2,1)} %fusion), calls=%async_computation.5 | async-start | bytes 2097152 | tf_op jit(solution)/shard_map/all_to_all | solution.py:24
  184.7 0.2 copy.31
  185.0 3.9 %prepare.1 = (f32[1344,256]{1,0:T(8,128)S(1)}, f32[1344,256]{1,0:T(8,128)S(1)}, bf16[1344,256]{1,0:T(8,128)(2,1)S(1)}) custom-call(s32[1]{0:T(128)} %bitcast.core, bf16[1024,256]{1,0:T(8,128)(2,1)S(1)} %bitcast.69, bf16[4,3,336,1024]{3,2,1,0:T(8,128)(2,1)} %bitcast.74), custom_call_target="tpu_custom_call" | custom-call | flops 1409286144 | bytes 2752512 | tf_op jit(solution)/shard_map/prepare/pallas_call | solution.py:296
  188.9 1.1 copy-done
  190.0 0.9 copy-done.2
  190.9 20.9 %all-to-all-done.5.parts = bf16[32,8,2048]{2,1,0:T(8,128)(2,1)S(1)} async-done(((bf16[32,8,2048]{2,1,0:T(8,128)(2,1)}), bf16[32,8,2048]{2,1,0:T(8,128)(2,1)S(1)}, u32[]{:S(2)}, u32[]{:S(2)}) %all-to-all-start.5) | async-done | bytes 1048608 | tf_op jit(solution)/shard_map/all_to_all | solution.py:24
  211.8 2.6 lower.1
  214.5 1.8 collective-permute-start.13
  216.3 0.8 collective-permute-done.13
  217.2 17.9 %all_to_all.56 = bf16[32,8,640]{2,1,0:T(8,128)(2,1)S(1)} all-to-all(bf16[32,8,640]{2,1,0:T(8,128)(2,1)S(1)} %pad_maximum_fusion.2), channel_id=1, replica_groups=mesh['dp'=4,'z'=8,'y'=4,'c'=2] {'z','y'}, dimensions={0} | all-to-all | bytes 655360 | tf_op jit(solution)/shard_map/all_to_all | solution.py:24
  235.1 2.5 collective-permute-start.14
  237.6 1.1 collective-permute-done.14.peer
  238.7 6.6 %expert.1 = (f32[256,640]{1,0:T(8,128)S(1)}, bf16[256,640]{1,0:T(8,128)(2,1)S(1)}) custom-call(s32[1]{0:T(128)} %bitcast.core, bf16[256,512]{1,0:T(8,128)(2,1)S(1)} %slice_bitcast_fusion.own, bf16[256,512]{1,0:T(8,128)(2,1)S(1)} %collective-permute-done.14.peer, f32[1344,256]{1,0:T(8,128)S(1)} %get-tuple-element.67.slope, f32[1344,256]{1,0:T(8,128)S(1)} %copy-done.1, ...), custom_call_target="tpu_custom_call" | custom-call | tf_op jit(solution)/shard_map/expert/pallas_call | solution.py:296
  245.4 0.5 collective-permute-start.15
  245.8 1.3 collective-permute-done.15
  247.1 16.3 %all_to_all.57 = bf16[32,8,640]{2,1,0:T(8,128)(2,1)S(1)} all-to-all(bf16[32,8,640]{2,1,0:T(8,128)(2,1)S(1)} %fusion.2), channel_id=1, replica_groups=mesh['dp'=4,'z'=8,'y'=4,'c'=2] {'z','y'}, dimensions={0} | all-to-all | bytes 655360 | tf_op jit(solution)/shard_map/all_to_all | solution.py:24
  263.5 0.8 broadcast_in_dim.55
  264.2 4.8 %all-to-all-start.8 = ((bf16[32,8,640]{2,1,0:T(8,128)(2,1)}), bf16[32,8,640]{2,1,0:T(8,128)(2,1)S(1)}, u32[]{:S(2)}, u32[]{:S(2)}) async-start(bf16[32,8,640]{2,1,0:T(8,128)(2,1)} %broadcast_in_dim.55), calls=%async_computation.8 | async-start | bytes 655360 | tf_op jit(solution)/shard_map/all_to_all | solution.py:24
  269.0 0.6 slice.37
  269.6 10.7 %all-to-all-done.8 = bf16[32,8,640]{2,1,0:T(8,128)(2,1)S(1)} async-done(((bf16[32,8,640]{2,1,0:T(8,128)(2,1)}), bf16[32,8,640]{2,1,0:T(8,128)(2,1)S(1)}, u32[]{:S(2)}, u32[]{:S(2)}) %all-to-all-start.8) | async-done | bytes 327712 | tf_op jit(solution)/shard_map/all_to_all | solution.py:24
  280.3 3.8 %collective-permute-start.16 = (bf16[256,512]{1,0:T(8,128)(2,1)S(1)}, bf16[256,512]{1,0:T(8,128)(2,1)S(1)}, u32[]{:S(2)}, u32[]{:S(2)}) collective-permute-start(bf16[256,512]{1,0:T(8,128)(2,1)S(1)} %slice.50), channel_id=1, source_target_pairs={{0,1},{1,0},{2,3},{3,2},{4,5},{5,4},{6,7},{7,6},{8,9},{9,8},{10,11... | collective-permute-start | bytes 786440 | tf_op jit(solution)/shard_map/ppermute | solution.py:20
  284.1 0.7 copy.32
  284.8 0.7 copy.33
  285.5 1.1 fusion.1
  (85 shorter events, 2.0 us)
Async XLA Ops:
  7.2 7.0 %copy-start.9 = (bf16[1024,64]{0,1:T(8,128)(2,1)S(1)}, bf16[1024,64]{0,1:T(8,128)(2,1)}, u32[]{:S(2)}) copy-start(bf16[1024,64]{0,1:T(8,128)(2,1)} %param.19) | copy-start | bytes 393220
  7.2 10.9 %copy-start.11 = (f32[256,22]{0,1:T(8,128)S(1)}, f32[256,22]{0,1:T(8,128)}, u32[]{:S(2)}) copy-start(f32[256,22]{0,1:T(8,128)} %param.14) | copy-start | bytes 67588
  7.2 10.9 %copy-start.12 = (s32[256,22]{0,1:T(8,128)S(1)}, s32[256,22]{0,1:T(8,128)}, u32[]{:S(2)}) copy-start(s32[256,22]{0,1:T(8,128)} %param.15) | copy-start | bytes 67588
  9.4 19.1 %all-to-all-start = ((bf16[4,256,512]{2,1,0:T(8,128)(2,1)}), bf16[4,256,512]{2,1,0:T(8,128)(2,1)S(1)}, u32[]{:S(2)}, u32[]{:S(2)}) async-start(bf16[4,256,512]{2,1,0:T(8,128)(2,1)} %broadcast_in_dim.24), calls=%async_computation | async-start | bytes 2097152 | tf_op jit(solution)/shard_map/all_to_all | solution.py:24
  14.2 21.4 %copy-start.7 = (bf16[1,1024,336]{1,2,0:T(8,128)(2,1)S(1)}, bf16[1,1024,336]{1,2,0:T(8,128)(2,1)}, u32[]{:S(2)}) copy-start(bf16[1,1024,336]{1,2,0:T(8,128)(2,1)} %param.16) | copy-start | bytes 2064388
  14.2 94.7 %all-gather.4.cloned.1.call-start = ((), (), s32[]{:S(2)}) async-start(), calls=%async_computation.9 | async-start | bytes 4718592 | tf_op jit(solution)/shard_map/all_gather | solution.py:503
  14.2 14.3 %collective-permute-start = (bf16[64,1024]{1,0:T(8,128)(2,1)S(1)}, bf16[64,1024]{1,0:T(8,128)(2,1)S(1)}, u32[]{:S(2)}, u32[]{:S(2)}) collective-permute-start(bf16[64,1024]{1,0:T(8,128)(2,1)S(1)} %bitcast.86), channel_id=1, source_target_pairs={{2,0},{4,2},{6,4},{0,6},{3,1},{5,3},{7,5},{1,7},{10,8},{12,10},{14... | collective-permute-start | bytes 393224 | tf_op jit(solution)/shard_map/ppermute | solution.py:484
  17.0 11.5 %collective-permute-start.1 = (bf16[64,1024]{1,0:T(8,128)(2,1)S(1)}, bf16[64,1024]{1,0:T(8,128)(2,1)S(1)}, u32[]{:S(2)}, u32[]{:S(2)}) collective-permute-start(bf16[64,1024]{1,0:T(8,128)(2,1)S(1)} %bitcast.87), channel_id=1, source_target_pairs={{4,0},{6,2},{0,4},{2,6},{5,1},{7,3},{1,5},{3,7},{12,8},{14,10},{8,... | collective-permute-start | bytes 393224 | tf_op jit(solution)/shard_map/ppermute | solution.py:484
  17.4 11.1 %collective-permute-start.2 = (bf16[64,1024]{1,0:T(8,128)(2,1)S(1)}, bf16[64,1024]{1,0:T(8,128)(2,1)S(1)}, u32[]{:S(2)}, u32[]{:S(2)}) collective-permute-start(bf16[64,1024]{1,0:T(8,128)(2,1)S(1)} %bitcast.88), channel_id=1, source_target_pairs={{6,0},{0,2},{2,4},{4,6},{7,1},{1,3},{3,5},{5,7},{14,8},{8,10},{10,... | collective-permute-start | bytes 393224 | tf_op jit(solution)/shard_map/ppermute | solution.py:484
  18.1 6.1 %collective-permute-start.3 = (f32[256]{0:T(256)S(1)}, f32[256]{0:T(256)S(1)}, u32[]{:S(2)}, u32[]{:S(2)}) collective-permute-start(f32[256]{0:T(256)S(1)} %get-tuple-element.40), channel_id=1, source_target_pairs={{0,64},{64,128},{128,192},{192,0},{1,65},{65,129},{129,193},{193,1... | collective-permute-start | bytes 3080 | tf_op jit(solution)/shard_map/ppermute | solution.py:491
  19.6 8.1 %collective-permute-start.4 = (f32[256]{0:T(256)S(1)}, f32[256]{0:T(256)S(1)}, u32[]{:S(2)}, u32[]{:S(2)}) collective-permute-start(f32[256]{0:T(256)S(1)} %get-tuple-element.40), channel_id=1, source_target_pairs={{0,128},{64,192},{128,0},{192,64},{1,129},{65,193},{129,1},{193,65... | collective-permute-start | bytes 3080 | tf_op jit(solution)/shard_map/ppermute | solution.py:491
  24.2 4.3 %collective-permute-start.5 = (f32[256]{0:T(256)S(1)}, f32[256]{0:T(256)S(1)}, u32[]{:S(2)}, u32[]{:S(2)}) collective-permute-start(f32[256]{0:T(256)S(1)} %get-tuple-element.40), channel_id=1, source_target_pairs={{0,192},{64,0},{128,64},{192,128},{1,193},{65,1},{129,65},{193,129... | collective-permute-start | bytes 3080 | tf_op jit(solution)/shard_map/ppermute | solution.py:491
  29.5 6.0 %collective-permute-start.6 = (bf16[4,256,512]{2,1,0:T(8,128)(2,1)S(1)}, bf16[4,256,512]{2,1,0:T(8,128)(2,1)S(1)}, u32[]{:S(2)}, u32[]{:S(2)}) collective-permute-start(bf16[4,256,512]{2,1,0:T(8,128)(2,1)S(1)} %all-to-all-done), channel_id=1, source_target_pairs={{0,1},{1,0},{2,3},{3,2},{4,5},{5,4},{6,7},{7,6},{8,9},{9,8},{10,11... | collective-permute-start | bytes 3145736 | tf_op jit(solution)/shard_map/ppermute | solution.py:20
  35.6 1.2 copy-start.8
  36.8 1.8 copy-start.5
  38.1 3.1 %collective-permute-start.7 = (bf16[336,1024]{1,0:T(8,128)(2,1)S(1)}, bf16[336,1024]{1,0:T(8,128)(2,1)S(1)}, u32[]{:S(2)}, u32[]{:S(2)}) collective-permute-start(bf16[336,1024]{1,0:T(8,128)(2,1)S(1)} %multiply_convert_fusion.own), channel_id=1, source_target_pairs={{0,1},{1,0},{2,3},{3,2},{4,5},{5,4},{6,7},{7,6},{8,9},{9,8},{10,11... | collective-permute-start | bytes 2064392 | tf_op jit(solution)/shard_map/ppermute | solution.py:20
  39.3 1.9 collective-permute-start.8
  39.5 1.5 collective-permute-start.9
  44.4 30.4 %all-to-all-start.1 = ((f32[4,256,512]{2,1,0:T(8,128)}), f32[4,256,512]{2,1,0:T(8,128)S(1)}, u32[]{:S(2)}, u32[]{:S(2)}) async-start(f32[4,256,512]{2,1,0:T(8,128)} %bitcast.14), calls=%async_computation.1 | async-start | bytes 4194304 | tf_op jit(solution)/shard_map/all_to_all | solution.py:24
  48.9 136.2 %all-gather.6.cloned.1.call-start = ((), (), s32[]{:S(2)}) async-start(), calls=%async_computation.10 | async-start | bytes 10321920 | tf_op jit(solution)/shard_map/all_gather | solution.py:520
  51.5 23.6 %copy-start.10 = (bf16[256,64]{0,1:T(8,128)(2,1)S(1)}, bf16[256,64]{0,1:T(8,128)(2,1)}, u32[]{:S(2)}) copy-start(bf16[256,64]{0,1:T(8,128)(2,1)} %param.13) | copy-start | bytes 98308
  104.7 4.2 %collective-permute-start.10 = (bf16[8,512]{1,0:T(8,128)(2,1)S(1)}, bf16[8,512]{1,0:T(8,128)(2,1)S(1)}, u32[]{:S(2)}, u32[]{:S(2)}) collective-permute-start(bf16[8,512]{1,0:T(8,128)(2,1)S(1)} %slice_reduce_fusion), channel_id=1, source_target_pairs={{0,1},{1,0},{2,3},{3,2},{4,5},{5,4},{6,7},{7,6},{8,9},{9,8},{10,11... | collective-permute-start | bytes 24584 | tf_op jit(solution)/shard_map/ppermute | solution.py:20
  112.1 33.2 %copy-start.13 = (bf16[4096]{0:T(1024)(128)(2,1)S(1)}, bf16[4096]{0:T(1024)(128)(2,1)}, u32[]{:S(2)}) copy-start(bf16[4096]{0:T(1024)(128)(2,1)} %param.20) | copy-start | bytes 24580
  112.1 34.7 %copy-start.14 = (s32[256]{0:T(256)S(1)}, s32[256]{0:T(256)}, u32[]{:S(2)}) copy-start(s32[256]{0:T(256)} %param.22) | copy-start | bytes 3076
  142.7 4.9 %collective-permute-start.11 = (bf16[256,2048]{1,0:T(8,128)(2,1)S(1)}, bf16[256,2048]{1,0:T(8,128)(2,1)S(1)}, u32[]{:S(2)}, u32[]{:S(2)}) collective-permute-start(bf16[256,2048]{1,0:T(8,128)(2,1)S(1)} %bitcast.67), channel_id=1, source_target_pairs={{0,1},{1,0},{2,3},{3,2},{4,5},{5,4},{6,7},{7,6},{8,9},{9,8},{10,11... | collective-permute-start | bytes 3145736 | tf_op jit(solution)/shard_map/ppermute | solution.py:20
  147.6 24.3 %copy-start.4 = (f32[256]{0:T(256)S(1)}, f32[256]{0:T(256)}, u32[]{:S(2)}) copy-start(f32[256]{0:T(256)} %param.23) | copy-start | bytes 3076
  175.6 3.5 %collective-permute-start.12 = (bf16[256,2048]{1,0:T(8,128)(2,1)S(1)}, bf16[256,2048]{1,0:T(8,128)(2,1)S(1)}, u32[]{:S(2)}, u32[]{:S(2)}) collective-permute-start(bf16[256,2048]{1,0:T(8,128)(2,1)S(1)} %get-tuple-element.58), channel_id=1, source_target_pairs={{0,1},{1,0},{2,3},{3,2},{4,5},{5,4},{6,7},{7,6},{8,9},{9,8},{10,11... | collective-permute-start | bytes 3145736 | tf_op jit(solution)/shard_map/ppermute | solution.py:20
  180.4 4.4 %copy-start.6 = (bf16[256,1024]{1,0:T(8,128)(2,1)S(1)}, bf16[256,1024]{1,0:T(8,128)(2,1)}, u32[]{:S(2)}) copy-start(bf16[256,1024]{1,0:T(8,128)(2,1)} %param.12) | copy-start | bytes 1572868
  180.4 31.4 %all-to-all-start.5 = ((bf16[32,8,2048]{2,1,0:T(8,128)(2,1)}), bf16[32,8,2048]{2,1,0:T(8,128)(2,1)S(1)}, u32[]{:S(2)}, u32[]{:S(2)}) async-start(bf16[32,8,2048]{2,1,0:T(8,128)(2,1)} %fusion), calls=%async_computation.5 | async-start | bytes 2097152 | tf_op jit(solution)/shard_map/all_to_all | solution.py:24
  188.9 1.1 copy-start
  190.0 0.9 copy-start.2
  214.4 24.3 %copy-start.1 = (f32[1344,256]{1,0:T(8,128)S(1)}, f32[1344,256]{1,0:T(8,128)}, u32[]{:S(2)}) copy-start(f32[1344,256]{1,0:T(8,128)} %copy-done) | copy-start | bytes 4128772
  214.4 24.3 %copy-start.3 = (bf16[1344,256]{1,0:T(8,128)(2,1)S(1)}, bf16[1344,256]{1,0:T(8,128)(2,1)}, u32[]{:S(2)}) copy-start(bf16[1344,256]{1,0:T(8,128)(2,1)} %copy-done.2) | copy-start | bytes 2064388
  214.5 2.7 collective-permute-start.13
  235.1 3.6 %collective-permute-start.14 = (bf16[256,512]{1,0:T(8,128)(2,1)S(1)}, bf16[256,512]{1,0:T(8,128)(2,1)S(1)}, u32[]{:S(2)}, u32[]{:S(2)}) collective-permute-start(bf16[256,512]{1,0:T(8,128)(2,1)S(1)} %slice_bitcast_fusion.own), channel_id=1, source_target_pairs={{0,1},{1,0},{2,3},{3,2},{4,5},{5,4},{6,7},{7,6},{8,9},{9,8},{10,11... | collective-permute-start | bytes 786440 | tf_op jit(solution)/shard_map/ppermute | solution.py:20
  245.4 1.7 collective-permute-start.15
  264.2 16.0 %all-to-all-start.8 = ((bf16[32,8,640]{2,1,0:T(8,128)(2,1)}), bf16[32,8,640]{2,1,0:T(8,128)(2,1)S(1)}, u32[]{:S(2)}, u32[]{:S(2)}) async-start(bf16[32,8,640]{2,1,0:T(8,128)(2,1)} %broadcast_in_dim.55), calls=%async_computation.8 | async-start | bytes 655360 | tf_op jit(solution)/shard_map/all_to_all | solution.py:24
  280.3 5.3 %collective-permute-start.16 = (bf16[256,512]{1,0:T(8,128)(2,1)S(1)}, bf16[256,512]{1,0:T(8,128)(2,1)S(1)}, u32[]{:S(2)}, u32[]{:S(2)}) collective-permute-start(bf16[256,512]{1,0:T(8,128)(2,1)S(1)} %slice.50), channel_id=1, source_target_pairs={{0,1},{1,0},{2,3},{3,2},{4,5},{5,4},{6,7},{7,6},{8,9},{9,8},{10,11... | collective-permute-start | bytes 786440 | tf_op jit(solution)/shard_map/ppermute | solution.py:20
Sparse Core Ops, SparseCore 0:
  29.6 61.3 all-gather.3
  92.8 89.3 all-gather.5

commit v8 on v7

--- a/solution.py
+++ b/solution.py
@@ -526,7 +526,7 @@
     comb_own = jnp.sum(dealt[:, :, :half], axis=0).astype(bf16)
     res_rows = dealt[:, :, half : half + cols].transpose(1, 0, 2).reshape(chunk, wide)
     hidden = call_lift(core_id, comb_own, swap(comb_own), res_rows, lift_wide)
-    hid_own = spread(hidden, plane).reshape(rows, wide)
+    hid_own = spread(spread(hidden, "z"), "y").transpose(1, 0, 2, 3).reshape(rows, wide)
 
     steps = 2
     gain_sides = norm_gain.astype(f32).reshape(places, 2, cols)

time: 294 us -> 293 us (level)
    all_to_all x5 -> x6, blocking collectives: 113 us -> 112 us  [deal(): return lax.all_to_all(x, axes, 0, 0, tiled=True)]
where the time goes in v8:
time: 293 us; the launch traced here: 292 us
  blocking collectives  112 us (38%)
  waiting for transfers between devices  65.8 us (22%)
  starting transfers between devices  49.1 us (17%)
  Pallas kernels  31.5 us (11%)
  between operations  14.5 us (5%)
  local copies, waits for them, and re-layouts  8.48 us (3%)
  other arithmetic  8.42 us (3%)
    all_to_all x6, blocking collectives, deal(): return lax.all_to_all(x, axes, 0, 0, tiled=True)  112 us
    all_to_all x4, waiting for transfers between devices, deal(): return lax.all_to_all(x, axes, 0, 0, tiled=True)  54.9 us
    pallas_call x8, Pallas kernels, call(): pl.pallas_call(kernel, grid_spec=pltpu.PrefetchScalarGridSpec(num_scalar_...  31.5 us
    ppermute x11, starting transfers between devices, swap(): return lax.ppermute(x, 'c', [(0, 1), (1, 0)])  19.3 us
    all_to_all x4, starting transfers between devices, deal(): return lax.all_to_all(x, axes, 0, 0, tiled=True)  18.4 us
    ppermute x11, waiting for transfers between devices, swap(): return lax.ppermute(x, 'c', [(0, 1), (1, 0)])  7.95 us
    ppermute x3, starting transfers between devices, on_device(): lax.ppermute(gate_own, 'dp', [(i, (i + k) % groups) for i in range(groups)])  7.52 us
  transfers between devices with their start and end apart: 23, of which 13 were waited for; matrix products, arithmetic and copies ran while one was open for 4% of the time, Pallas kernels for 8%

profile of v8, /device:TPU:1, one launch (start us, length us, event | category | flops | bytes accessed | tf_op | source)
XLA Modules:
  0.0 292.1 jit_solution(1770421424331477226)
XLA Ops:
  7.2 1.1 slice_select_fusion
  8.3 1.1 broadcast_in_dim.26
  9.4 4.8 %all-to-all-start = ((bf16[4,256,512]{2,1,0:T(8,128)(2,1)}), bf16[4,256,512]{2,1,0:T(8,128)(2,1)S(1)}, u32[]{:S(2)}, u32[]{:S(2)}) async-start(bf16[4,256,512]{2,1,0:T(8,128)(2,1)} %broadcast_in_dim.26), calls=%async_computation | async-start | bytes 2097152 | tf_op jit(solution)/shard_map/all_to_all | solution.py:24
  14.2 2.8 collective-permute-start
  17.0 0.3 collective-permute-start.1
  17.4 0.7 collective-permute-start.2
  18.1 1.5 collective-permute-start.3
  19.6 2.4 collective-permute-start.4
  22.0 2.1 collective-permute-done.3
  24.2 3.6 %collective-permute-start.5 = (f32[256]{0:T(256)S(1)}, f32[256]{0:T(256)S(1)}, u32[]{:S(2)}, u32[]{:S(2)}) collective-permute-start(f32[256]{0:T(256)S(1)} %get-tuple-element.40), channel_id=1, source_target_pairs={{0,192},{64,0},{128,64},{192,128},{1,193},{65,1},{129,65},{193,129... | collective-permute-start | bytes 3080 | tf_op jit(solution)/shard_map/ppermute | solution.py:491
  27.8 0.7 collective-permute-done.5
  28.7 0.8 constant_dynamic-slice_fusion
  29.5 3.8 %collective-permute-start.6 = (bf16[4,256,512]{2,1,0:T(8,128)(2,1)S(1)}, bf16[4,256,512]{2,1,0:T(8,128)(2,1)S(1)}, u32[]{:S(2)}, u32[]{:S(2)}) collective-permute-start(bf16[4,256,512]{2,1,0:T(8,128)(2,1)S(1)} %all-to-all-done), channel_id=1, source_target_pairs={{0,1},{1,0},{2,3},{3,2},{4,5},{5,4},{6,7},{7,6},{8,9},{9,8},{10,11... | collective-permute-start | bytes 3145736 | tf_op jit(solution)/shard_map/ppermute | solution.py:20
  33.3 2.3 collective-permute-done.6
  35.6 1.2 convolution_bitcast_fusion.1
  36.8 1.3 multiply_convert_fusion.own
  38.1 0.5 collective-permute-start.7
  38.5 0.8 broadcast_select_fusion
  39.5 0.5 collective-permute-start.9
  40.0 1.0 collective-permute-done.9
  41.2 3.2 %mix.1 = f32[1024,512]{1,0:T(8,128)} custom-call(s32[2]{0:T(128)S(1)} %pad_add_fusion.spot, bf16[336,1024]{1,0:T(8,128)(2,1)S(1)} %multiply_convert_fusion.own, bf16[336,1024]{1,0:T(8,128)(2,1)S(1)} %collective-permute-done.7.peer, bf16[336,512]{1,0:T(8,128)(2,1)S(1)} %get-tuple-element.87.keep, bf16[336,512]{1,0:T(8,128)(2,1)S(1)} %collective-permute-done.8.other, ...), custom_call_target="tpu_custom_call" | custom-call | tf_op jit(solution)/shard_map/mix/pallas_call | solution.py:296
  44.4 4.5 %all-to-all-start.1 = ((f32[4,256,512]{2,1,0:T(8,128)}), f32[4,256,512]{2,1,0:T(8,128)S(1)}, u32[]{:S(2)}, u32[]{:S(2)}) async-start(f32[4,256,512]{2,1,0:T(8,128)} %bitcast.14), calls=%async_computation.1 | async-start | bytes 4194304 | tf_op jit(solution)/shard_map/all_to_all | solution.py:24
  48.9 2.6 pad_maximum_fusion
  51.5 23.3 %all-to-all-done.1 = f32[4,256,512]{2,1,0:T(8,128)S(1)} async-done(((f32[4,256,512]{2,1,0:T(8,128)}), f32[4,256,512]{2,1,0:T(8,128)S(1)}, u32[]{:S(2)}, u32[]{:S(2)}) %all-to-all-start.1) | async-done | bytes 2097184 | tf_op jit(solution)/shard_map/all_to_all | solution.py:24
  74.8 0.2 reduce_sum.40
  75.3 29.3 %all_to_all.58 = f32[32,8,640]{2,1,0:T(8,128)S(1)} all-to-all(f32[32,8,640]{2,1,0:T(8,128)S(1)} %pad_maximum_fusion.1), channel_id=1, replica_groups=mesh['dp'=4,'z'=8,'y'=4,'c'=2] {'z','y'}, dimensions={0} | all-to-all | bytes 1310720 | tf_op jit(solution)/shard_map/all_to_all | solution.py:24
  104.7 3.4 %collective-permute-start.10 = (bf16[8,512]{1,0:T(8,128)(2,1)S(1)}, bf16[8,512]{1,0:T(8,128)(2,1)S(1)}, u32[]{:S(2)}, u32[]{:S(2)}) collective-permute-start(bf16[8,512]{1,0:T(8,128)(2,1)S(1)} %slice_reduce_fusion), channel_id=1, source_target_pairs={{0,1},{1,0},{2,3},{3,2},{4,5},{5,4},{6,7},{7,6},{8,9},{9,8},{10,11... | collective-permute-start | bytes 24584 | tf_op jit(solution)/shard_map/ppermute | solution.py:20
  108.3 0.7 collective-permute-done.10
  108.9 3.2 %lift.1.hidden = bf16[8,2048]{1,0:T(8,128)(2,1)S(1)} custom-call(s32[1]{0:T(128)} %bitcast.core, f32[8,512]{1,0:T(8,128)S(1)} %convert_element_type.59.own, f32[8,512]{1,0:T(8,128)S(1)} %convert_element_type.60.peer, f32[8,2048]{1,0:T(8,128)S(1)} %reshape.94.residual, bf16[2048,1024]{1,0:T(8,128)(2,1)} %bitcast.77), custom_call_target="tpu_custom_call" | custom-call | tf_op jit(solution)/shard_map/lift/pallas_call | solution.py:296
  112.1 14.3 %all_to_all.59 = bf16[8,8,2048]{2,1,0:T(8,128)(2,1)S(1)} all-to-all(bf16[8,8,2048]{2,1,0:T(8,128)(2,1)S(1)} %broadcast_in_dim.27), channel_id=1, replica_groups=mesh['dp'=4,'z'=8,'y'=4,'c'=2] {'z'}, dimensions={0} | all-to-all | bytes 524288 | tf_op jit(solution)/shard_map/all_to_all | solution.py:24
  126.6 17.1 %all_to_all.60 = bf16[4,8,8,2048]{3,2,1,0:T(8,128)(2,1)S(1)} all-to-all(bf16[4,8,8,2048]{3,2,1,0:T(8,128)(2,1)S(1)} %broadcast_in_dim.28), channel_id=1, replica_groups=mesh['dp'=4,'z'=8,'y'=4,'c'=2] {'y'}, dimensions={0} | all-to-all | bytes 2097152 | tf_op jit(solution)/shard_map/all_to_all | solution.py:24
  143.9 2.2 collective-permute-start.11
  146.2 0.5 broadcast.40
  146.7 0.7 fusion.10
  147.8 0.6 collective-permute-done.11.peer
  148.4 5.2 %head.1 = (f32[256,1024]{1,0:T(8,128)S(1)}, f32[8,128]{1,0:T(8,128)S(1)}, f32[256,128]{1,0:T(8,128)S(1)}) custom-call(s32[1]{0:T(128)} %bitcast.core, bf16[256,2048]{1,0:T(8,128)(2,1)S(1)} %bitcast.69, bf16[256,2048]{1,0:T(8,128)(2,1)S(1)} %collective-permute-done.11.peer, f32[4,1024]{1,0:T(4,128)S(1)} %pad_maximum_fusion.3.gain, ...), custom_call_target="tpu_custom_call" | custom-call | tf_op jit(solution)/shard_map/head/pallas_call | solution.py:296
  153.6 16.9 %all_to_all.61.stats = f32[64,8,128]{2,1,0:T(8,128)S(1)} all-to-all(f32[64,8,128]{2,1,0:T(8,128)S(1)} %broadcast_in_dim.58), channel_id=1, replica_groups=mesh['dp'=4,'z'=8,'y'=4,'c'=2] {'z','y','c'}, dimensions={0} | all-to-all | bytes 524288 | tf_op jit(solution)/shard_map/all_to_all | solution.py:24
  170.4 3.7 %loss.1 = (bf16[256,1024]{1,0:T(8,128)(2,1)S(1)}, bf16[256,2048]{1,0:T(8,128)(2,1)S(1)}, f32[8,256]{1,0:T(8,128)S(1)}, f32[256,128]{1,0:T(8,128)S(1)}) custom-call(s32[1]{0:T(128)} %bitcast.core, f32[64,8,128]{2,1,0:T(8,128)S(1)} %all_to_all.61.stats, f32[256,1024]{1,0:T(8,128)S(1)} %get-tuple-element.54.logits, s32[256,1]{1,0:T(8,128)S(1)} %copy.30.target, ...), custom_call_target="tpu_custom_call" | custom-call | tf_op jit(solution)/shard_map/loss/pallas_call | solution.py:296
  174.1 0.4 collective-permute-start.12
  174.5 3.1 %keep.1 = f32[256,2048]{1,0:T(8,128)S(1)} custom-call(s32[1]{0:T(128)} %bitcast.core, bf16[256,1024]{1,0:T(8,128)(2,1)S(1)} %get-tuple-element.57.grad, bf16[32,2,64,1024]{3,2,1,0:T(8,128)(2,1)} %bitcast.74), custom_call_target="tpu_custom_call" | custom-call | flops 1073741824 | bytes 2097152 | tf_op jit(solution)/shard_map/keep/pallas_call | solution.py:296
  177.7 1.3 fusion
  179.0 4.4 %all-to-all-start.6 = ((bf16[32,8,2048]{2,1,0:T(8,128)(2,1)}), bf16[32,8,2048]{2,1,0:T(8,128)(2,1)S(1)}, u32[]{:S(2)}, u32[]{:S(2)}) async-start(bf16[32,8,2048]{2,1,0:T(8,128)(2,1)} %fusion), calls=%async_computation.6 | async-start | bytes 2097152 | tf_op jit(solution)/shard_map/all_to_all | solution.py:24
  183.6 3.9 %prepare.1 = (f32[1344,256]{1,0:T(8,128)S(1)}, f32[1344,256]{1,0:T(8,128)S(1)}, bf16[1344,256]{1,0:T(8,128)(2,1)S(1)}) custom-call(s32[1]{0:T(128)} %bitcast.core, bf16[1024,256]{1,0:T(8,128)(2,1)S(1)} %bitcast.70, bf16[4,3,336,1024]{3,2,1,0:T(8,128)(2,1)} %bitcast.75), custom_call_target="tpu_custom_call" | custom-call | flops 1409286144 | bytes 2752512 | tf_op jit(solution)/shard_map/prepare/pallas_call | solution.py:296
  187.5 1.1 copy-done
  188.6 0.9 copy-done.2
  189.5 20.9 %all-to-all-done.6.parts = bf16[32,8,2048]{2,1,0:T(8,128)(2,1)S(1)} async-done(((bf16[32,8,2048]{2,1,0:T(8,128)(2,1)}), bf16[32,8,2048]{2,1,0:T(8,128)(2,1)S(1)}, u32[]{:S(2)}, u32[]{:S(2)}) %all-to-all-start.6) | async-done | bytes 1048608 | tf_op jit(solution)/shard_map/all_to_all | solution.py:24
  210.4 2.6 lower.1
  213.1 1.8 collective-permute-start.13
  214.9 0.8 collective-permute-done.13
  215.8 17.9 %all_to_all.62 = bf16[32,8,640]{2,1,0:T(8,128)(2,1)S(1)} all-to-all(bf16[32,8,640]{2,1,0:T(8,128)(2,1)S(1)} %pad_maximum_fusion.2), channel_id=1, replica_groups=mesh['dp'=4,'z'=8,'y'=4,'c'=2] {'z','y'}, dimensions={0} | all-to-all | bytes 655360 | tf_op jit(solution)/shard_map/all_to_all | solution.py:24
  233.7 2.5 collective-permute-start.14
  236.2 1.1 collective-permute-done.14.peer
  237.3 6.6 %expert.1 = (f32[256,640]{1,0:T(8,128)S(1)}, bf16[256,640]{1,0:T(8,128)(2,1)S(1)}) custom-call(s32[1]{0:T(128)} %bitcast.core, bf16[256,512]{1,0:T(8,128)(2,1)S(1)} %slice_bitcast_fusion.own, bf16[256,512]{1,0:T(8,128)(2,1)S(1)} %collective-permute-done.14.peer, f32[1344,256]{1,0:T(8,128)S(1)} %get-tuple-element.67.slope, f32[1344,256]{1,0:T(8,128)S(1)} %copy-done.1, ...), custom_call_target="tpu_custom_call" | custom-call | tf_op jit(solution)/shard_map/expert/pallas_call | solution.py:296
  243.9 0.5 collective-permute-start.15
  244.4 1.3 collective-permute-done.15
  245.7 16.3 %all_to_all.63 = bf16[32,8,640]{2,1,0:T(8,128)(2,1)S(1)} all-to-all(bf16[32,8,640]{2,1,0:T(8,128)(2,1)S(1)} %fusion.2), channel_id=1, replica_groups=mesh['dp'=4,'z'=8,'y'=4,'c'=2] {'z','y'}, dimensions={0} | all-to-all | bytes 655360 | tf_op jit(solution)/shard_map/all_to_all | solution.py:24
  262.1 0.8 broadcast_in_dim.62
  262.8 4.8 %all-to-all-start.9 = ((bf16[32,8,640]{2,1,0:T(8,128)(2,1)}), bf16[32,8,640]{2,1,0:T(8,128)(2,1)S(1)}, u32[]{:S(2)}, u32[]{:S(2)}) async-start(bf16[32,8,640]{2,1,0:T(8,128)(2,1)} %broadcast_in_dim.62), calls=%async_computation.9 | async-start | bytes 655360 | tf_op jit(solution)/shard_map/all_to_all | solution.py:24
  267.6 0.6 slice.37
  268.2 10.7 %all-to-all-done.9 = bf16[32,8,640]{2,1,0:T(8,128)(2,1)S(1)} async-done(((bf16[32,8,640]{2,1,0:T(8,128)(2,1)}), bf16[32,8,640]{2,1,0:T(8,128)(2,1)S(1)}, u32[]{:S(2)}, u32[]{:S(2)}) %all-to-all-start.9) | async-done | bytes 327712 | tf_op jit(solution)/shard_map/all_to_all | solution.py:24
  278.8 3.8 %collective-permute-start.16 = (bf16[256,512]{1,0:T(8,128)(2,1)S(1)}, bf16[256,512]{1,0:T(8,128)(2,1)S(1)}, u32[]{:S(2)}, u32[]{:S(2)}) collective-permute-start(bf16[256,512]{1,0:T(8,128)(2,1)S(1)} %slice.50), channel_id=1, source_target_pairs={{0,1},{1,0},{2,3},{3,2},{4,5},{5,4},{6,7},{7,6},{8,9},{9,8},{10,11... | collective-permute-start | bytes 786440 | tf_op jit(solution)/shard_map/ppermute | solution.py:20
  282.7 0.7 copy.33
  283.4 0.7 copy.34
  284.1 1.1 fusion.1
  (88 shorter events, 2.3 us)
Async XLA Ops:
  7.2 7.0 %copy-start.9 = (bf16[1024,64]{0,1:T(8,128)(2,1)S(1)}, bf16[1024,64]{0,1:T(8,128)(2,1)}, u32[]{:S(2)}) copy-start(bf16[1024,64]{0,1:T(8,128)(2,1)} %param.19) | copy-start | bytes 393220
  7.2 10.9 %copy-start.11 = (f32[256,22]{0,1:T(8,128)S(1)}, f32[256,22]{0,1:T(8,128)}, u32[]{:S(2)}) copy-start(f32[256,22]{0,1:T(8,128)} %param.14) | copy-start | bytes 67588
  7.2 10.9 %copy-start.12 = (s32[256,22]{0,1:T(8,128)S(1)}, s32[256,22]{0,1:T(8,128)}, u32[]{:S(2)}) copy-start(s32[256,22]{0,1:T(8,128)} %param.15) | copy-start | bytes 67588
  9.4 19.1 %all-to-all-start = ((bf16[4,256,512]{2,1,0:T(8,128)(2,1)}), bf16[4,256,512]{2,1,0:T(8,128)(2,1)S(1)}, u32[]{:S(2)}, u32[]{:S(2)}) async-start(bf16[4,256,512]{2,1,0:T(8,128)(2,1)} %broadcast_in_dim.26), calls=%async_computation | async-start | bytes 2097152 | tf_op jit(solution)/shard_map/all_to_all | solution.py:24
  14.2 21.4 %copy-start.7 = (bf16[1,1024,336]{1,2,0:T(8,128)(2,1)S(1)}, bf16[1,1024,336]{1,2,0:T(8,128)(2,1)}, u32[]{:S(2)}) copy-start(bf16[1,1024,336]{1,2,0:T(8,128)(2,1)} %param.16) | copy-start | bytes 2064388
  14.2 94.7 %all-gather.4.cloned.1.call-start = ((), (), s32[]{:S(2)}) async-start(), calls=%async_computation.10 | async-start | bytes 4718592 | tf_op jit(solution)/shard_map/all_gather | solution.py:503
  14.2 14.3 %collective-permute-start = (bf16[64,1024]{1,0:T(8,128)(2,1)S(1)}, bf16[64,1024]{1,0:T(8,128)(2,1)S(1)}, u32[]{:S(2)}, u32[]{:S(2)}) collective-permute-start(bf16[64,1024]{1,0:T(8,128)(2,1)S(1)} %bitcast.88), channel_id=1, source_target_pairs={{2,0},{4,2},{6,4},{0,6},{3,1},{5,3},{7,5},{1,7},{10,8},{12,10},{14... | collective-permute-start | bytes 393224 | tf_op jit(solution)/shard_map/ppermute | solution.py:484
  17.0 11.5 %collective-permute-start.1 = (bf16[64,1024]{1,0:T(8,128)(2,1)S(1)}, bf16[64,1024]{1,0:T(8,128)(2,1)S(1)}, u32[]{:S(2)}, u32[]{:S(2)}) collective-permute-start(bf16[64,1024]{1,0:T(8,128)(2,1)S(1)} %bitcast.89), channel_id=1, source_target_pairs={{4,0},{6,2},{0,4},{2,6},{5,1},{7,3},{1,5},{3,7},{12,8},{14,10},{8,... | collective-permute-start | bytes 393224 | tf_op jit(solution)/shard_map/ppermute | solution.py:484
  17.4 11.1 %collective-permute-start.2 = (bf16[64,1024]{1,0:T(8,128)(2,1)S(1)}, bf16[64,1024]{1,0:T(8,128)(2,1)S(1)}, u32[]{:S(2)}, u32[]{:S(2)}) collective-permute-start(bf16[64,1024]{1,0:T(8,128)(2,1)S(1)} %bitcast.90), channel_id=1, source_target_pairs={{6,0},{0,2},{2,4},{4,6},{7,1},{1,3},{3,5},{5,7},{14,8},{8,10},{10,... | collective-permute-start | bytes 393224 | tf_op jit(solution)/shard_map/ppermute | solution.py:484
  18.1 6.1 %collective-permute-start.3 = (f32[256]{0:T(256)S(1)}, f32[256]{0:T(256)S(1)}, u32[]{:S(2)}, u32[]{:S(2)}) collective-permute-start(f32[256]{0:T(256)S(1)} %get-tuple-element.40), channel_id=1, source_target_pairs={{0,64},{64,128},{128,192},{192,0},{1,65},{65,129},{129,193},{193,1... | collective-permute-start | bytes 3080 | tf_op jit(solution)/shard_map/ppermute | solution.py:491
  19.6 8.1 %collective-permute-start.4 = (f32[256]{0:T(256)S(1)}, f32[256]{0:T(256)S(1)}, u32[]{:S(2)}, u32[]{:S(2)}) collective-permute-start(f32[256]{0:T(256)S(1)} %get-tuple-element.40), channel_id=1, source_target_pairs={{0,128},{64,192},{128,0},{192,64},{1,129},{65,193},{129,1},{193,65... | collective-permute-start | bytes 3080 | tf_op jit(solution)/shard_map/ppermute | solution.py:491
  24.2 4.3 %collective-permute-start.5 = (f32[256]{0:T(256)S(1)}, f32[256]{0:T(256)S(1)}, u32[]{:S(2)}, u32[]{:S(2)}) collective-permute-start(f32[256]{0:T(256)S(1)} %get-tuple-element.40), channel_id=1, source_target_pairs={{0,192},{64,0},{128,64},{192,128},{1,193},{65,1},{129,65},{193,129... | collective-permute-start | bytes 3080 | tf_op jit(solution)/shard_map/ppermute | solution.py:491
  29.5 6.0 %collective-permute-start.6 = (bf16[4,256,512]{2,1,0:T(8,128)(2,1)S(1)}, bf16[4,256,512]{2,1,0:T(8,128)(2,1)S(1)}, u32[]{:S(2)}, u32[]{:S(2)}) collective-permute-start(bf16[4,256,512]{2,1,0:T(8,128)(2,1)S(1)} %all-to-all-done), channel_id=1, source_target_pairs={{0,1},{1,0},{2,3},{3,2},{4,5},{5,4},{6,7},{7,6},{8,9},{9,8},{10,11... | collective-permute-start | bytes 3145736 | tf_op jit(solution)/shard_map/ppermute | solution.py:20
  35.6 1.2 copy-start.8
  36.8 1.8 copy-start.5
  38.1 3.1 %collective-permute-start.7 = (bf16[336,1024]{1,0:T(8,128)(2,1)S(1)}, bf16[336,1024]{1,0:T(8,128)(2,1)S(1)}, u32[]{:S(2)}, u32[]{:S(2)}) collective-permute-start(bf16[336,1024]{1,0:T(8,128)(2,1)S(1)} %multiply_convert_fusion.own), channel_id=1, source_target_pairs={{0,1},{1,0},{2,3},{3,2},{4,5},{5,4},{6,7},{7,6},{8,9},{9,8},{10,11... | collective-permute-start | bytes 2064392 | tf_op jit(solution)/shard_map/ppermute | solution.py:20
  39.3 1.9 collective-permute-start.8
  39.5 1.5 collective-permute-start.9
  44.4 30.4 %all-to-all-start.1 = ((f32[4,256,512]{2,1,0:T(8,128)}), f32[4,256,512]{2,1,0:T(8,128)S(1)}, u32[]{:S(2)}, u32[]{:S(2)}) async-start(f32[4,256,512]{2,1,0:T(8,128)} %bitcast.14), calls=%async_computation.1 | async-start | bytes 4194304 | tf_op jit(solution)/shard_map/all_to_all | solution.py:24
  48.9 134.8 %all-gather.6.cloned.1.call-start = ((), (), s32[]{:S(2)}) async-start(), calls=%async_computation.11 | async-start | bytes 10321920 | tf_op jit(solution)/shard_map/all_gather | solution.py:520
  51.5 23.6 %copy-start.10 = (bf16[256,64]{0,1:T(8,128)(2,1)S(1)}, bf16[256,64]{0,1:T(8,128)(2,1)}, u32[]{:S(2)}) copy-start(bf16[256,64]{0,1:T(8,128)(2,1)} %param.13) | copy-start | bytes 98308
  104.7 4.2 %collective-permute-start.10 = (bf16[8,512]{1,0:T(8,128)(2,1)S(1)}, bf16[8,512]{1,0:T(8,128)(2,1)S(1)}, u32[]{:S(2)}, u32[]{:S(2)}) collective-permute-start(bf16[8,512]{1,0:T(8,128)(2,1)S(1)} %slice_reduce_fusion), channel_id=1, source_target_pairs={{0,1},{1,0},{2,3},{3,2},{4,5},{5,4},{6,7},{7,6},{8,9},{9,8},{10,11... | collective-permute-start | bytes 24584 | tf_op jit(solution)/shard_map/ppermute | solution.py:20
  126.6 19.5 %copy-start.13 = (bf16[4096]{0:T(1024)(128)(2,1)S(1)}, bf16[4096]{0:T(1024)(128)(2,1)}, u32[]{:S(2)}) copy-start(bf16[4096]{0:T(1024)(128)(2,1)} %param.20) | copy-start | bytes 24580
  126.6 21.0 %copy-start.14 = (s32[256]{0:T(256)S(1)}, s32[256]{0:T(256)}, u32[]{:S(2)}) copy-start(s32[256]{0:T(256)} %param.22) | copy-start | bytes 3076
  143.9 4.5 %collective-permute-start.11 = (bf16[256,2048]{1,0:T(8,128)(2,1)S(1)}, bf16[256,2048]{1,0:T(8,128)(2,1)S(1)}, u32[]{:S(2)}, u32[]{:S(2)}) collective-permute-start(bf16[256,2048]{1,0:T(8,128)(2,1)S(1)} %bitcast.68), channel_id=1, source_target_pairs={{0,1},{1,0},{2,3},{3,2},{4,5},{5,4},{6,7},{7,6},{8,9},{9,8},{10,11... | collective-permute-start | bytes 3145736 | tf_op jit(solution)/shard_map/ppermute | solution.py:20
  148.4 22.1 %copy-start.4 = (f32[256]{0:T(256)S(1)}, f32[256]{0:T(256)}, u32[]{:S(2)}) copy-start(f32[256]{0:T(256)} %param.23) | copy-start | bytes 3076
  174.1 3.5 %collective-permute-start.12 = (bf16[256,2048]{1,0:T(8,128)(2,1)S(1)}, bf16[256,2048]{1,0:T(8,128)(2,1)S(1)}, u32[]{:S(2)}, u32[]{:S(2)}) collective-permute-start(bf16[256,2048]{1,0:T(8,128)(2,1)S(1)} %get-tuple-element.58), channel_id=1, source_target_pairs={{0,1},{1,0},{2,3},{3,2},{4,5},{5,4},{6,7},{7,6},{8,9},{9,8},{10,11... | collective-permute-start | bytes 3145736 | tf_op jit(solution)/shard_map/ppermute | solution.py:20
  179.0 4.4 %copy-start.6 = (bf16[256,1024]{1,0:T(8,128)(2,1)S(1)}, bf16[256,1024]{1,0:T(8,128)(2,1)}, u32[]{:S(2)}) copy-start(bf16[256,1024]{1,0:T(8,128)(2,1)} %param.12) | copy-start | bytes 1572868
  179.0 31.4 %all-to-all-start.6 = ((bf16[32,8,2048]{2,1,0:T(8,128)(2,1)}), bf16[32,8,2048]{2,1,0:T(8,128)(2,1)S(1)}, u32[]{:S(2)}, u32[]{:S(2)}) async-start(bf16[32,8,2048]{2,1,0:T(8,128)(2,1)} %fusion), calls=%async_computation.6 | async-start | bytes 2097152 | tf_op jit(solution)/shard_map/all_to_all | solution.py:24
  187.5 1.1 copy-start
  188.6 0.9 copy-start.2
  213.0 24.3 %copy-start.1 = (f32[1344,256]{1,0:T(8,128)S(1)}, f32[1344,256]{1,0:T(8,128)}, u32[]{:S(2)}) copy-start(f32[1344,256]{1,0:T(8,128)} %copy-done) | copy-start | bytes 4128772
  213.0 24.3 %copy-start.3 = (bf16[1344,256]{1,0:T(8,128)(2,1)S(1)}, bf16[1344,256]{1,0:T(8,128)(2,1)}, u32[]{:S(2)}) copy-start(bf16[1344,256]{1,0:T(8,128)(2,1)} %copy-done.2) | copy-start | bytes 2064388
  213.1 2.6 collective-permute-start.13
  233.7 3.6 %collective-permute-start.14 = (bf16[256,512]{1,0:T(8,128)(2,1)S(1)}, bf16[256,512]{1,0:T(8,128)(2,1)S(1)}, u32[]{:S(2)}, u32[]{:S(2)}) collective-permute-start(bf16[256,512]{1,0:T(8,128)(2,1)S(1)} %slice_bitcast_fusion.own), channel_id=1, source_target_pairs={{0,1},{1,0},{2,3},{3,2},{4,5},{5,4},{6,7},{7,6},{8,9},{9,8},{10,11... | collective-permute-start | bytes 786440 | tf_op jit(solution)/shard_map/ppermute | solution.py:20
  243.9 1.7 collective-permute-start.15
  262.8 16.0 %all-to-all-start.9 = ((bf16[32,8,640]{2,1,0:T(8,128)(2,1)}), bf16[32,8,640]{2,1,0:T(8,128)(2,1)S(1)}, u32[]{:S(2)}, u32[]{:S(2)}) async-start(bf16[32,8,640]{2,1,0:T(8,128)(2,1)} %broadcast_in_dim.62), calls=%async_computation.9 | async-start | bytes 655360 | tf_op jit(solution)/shard_map/all_to_all | solution.py:24
  278.8 5.3 %collective-permute-start.16 = (bf16[256,512]{1,0:T(8,128)(2,1)S(1)}, bf16[256,512]{1,0:T(8,128)(2,1)S(1)}, u32[]{:S(2)}, u32[]{:S(2)}) collective-permute-start(bf16[256,512]{1,0:T(8,128)(2,1)S(1)} %slice.50), channel_id=1, source_target_pairs={{0,1},{1,0},{2,3},{3,2},{4,5},{5,4},{6,7},{7,6},{8,9},{9,8},{10,11... | collective-permute-start | bytes 786440 | tf_op jit(solution)/shard_map/ppermute | solution.py:20
Sparse Core Ops, SparseCore 0:
  29.6 61.3 all-gather.3
  92.8 89.3 all-gather.5

commit v9 on v8

--- a/solution.py
+++ b/solution.py
@@ -375,8 +375,8 @@
     )[0]
 
 
-def call_lower(place, parts, hidden, gain, marks, lift):
-    places, chunk, wide = parts.shape
+def call_lower(place, parts, hidden, gain, marks, lift, places):
+    _, chunk, wide = parts.shape
     width = lift.shape[1]
     return call(
         lower_kernel,
@@ -544,11 +544,13 @@
     row_loss = loss[0]
     keep = call_keep(core_id, grad, vocab)
     keep = (keep + swap(send).astype(f32)).astype(bf16)
-    parts = deal(keep.reshape(places, chunk, wide), plane)
+    keep = keep.reshape(places // ring, ring, chunk, wide).transpose(1, 0, 2, 3)
+    keep = jnp.sum(deal(keep, "y").astype(f32), axis=0).astype(bf16)
+    parts = deal(keep, "z")
     prepared = call_prepare(core_id, latent.T, weights)
     parts, *prepared = lax.optimization_barrier((parts, *prepared))
     chunks, partial = call_lower(
-        place.astype(jnp.int32)[None], parts, hidden, gain_own.reshape(1, wide), marks, lift_wide
+        place.astype(jnp.int32)[None], parts, hidden, gain_own.reshape(1, wide), marks, lift_wide, places
     )
     cg_rows = (mine(partial, 1) + swap(other(partial, 1))).astype(bf16)
     cg_rows = jnp.broadcast_to(cg_rows[None], (places, chunk, half))

time: 293 us -> 294 us (level)
  waiting for transfers between devices: 65.8 us -> 48.7 us
  blocking collectives: 112 us -> 128 us
    all_to_all x6 -> x7, blocking collectives: 112 us -> 128 us  [deal(): return lax.all_to_all(x, axes, 0, 0, tiled=True)]
    all_to_all x4, waiting for transfers between devices: 54.9 us -> 38.9 us  [deal(): return lax.all_to_all(x, axes, 0, 0, tiled=True)]
  transfers between devices with their start and end apart: 23 -> 23, of which waited for: 13 -> 12; matrix products, arithmetic and copies ran while one was open for 4% -> 5% of each run, Pallas kernels for 8% -> 8%
where the time goes in v9:
time: 294 us; the launch traced here: 293 us
  blocking collectives  128 us (44%)
  waiting for transfers between devices  48.7 us (17%)
  starting transfers between devices  48.3 us (16%)
  Pallas kernels  31.3 us (11%)
  between operations  14.6 us (5%)
  local copies, waits for them, and re-layouts  9.83 us (3%)
  other arithmetic  9.52 us (3%)
    all_to_all x7, blocking collectives, deal(): return lax.all_to_all(x, axes, 0, 0, tiled=True)  128 us
    all_to_all x4, waiting for transfers between devices, deal(): return lax.all_to_all(x, axes, 0, 0, tiled=True)  38.9 us
    pallas_call x8, Pallas kernels, call(): pl.pallas_call(kernel, grid_spec=pltpu.PrefetchScalarGridSpec(num_scalar_...  31.3 us
    ppermute x11, starting transfers between devices, swap(): return lax.ppermute(x, 'c', [(0, 1), (1, 0)])  19.3 us
    all_to_all x4, starting transfers between devices, deal(): return lax.all_to_all(x, axes, 0, 0, tiled=True)  17.7 us
    ppermute x3, starting transfers between devices, on_device(): lax.ppermute(gate_own, 'dp', [(i, (i + k) % groups) for i in range(groups)])  7.45 us
    ppermute x11, waiting for transfers between devices, swap(): return lax.ppermute(x, 'c', [(0, 1), (1, 0)])  7.36 us
  transfers between devices with their start and end apart: 23, of which 12 were waited for; matrix products, arithmetic and copies ran while one was open for 5% of the time, Pallas kernels for 8%

profile of v9, /device:TPU:1, one launch (start us, length us, event | category | flops | bytes accessed | tf_op | source)
XLA Modules:
  0.0 292.7 jit_solution(8082806153103050170)
XLA Ops:
  7.2 1.1 slice_select_fusion
  8.3 1.1 broadcast_in_dim.26
  9.4 4.8 %all-to-all-start = ((bf16[4,256,512]{2,1,0:T(8,128)(2,1)}), bf16[4,256,512]{2,1,0:T(8,128)(2,1)S(1)}, u32[]{:S(2)}, u32[]{:S(2)}) async-start(bf16[4,256,512]{2,1,0:T(8,128)(2,1)} %broadcast_in_dim.26), calls=%async_computation | async-start | bytes 2097152 | tf_op jit(solution)/shard_map/all_to_all | solution.py:24
  14.2 2.8 collective-permute-start
  17.4 0.7 collective-permute-start.2
  18.1 0.6 fusion.3
  18.7 1.5 collective-permute-start.3
  20.2 2.4 collective-permute-start.4
  22.6 1.6 collective-permute-done.3
  24.2 3.6 %collective-permute-start.5 = (f32[256]{0:T(256)S(1)}, f32[256]{0:T(256)S(1)}, u32[]{:S(2)}, u32[]{:S(2)}) collective-permute-start(f32[256]{0:T(256)S(1)} %get-tuple-element.40), channel_id=1, source_target_pairs={{0,192},{64,0},{128,64},{192,128},{1,193},{65,1},{129,65},{193,129... | collective-permute-start | bytes 3080 | tf_op jit(solution)/shard_map/ppermute | solution.py:491
  27.8 0.7 collective-permute-done.5
  28.7 0.8 constant_dynamic-slice_fusion
  29.5 3.8 %collective-permute-start.6 = (bf16[4,256,512]{2,1,0:T(8,128)(2,1)S(1)}, bf16[4,256,512]{2,1,0:T(8,128)(2,1)S(1)}, u32[]{:S(2)}, u32[]{:S(2)}) collective-permute-start(bf16[4,256,512]{2,1,0:T(8,128)(2,1)S(1)} %all-to-all-done), channel_id=1, source_target_pairs={{0,1},{1,0},{2,3},{3,2},{4,5},{5,4},{6,7},{7,6},{8,9},{9,8},{10,11... | collective-permute-start | bytes 3145736 | tf_op jit(solution)/shard_map/ppermute | solution.py:20
  33.3 2.3 collective-permute-done.6
  35.6 1.2 convolution_bitcast_fusion.1
  36.8 1.3 multiply_convert_fusion.own
  38.1 0.5 collective-permute-start.7
  38.5 0.8 broadcast_select_fusion
  39.5 0.5 collective-permute-start.9
  40.0 1.0 collective-permute-done.9
  41.2 3.2 %mix.1 = f32[1024,512]{1,0:T(8,128)} custom-call(s32[2]{0:T(128)S(1)} %pad_add_fusion.spot, bf16[336,1024]{1,0:T(8,128)(2,1)S(1)} %multiply_convert_fusion.own, bf16[336,1024]{1,0:T(8,128)(2,1)S(1)} %collective-permute-done.7.peer, bf16[336,512]{1,0:T(8,128)(2,1)S(1)} %get-tuple-element.87.keep, bf16[336,512]{1,0:T(8,128)(2,1)S(1)} %collective-permute-done.8.other, ...), custom_call_target="tpu_custom_call" | custom-call | tf_op jit(solution)/shard_map/mix/pallas_call | solution.py:296
  44.4 4.5 %all-to-all-start.1 = ((f32[4,256,512]{2,1,0:T(8,128)}), f32[4,256,512]{2,1,0:T(8,128)S(1)}, u32[]{:S(2)}, u32[]{:S(2)}) async-start(f32[4,256,512]{2,1,0:T(8,128)} %bitcast.14), calls=%async_computation.1 | async-start | bytes 4194304 | tf_op jit(solution)/shard_map/all_to_all | solution.py:24
  48.9 2.6 pad_maximum_fusion
  51.5 23.3 %all-to-all-done.1 = f32[4,256,512]{2,1,0:T(8,128)S(1)} async-done(((f32[4,256,512]{2,1,0:T(8,128)}), f32[4,256,512]{2,1,0:T(8,128)S(1)}, u32[]{:S(2)}, u32[]{:S(2)}) %all-to-all-start.1) | async-done | bytes 2097184 | tf_op jit(solution)/shard_map/all_to_all | solution.py:24
  75.3 29.6 %all_to_all.63 = f32[32,8,640]{2,1,0:T(8,128)S(1)} all-to-all(f32[32,8,640]{2,1,0:T(8,128)S(1)} %pad_maximum_fusion.1), channel_id=1, replica_groups=mesh['dp'=4,'z'=8,'y'=4,'c'=2] {'z','y'}, dimensions={0} | all-to-all | bytes 1310720 | tf_op jit(solution)/shard_map/all_to_all | solution.py:24
  104.9 3.2 %collective-permute-start.10 = (bf16[8,512]{1,0:T(8,128)(2,1)S(1)}, bf16[8,512]{1,0:T(8,128)(2,1)S(1)}, u32[]{:S(2)}, u32[]{:S(2)}) collective-permute-start(bf16[8,512]{1,0:T(8,128)(2,1)S(1)} %slice_reduce_fusion), channel_id=1, source_target_pairs={{0,1},{1,0},{2,3},{3,2},{4,5},{5,4},{6,7},{7,6},{8,9},{9,8},{10,11... | collective-permute-start | bytes 24584 | tf_op jit(solution)/shard_map/ppermute | solution.py:20
  108.3 0.7 collective-permute-done.10
  109.0 3.2 %lift.1.hidden = bf16[8,2048]{1,0:T(8,128)(2,1)S(1)} custom-call(s32[1]{0:T(128)} %bitcast.core, f32[8,512]{1,0:T(8,128)S(1)} %convert_element_type.61.own, f32[8,512]{1,0:T(8,128)S(1)} %convert_element_type.62.peer, f32[8,2048]{1,0:T(8,128)S(1)} %reshape.94.residual, bf16[2048,1024]{1,0:T(8,128)(2,1)} %bitcast.79), custom_call_target="tpu_custom_call" | custom-call | tf_op jit(solution)/shard_map/lift/pallas_call | solution.py:296
  112.2 14.4 %all_to_all.64 = bf16[8,8,2048]{2,1,0:T(8,128)(2,1)S(1)} all-to-all(bf16[8,8,2048]{2,1,0:T(8,128)(2,1)S(1)} %broadcast_in_dim.27), channel_id=1, replica_groups=mesh['dp'=4,'z'=8,'y'=4,'c'=2] {'z'}, dimensions={0} | all-to-all | bytes 524288 | tf_op jit(solution)/shard_map/all_to_all | solution.py:24
  126.7 17.1 %all_to_all.65 = bf16[4,8,8,2048]{3,2,1,0:T(8,128)(2,1)S(1)} all-to-all(bf16[4,8,8,2048]{3,2,1,0:T(8,128)(2,1)S(1)} %broadcast_in_dim.28), channel_id=1, replica_groups=mesh['dp'=4,'z'=8,'y'=4,'c'=2] {'y'}, dimensions={0} | all-to-all | bytes 2097152 | tf_op jit(solution)/shard_map/all_to_all | solution.py:24
  143.9 2.2 collective-permute-start.11
  146.2 0.6 broadcast.40
  146.8 1.3 fusion.9
  148.5 5.2 %head.1 = (f32[256,1024]{1,0:T(8,128)S(1)}, f32[8,128]{1,0:T(8,128)S(1)}, f32[256,128]{1,0:T(8,128)S(1)}) custom-call(s32[1]{0:T(128)} %bitcast.core, bf16[256,2048]{1,0:T(8,128)(2,1)S(1)} %bitcast.71, bf16[256,2048]{1,0:T(8,128)(2,1)S(1)} %collective-permute-done.11.peer, f32[4,1024]{1,0:T(4,128)S(1)} %pad_maximum_fusion.3.gain, ...), custom_call_target="tpu_custom_call" | custom-call | tf_op jit(solution)/shard_map/head/pallas_call | solution.py:296
  153.7 16.8 %all_to_all.66.stats = f32[64,8,128]{2,1,0:T(8,128)S(1)} all-to-all(f32[64,8,128]{2,1,0:T(8,128)S(1)} %broadcast_in_dim.58), channel_id=1, replica_groups=mesh['dp'=4,'z'=8,'y'=4,'c'=2] {'z','y','c'}, dimensions={0} | all-to-all | bytes 524288 | tf_op jit(solution)/shard_map/all_to_all | solution.py:24
  170.4 3.7 %loss.1 = (bf16[256,1024]{1,0:T(8,128)(2,1)S(1)}, bf16[256,2048]{1,0:T(8,128)(2,1)S(1)}, f32[8,256]{1,0:T(8,128)S(1)}, f32[256,128]{1,0:T(8,128)S(1)}) custom-call(s32[1]{0:T(128)} %bitcast.core, f32[64,8,128]{2,1,0:T(8,128)S(1)} %all_to_all.66.stats, f32[256,1024]{1,0:T(8,128)S(1)} %get-tuple-element.54.logits, s32[256,1]{1,0:T(8,128)S(1)} %copy.30.target, ...), custom_call_target="tpu_custom_call" | custom-call | tf_op jit(solution)/shard_map/loss/pallas_call | solution.py:296
  174.1 0.6 copy-done.4
  175.1 3.1 %keep.1 = f32[256,2048]{1,0:T(8,128)S(1)} custom-call(s32[1]{0:T(128)} %bitcast.core, bf16[256,1024]{1,0:T(8,128)(2,1)S(1)} %get-tuple-element.57.grad, bf16[32,2,64,1024]{3,2,1,0:T(8,128)(2,1)} %bitcast.76), custom_call_target="tpu_custom_call" | custom-call | flops 1073741824 | bytes 2097152 | tf_op jit(solution)/shard_map/keep/pallas_call | solution.py:296
  178.7 17.9 %all_to_all.67 = bf16[4,8,8,2048]{3,2,1,0:T(8,128)(2,1)S(1)} all-to-all(bf16[4,8,8,2048]{3,2,1,0:T(8,128)(2,1)S(1)} %bitcast.82), channel_id=1, replica_groups=mesh['dp'=4,'z'=8,'y'=4,'c'=2] {'y'}, dimensions={0} | all-to-all | bytes 2097152 | tf_op jit(solution)/shard_map/all_to_all | solution.py:24
  196.6 0.9 reduce_sum.54
  197.5 3.6 %all-to-all-start.7 = ((bf16[8,8,2048]{2,1,0:T(8,128)(2,1)}), bf16[8,8,2048]{2,1,0:T(8,128)(2,1)S(1)}, u32[]{:S(2)}, u32[]{:S(2)}) async-start(bf16[8,8,2048]{2,1,0:T(8,128)(2,1)} %reduce_sum.54), calls=%async_computation.7 | async-start | bytes 524288 | tf_op jit(solution)/shard_map/all_to_all | solution.py:24
  201.4 3.9 %prepare.1 = (f32[1344,256]{1,0:T(8,128)S(1)}, f32[1344,256]{1,0:T(8,128)S(1)}, bf16[1344,256]{1,0:T(8,128)(2,1)S(1)}) custom-call(s32[1]{0:T(128)} %bitcast.core, bf16[1024,256]{1,0:T(8,128)(2,1)S(1)} %bitcast.72, bf16[4,3,336,1024]{3,2,1,0:T(8,128)(2,1)} %bitcast.77), custom_call_target="tpu_custom_call" | custom-call | flops 1409286144 | bytes 2752512 | tf_op jit(solution)/shard_map/prepare/pallas_call | solution.py:296
  205.3 0.8 copy-done
  206.2 4.9 %all-to-all-done.7.parts = bf16[8,8,2048]{2,1,0:T(8,128)(2,1)S(1)} async-done(((bf16[8,8,2048]{2,1,0:T(8,128)(2,1)}), bf16[8,8,2048]{2,1,0:T(8,128)(2,1)S(1)}, u32[]{:S(2)}, u32[]{:S(2)}) %all-to-all-start.7) | async-done | bytes 262176 | tf_op jit(solution)/shard_map/all_to_all | solution.py:24
  211.1 0.8 copy-done.3
  211.9 0.9 copy-done.5
  212.8 2.5 lower.1
  215.3 2.4 collective-permute-start.13
  217.7 0.8 collective-permute-done.13
  218.6 16.1 %all_to_all.68 = bf16[32,8,640]{2,1,0:T(8,128)(2,1)S(1)} all-to-all(bf16[32,8,640]{2,1,0:T(8,128)(2,1)S(1)} %pad_maximum_fusion.2), channel_id=1, replica_groups=mesh['dp'=4,'z'=8,'y'=4,'c'=2] {'z','y'}, dimensions={0} | all-to-all | bytes 655360 | tf_op jit(solution)/shard_map/all_to_all | solution.py:24
  234.7 2.2 collective-permute-start.14
  236.8 1.1 collective-permute-done.14.peer
  238.0 6.6 %expert.1 = (f32[256,640]{1,0:T(8,128)S(1)}, bf16[256,640]{1,0:T(8,128)(2,1)S(1)}) custom-call(s32[1]{0:T(128)} %bitcast.core, bf16[256,512]{1,0:T(8,128)(2,1)S(1)} %slice_bitcast_fusion.own, bf16[256,512]{1,0:T(8,128)(2,1)S(1)} %collective-permute-done.14.peer, f32[1344,256]{1,0:T(8,128)S(1)} %get-tuple-element.67.slope, ...), custom_call_target="tpu_custom_call" | custom-call | tf_op jit(solution)/shard_map/expert/pallas_call | solution.py:296
  244.6 0.5 collective-permute-start.15
  245.1 1.3 collective-permute-done.15
  246.4 16.2 %all_to_all.69 = bf16[32,8,640]{2,1,0:T(8,128)(2,1)S(1)} all-to-all(bf16[32,8,640]{2,1,0:T(8,128)(2,1)S(1)} %fusion.1), channel_id=1, replica_groups=mesh['dp'=4,'z'=8,'y'=4,'c'=2] {'z','y'}, dimensions={0} | all-to-all | bytes 655360 | tf_op jit(solution)/shard_map/all_to_all | solution.py:24
  262.7 0.8 broadcast_in_dim.62
  263.4 4.8 %all-to-all-start.10 = ((bf16[32,8,640]{2,1,0:T(8,128)(2,1)}), bf16[32,8,640]{2,1,0:T(8,128)(2,1)S(1)}, u32[]{:S(2)}, u32[]{:S(2)}) async-start(bf16[32,8,640]{2,1,0:T(8,128)(2,1)} %broadcast_in_dim.62), calls=%async_computation.10 | async-start | bytes 655360 | tf_op jit(solution)/shard_map/all_to_all | solution.py:24
  268.2 0.6 slice.37
  268.8 10.7 %all-to-all-done.10 = bf16[32,8,640]{2,1,0:T(8,128)(2,1)S(1)} async-done(((bf16[32,8,640]{2,1,0:T(8,128)(2,1)}), bf16[32,8,640]{2,1,0:T(8,128)(2,1)S(1)}, u32[]{:S(2)}, u32[]{:S(2)}) %all-to-all-start.10) | async-done | bytes 327712 | tf_op jit(solution)/shard_map/all_to_all | solution.py:24
  279.5 3.8 %collective-permute-start.16 = (bf16[256,512]{1,0:T(8,128)(2,1)S(1)}, bf16[256,512]{1,0:T(8,128)(2,1)S(1)}, u32[]{:S(2)}, u32[]{:S(2)}) collective-permute-start(bf16[256,512]{1,0:T(8,128)(2,1)S(1)} %slice.50), channel_id=1, source_target_pairs={{0,1},{1,0},{2,3},{3,2},{4,5},{5,4},{6,7},{7,6},{8,9},{9,8},{10,11... | collective-permute-start | bytes 786440 | tf_op jit(solution)/shard_map/ppermute | solution.py:20
  283.3 0.7 copy.34
  284.1 0.7 copy.35
  284.8 1.1 fusion
  (99 shorter events, 3.6 us)
Async XLA Ops:
  7.2 7.0 %copy-start.11 = (bf16[1024,64]{0,1:T(8,128)(2,1)S(1)}, bf16[1024,64]{0,1:T(8,128)(2,1)}, u32[]{:S(2)}) copy-start(bf16[1024,64]{0,1:T(8,128)(2,1)} %param.19) | copy-start | bytes 393220
  7.2 10.9 %copy-start.15 = (f32[256,22]{0,1:T(8,128)S(1)}, f32[256,22]{0,1:T(8,128)}, u32[]{:S(2)}) copy-start(f32[256,22]{0,1:T(8,128)} %param.14) | copy-start | bytes 67588
  7.2 10.9 %copy-start.16 = (s32[256,22]{0,1:T(8,128)S(1)}, s32[256,22]{0,1:T(8,128)}, u32[]{:S(2)}) copy-start(s32[256,22]{0,1:T(8,128)} %param.15) | copy-start | bytes 67588
  9.4 19.1 %all-to-all-start = ((bf16[4,256,512]{2,1,0:T(8,128)(2,1)}), bf16[4,256,512]{2,1,0:T(8,128)(2,1)S(1)}, u32[]{:S(2)}, u32[]{:S(2)}) async-start(bf16[4,256,512]{2,1,0:T(8,128)(2,1)} %broadcast_in_dim.26), calls=%async_computation | async-start | bytes 2097152 | tf_op jit(solution)/shard_map/all_to_all | solution.py:24
  14.2 21.4 %copy-start.9 = (bf16[1,1024,336]{1,2,0:T(8,128)(2,1)S(1)}, bf16[1,1024,336]{1,2,0:T(8,128)(2,1)}, u32[]{:S(2)}) copy-start(bf16[1,1024,336]{1,2,0:T(8,128)(2,1)} %param.16) | copy-start | bytes 2064388
  14.2 94.7 %all-gather.4.cloned.1.call-start = ((), (), s32[]{:S(2)}) async-start(), calls=%async_computation.11 | async-start | bytes 4718592 | tf_op jit(solution)/shard_map/all_gather | solution.py:503
  14.2 14.3 %collective-permute-start = (bf16[64,1024]{1,0:T(8,128)(2,1)S(1)}, bf16[64,1024]{1,0:T(8,128)(2,1)S(1)}, u32[]{:S(2)}, u32[]{:S(2)}) collective-permute-start(bf16[64,1024]{1,0:T(8,128)(2,1)S(1)} %bitcast.92), channel_id=1, source_target_pairs={{2,0},{4,2},{6,4},{0,6},{3,1},{5,3},{7,5},{1,7},{10,8},{12,10},{14... | collective-permute-start | bytes 393224 | tf_op jit(solution)/shard_map/ppermute | solution.py:484
  17.0 11.5 %collective-permute-start.1 = (bf16[64,1024]{1,0:T(8,128)(2,1)S(1)}, bf16[64,1024]{1,0:T(8,128)(2,1)S(1)}, u32[]{:S(2)}, u32[]{:S(2)}) collective-permute-start(bf16[64,1024]{1,0:T(8,128)(2,1)S(1)} %bitcast.93), channel_id=1, source_target_pairs={{4,0},{6,2},{0,4},{2,6},{5,1},{7,3},{1,5},{3,7},{12,8},{14,10},{8,... | collective-permute-start | bytes 393224 | tf_op jit(solution)/shard_map/ppermute | solution.py:484
  17.4 11.1 %collective-permute-start.2 = (bf16[64,1024]{1,0:T(8,128)(2,1)S(1)}, bf16[64,1024]{1,0:T(8,128)(2,1)S(1)}, u32[]{:S(2)}, u32[]{:S(2)}) collective-permute-start(bf16[64,1024]{1,0:T(8,128)(2,1)S(1)} %bitcast.94), channel_id=1, source_target_pairs={{6,0},{0,2},{2,4},{4,6},{7,1},{1,3},{3,5},{5,7},{14,8},{8,10},{10,... | collective-permute-start | bytes 393224 | tf_op jit(solution)/shard_map/ppermute | solution.py:484
  18.7 5.5 %collective-permute-start.3 = (f32[256]{0:T(256)S(1)}, f32[256]{0:T(256)S(1)}, u32[]{:S(2)}, u32[]{:S(2)}) collective-permute-start(f32[256]{0:T(256)S(1)} %get-tuple-element.40), channel_id=1, source_target_pairs={{0,64},{64,128},{128,192},{192,0},{1,65},{65,129},{129,193},{193,1... | collective-permute-start | bytes 3080 | tf_op jit(solution)/shard_map/ppermute | solution.py:491
  20.2 7.6 %collective-permute-start.4 = (f32[256]{0:T(256)S(1)}, f32[256]{0:T(256)S(1)}, u32[]{:S(2)}, u32[]{:S(2)}) collective-permute-start(f32[256]{0:T(256)S(1)} %get-tuple-element.40), channel_id=1, source_target_pairs={{0,128},{64,192},{128,0},{192,64},{1,129},{65,193},{129,1},{193,65... | collective-permute-start | bytes 3080 | tf_op jit(solution)/shard_map/ppermute | solution.py:491
  24.2 4.3 %collective-permute-start.5 = (f32[256]{0:T(256)S(1)}, f32[256]{0:T(256)S(1)}, u32[]{:S(2)}, u32[]{:S(2)}) collective-permute-start(f32[256]{0:T(256)S(1)} %get-tuple-element.40), channel_id=1, source_target_pairs={{0,192},{64,0},{128,64},{192,128},{1,193},{65,1},{129,65},{193,129... | collective-permute-start | bytes 3080 | tf_op jit(solution)/shard_map/ppermute | solution.py:491
  29.5 6.0 %collective-permute-start.6 = (bf16[4,256,512]{2,1,0:T(8,128)(2,1)S(1)}, bf16[4,256,512]{2,1,0:T(8,128)(2,1)S(1)}, u32[]{:S(2)}, u32[]{:S(2)}) collective-permute-start(bf16[4,256,512]{2,1,0:T(8,128)(2,1)S(1)} %all-to-all-done), channel_id=1, source_target_pairs={{0,1},{1,0},{2,3},{3,2},{4,5},{5,4},{6,7},{7,6},{8,9},{9,8},{10,11... | collective-permute-start | bytes 3145736 | tf_op jit(solution)/shard_map/ppermute | solution.py:20
  35.6 1.2 copy-start.10
  36.8 1.8 copy-start.7
  38.1 3.1 %collective-permute-start.7 = (bf16[336,1024]{1,0:T(8,128)(2,1)S(1)}, bf16[336,1024]{1,0:T(8,128)(2,1)S(1)}, u32[]{:S(2)}, u32[]{:S(2)}) collective-permute-start(bf16[336,1024]{1,0:T(8,128)(2,1)S(1)} %multiply_convert_fusion.own), channel_id=1, source_target_pairs={{0,1},{1,0},{2,3},{3,2},{4,5},{5,4},{6,7},{7,6},{8,9},{9,8},{10,11... | collective-permute-start | bytes 2064392 | tf_op jit(solution)/shard_map/ppermute | solution.py:20
  39.3 1.9 collective-permute-start.8
  39.5 1.5 collective-permute-start.9
  44.4 30.4 %all-to-all-start.1 = ((f32[4,256,512]{2,1,0:T(8,128)}), f32[4,256,512]{2,1,0:T(8,128)S(1)}, u32[]{:S(2)}, u32[]{:S(2)}) async-start(f32[4,256,512]{2,1,0:T(8,128)} %bitcast.14), calls=%async_computation.1 | async-start | bytes 4194304 | tf_op jit(solution)/shard_map/all_to_all | solution.py:24
  48.9 152.6 %all-gather.6.cloned.1.call-start = ((), (), s32[]{:S(2)}) async-start(), calls=%async_computation.12 | async-start | bytes 10321920 | tf_op jit(solution)/shard_map/all_gather | solution.py:520
  51.5 23.6 %copy-start.14 = (bf16[256,64]{0,1:T(8,128)(2,1)S(1)}, bf16[256,64]{0,1:T(8,128)(2,1)}, u32[]{:S(2)}) copy-start(bf16[256,64]{0,1:T(8,128)(2,1)} %param.13) | copy-start | bytes 98308
  104.9 4.0 %collective-permute-start.10 = (bf16[8,512]{1,0:T(8,128)(2,1)S(1)}, bf16[8,512]{1,0:T(8,128)(2,1)S(1)}, u32[]{:S(2)}, u32[]{:S(2)}) collective-permute-start(bf16[8,512]{1,0:T(8,128)(2,1)S(1)} %slice_reduce_fusion), channel_id=1, source_target_pairs={{0,1},{1,0},{2,3},{3,2},{4,5},{5,4},{6,7},{7,6},{8,9},{9,8},{10,11... | collective-permute-start | bytes 24584 | tf_op jit(solution)/shard_map/ppermute | solution.py:20
  112.1 31.6 %copy-start.2 = (bf16[8,2048]{1,0:T(8,128)(2,1)}, bf16[8,2048]{1,0:T(8,128)(2,1)S(1)}, u32[]{:S(2)}) copy-start(bf16[8,2048]{1,0:T(8,128)(2,1)S(1)} %lift.1.hidden) | copy-start | bytes 98308
  126.6 19.5 %copy-start.17 = (bf16[4096]{0:T(1024)(128)(2,1)S(1)}, bf16[4096]{0:T(1024)(128)(2,1)}, u32[]{:S(2)}) copy-start(bf16[4096]{0:T(1024)(128)(2,1)} %param.20) | copy-start | bytes 24580
  126.6 21.6 %copy-start.18 = (s32[256]{0:T(256)S(1)}, s32[256]{0:T(256)}, u32[]{:S(2)}) copy-start(s32[256]{0:T(256)} %param.22) | copy-start | bytes 3076
  143.9 4.6 %collective-permute-start.11 = (bf16[256,2048]{1,0:T(8,128)(2,1)S(1)}, bf16[256,2048]{1,0:T(8,128)(2,1)S(1)}, u32[]{:S(2)}, u32[]{:S(2)}) collective-permute-start(bf16[256,2048]{1,0:T(8,128)(2,1)S(1)} %bitcast.70), channel_id=1, source_target_pairs={{0,1},{1,0},{2,3},{3,2},{4,5},{5,4},{6,7},{7,6},{8,9},{9,8},{10,11... | collective-permute-start | bytes 3145736 | tf_op jit(solution)/shard_map/ppermute | solution.py:20
  148.4 22.0 %copy-start.6 = (f32[256]{0:T(256)S(1)}, f32[256]{0:T(256)}, u32[]{:S(2)}) copy-start(f32[256]{0:T(256)} %param.23) | copy-start | bytes 3076
  174.1 0.6 copy-start.4
  174.8 3.4 %collective-permute-start.12 = (bf16[256,2048]{1,0:T(8,128)(2,1)S(1)}, bf16[256,2048]{1,0:T(8,128)(2,1)S(1)}, u32[]{:S(2)}, u32[]{:S(2)}) collective-permute-start(bf16[256,2048]{1,0:T(8,128)(2,1)S(1)} %get-tuple-element.58), channel_id=1, source_target_pairs={{0,1},{1,0},{2,3},{3,2},{4,5},{5,4},{6,7},{7,6},{8,9},{9,8},{10,11... | collective-permute-start | bytes 3145736 | tf_op jit(solution)/shard_map/ppermute | solution.py:20
  178.6 22.5 %copy-start.8 = (bf16[256,1024]{1,0:T(8,128)(2,1)S(1)}, bf16[256,1024]{1,0:T(8,128)(2,1)}, u32[]{:S(2)}) copy-start(bf16[256,1024]{1,0:T(8,128)(2,1)} %param.12) | copy-start | bytes 1572868
  178.6 22.7 %copy-start.13 = (f32[32,1,64]{2,1,0:T(1,128)S(1)}, f32[32,1,64]{2,1,0:T(1,128)}, u32[]{:S(2)}) copy-start(f32[32,1,64]{2,1,0:T(1,128)} %get-tuple-element.85) | copy-start | bytes 24580
  197.5 13.6 %all-to-all-start.7 = ((bf16[8,8,2048]{2,1,0:T(8,128)(2,1)}), bf16[8,8,2048]{2,1,0:T(8,128)(2,1)S(1)}, u32[]{:S(2)}, u32[]{:S(2)}) async-start(bf16[8,8,2048]{2,1,0:T(8,128)(2,1)} %reduce_sum.54), calls=%async_computation.7 | async-start | bytes 524288 | tf_op jit(solution)/shard_map/all_to_all | solution.py:24
  205.3 0.8 copy-start
  211.1 0.8 copy-start.3
  211.9 0.9 copy-start.5
  215.3 21.6 %copy-start.12 = (f32[22,256]{1,0:T(8,128)S(1)}, f32[22,256]{1,0:T(8,128)}, u32[]{:S(2)}) copy-start(f32[22,256]{1,0:T(8,128)} %get-tuple-element.88) | copy-start | bytes 67588
  215.3 22.7 %copy-start.1 = (bf16[1344,256]{1,0:T(8,128)(2,1)S(1)}, bf16[1344,256]{1,0:T(8,128)(2,1)}, u32[]{:S(2)}) copy-start(bf16[1344,256]{1,0:T(8,128)(2,1)} %copy-done) | copy-start | bytes 2064388
  215.3 3.2 %collective-permute-start.13 = (f32[8,512]{1,0:T(8,128)S(1)}, f32[8,512]{1,0:T(8,128)S(1)}, u32[]{:S(2)}, u32[]{:S(2)}) collective-permute-start(f32[8,512]{1,0:T(8,128)S(1)} %slice_select_fusion.1), channel_id=1, source_target_pairs={{0,1},{1,0},{2,3},{3,2},{4,5},{5,4},{6,7},{7,6},{8,9},{9,8},{10,11... | collective-permute-start | bytes 49160 | tf_op jit(solution)/shard_map/ppermute | solution.py:20
  234.7 3.3 %collective-permute-start.14 = (bf16[256,512]{1,0:T(8,128)(2,1)S(1)}, bf16[256,512]{1,0:T(8,128)(2,1)S(1)}, u32[]{:S(2)}, u32[]{:S(2)}) collective-permute-start(bf16[256,512]{1,0:T(8,128)(2,1)S(1)} %slice_bitcast_fusion.own), channel_id=1, source_target_pairs={{0,1},{1,0},{2,3},{3,2},{4,5},{5,4},{6,7},{7,6},{8,9},{9,8},{10,11... | collective-permute-start | bytes 786440 | tf_op jit(solution)/shard_map/ppermute | solution.py:20
  244.6 1.7 collective-permute-start.15
  263.4 16.0 %all-to-all-start.10 = ((bf16[32,8,640]{2,1,0:T(8,128)(2,1)}), bf16[32,8,640]{2,1,0:T(8,128)(2,1)S(1)}, u32[]{:S(2)}, u32[]{:S(2)}) async-start(bf16[32,8,640]{2,1,0:T(8,128)(2,1)} %broadcast_in_dim.62), calls=%async_computation.10 | async-start | bytes 655360 | tf_op jit(solution)/shard_map/all_to_all | solution.py:24
  279.5 5.3 %collective-permute-start.16 = (bf16[256,512]{1,0:T(8,128)(2,1)S(1)}, bf16[256,512]{1,0:T(8,128)(2,1)S(1)}, u32[]{:S(2)}, u32[]{:S(2)}) collective-permute-start(bf16[256,512]{1,0:T(8,128)(2,1)S(1)} %slice.50), channel_id=1, source_target_pairs={{0,1},{1,0},{2,3},{3,2},{4,5},{5,4},{6,7},{7,6},{8,9},{9,8},{10,11... | collective-permute-start | bytes 786440 | tf_op jit(solution)/shard_map/ppermute | solution.py:20
Sparse Core Ops, SparseCore 0:
  29.6 61.3 all-gather.3
  92.8 89.3 all-gather.5
